TPU v7x, 32 devices: a whole 2x2x4 slice. The times are simulated.
32 devices in a mesh: shard: 2 (over x), rows: 16 (over z, y, core), dims: 1.
Axes of the slice: x: 2, y: 2, z: 4, core: 2. Of those that a mesh axis runs over, the one named last changes fastest.
Arguments:
- train_grads: bfloat16 [32768, 4096], P(('shard', 'rows'), 'dims'), parts along dimension 0, may hold values from -6 to 6
- query_grads: bfloat16 [4096, 4096], P(('shard', 'rows'), 'dims'), parts along dimension 0, may hold values from -6 to 6
- pair_query: int32 [256, 8], P(('shard', 'rows')), parts along dimension 0, may hold values from 0 to 15, all different within a row
- layer_slot: int32 [16], replicated, may hold values from 0 to 15, each once
- in_factor: float32 [16, 16, 16], replicated, may hold values from -1.5 to 1.5
- out_factor: float32 [16, 16, 16], replicated, may hold values from -1.5 to 1.5
Outputs:
- scores: float32 [256, 8, 128, 128], P(('shard', 'rows'), None, 'dims'), parts along dimension 0
There are 2 independent parts, one for each index of `shard`. A program takes and returns all parts, laid end to end along the dimension named above; an argument that names none is the same for every part. Nothing has to cross between parts.
Inputs may be any that keep to these rules, and one draw needn't show every extreme that they name: `pair_query`: the 8 query blocks of one training block are distinct; every query block is named somewhere. `layer_slot`: each slot holds exactly one layer.
All inputs are finite; a program needn't handle non-finite values.
Results may differ from a plain program's by a relative error of at most 0.0029.
Values may be sent and summed in bfloat16 or wider, within the bound.
No kernel may reach another device: no remote copies, remote signals or barrier semaphores. Data moves between devices by JAX's collectives and lax.ppermute only.
A program may use at most 128 MiB of HBM per device.

v0:
```python
import jax
import jax.numpy as jnp
from jax import lax
from jax.sharding import PartitionSpec as P

PROJ = 16
BLK = 128


def local(train_grads, query_grads, pair_query, layer_slot, in_factor, out_factor):
    dims_count = lax.axis_size("dims")
    dims_index = lax.axis_index("dims")
    width = query_grads.shape[1]
    local_layers = width // (PROJ * PROJ)
    slots = dims_index * local_layers + jnp.arange(local_layers, dtype=jnp.int32)
    onehot = (slots[:, None] == layer_slot[None, :]).astype(jnp.float32)
    a_fac = jnp.einsum("sl,lij->sij", onehot, in_factor, precision=lax.Precision.HIGHEST)
    b_fac = jnp.einsum("sl,lij->sij", onehot, out_factor, precision=lax.Precision.HIGHEST)
    nrow = query_grads.shape[0]
    query = query_grads.astype(jnp.float32).reshape(nrow, local_layers, PROJ, PROJ)
    left = jnp.einsum("sia,rsab->rsib", a_fac, query, precision=lax.Precision.HIGHEST)
    both = jnp.einsum("rsib,sbo->rsio", left, b_fac, precision=lax.Precision.HIGHEST)
    precond = both.reshape(nrow, width).astype(jnp.bfloat16)
    gathered = lax.all_gather(precond, "rows", axis=0, tiled=True)
    qblocks = gathered.reshape(gathered.shape[0] // BLK, BLK, width)
    tblocks = train_grads.reshape(train_grads.shape[0] // BLK, BLK, width)

    def one_block(items):
        tblock, ids = items
        chosen = qblocks[ids]
        return jnp.einsum("rg,kqg->krq", tblock, chosen, preferred_element_type=jnp.float32)

    partial_scores = lax.map(one_block, (tblocks, pair_query))
    summed = lax.psum(partial_scores, "dims")
    share = BLK // dims_count
    return lax.dynamic_slice_in_dim(summed, dims_index * share, share, 2)


def solution(mesh):
    in_specs = (
        P(("shard", "rows"), "dims"),
        P(("shard", "rows"), "dims"),
        P(("shard", "rows"), None),
        P(),
        P(),
        P(),
    )
    out_specs = P(("shard", "rows"), None, "dims", None)
    return jax.shard_map(local, mesh=mesh, in_specs=in_specs, out_specs=out_specs, check_vma=False)
```

profile of v0, /device:TPU:0, one launch (start us, length us, event | category | flops | bytes accessed | tf_op | source)
XLA Modules:
  0.0 320.9 jit_solution(11796773966376466433)
XLA Ops:
  6.5 1.6 copy.9
  8.2 0.9 convolution_bitcast_fusion.1
  9.1 1.1 convolution_bitcast_fusion.2
  10.2 1.0 fusion.11
  11.2 3.3 %fusion.8 = bf16[16,16,128,16]{2,1,3,0:T(8,128)(2,1)} fusion(f32[16,16,128,16]{2,1,3,0:T(8,128)S(1)} %fusion.11, f32[16,16,16,1]{2,0,1,3:T(8,128)S(1)} %convolution_bitcast_fusion.2), kind=kOutput, calls=%fused_computation.14 | convolution fusion | flops 101187584 | bytes 3162112 | tf_op jit(solution)/shard_map/rsib,sbo->rsio/dot_general | solution.py:22
  14.5 133.2 %all-gather.2.cloned.1.call-done = bf16[2048,4096]{0,1:T(8,128)(2,1)} async-done(((bf16[128,4096]{0,1:T(8,128)(2,1)}), bf16[2048,4096]{0,1:T(8,128)(2,1)}) %all-gather.2.cloned.1.call-update) | async-done | bytes 16777232 | tf_op jit(solution)/shard_map/all_gather | solution.py:24
  147.7 21.4 %copy.10 = bf16[2048,4096]{1,0:T(8,128)(2,1)} copy(bf16[2048,4096]{0,1:T(8,128)(2,1)} %all-gather.2.cloned.1.call-done) | data formatting | bytes 33554432 | tf_op jit(solution)/shard_map/all_gather | solution.py:24
  169.1 145.0 %while.10 = (s32[]{:T(128)}, f32[8,8,128,128]{3,2,1,0:T(8,128)}, s32[8,8]{1,0:T(8,128)}, bf16[16,128,4096]{2,1,0:T(8,128)(2,1)}, bf16[8,128,4096]{2,1,0:T(8,128)(2,1)}, /*index=5*/s32[]{:T(128)}) while((s32[]{:T(128)}, f32[8,8,128,128]{3,2,1,0:T(8,128)}, s32[8,8]{1,0:T(8,128)}, bf16[16,128,4096]{2,1,0:T(8,128)(2,1)}, ...), condition=%wide.region_1.2_spmd, body=%wide.region_0.1_spmd.sunk | while | flops 1073742848 | bytes 28841160 | solution.py:33
  169.8 10.4 %gather_fusion = bf16[8,128,4096]{2,1,0:T(8,128)(2,1)} fusion(bf16[16,128,4096]{2,1,0:T(8,128)(2,1)} %get-tuple-element.89, s32[1024]{0:T(1024)S(1)} %pad_clamp_fusion.2), kind=kCustom, calls=%fused_computation.clone.1 | custom fusion | bytes 16777248 | tf_op jit(solution)/shard_map/while/body/eval_jaxpr/gather | solution.py:30
  180.2 5.9 %convolution_bitcast_fusion.4 = f32[1,8,128,128]{2,3,1,0:T(8,128)S(1)} fusion(bf16[8,128,4096]{2,1,0:T(8,128)(2,1)} %gather_fusion, bf16[8,128,4096]{2,1,0:T(8,128)(2,1)} %get-tuple-element.90, s32[]{:T(128)} %get-tuple-element.80), kind=kOutput, calls=%fused_computation.1.clone.1 | convolution fusion | flops 1073741824 | bytes 9961984 | tf_op jit(solution)/shard_map/while/body/eval_jaxpr/rg,kqg->krq/dot_general | solution.py:31
  186.4 0.8 constant_dynamic-update-slice_fusion.2
  187.9 10.4 %gather_fusion = bf16[8,128,4096]{2,1,0:T(8,128)(2,1)} fusion(bf16[16,128,4096]{2,1,0:T(8,128)(2,1)} %get-tuple-element.89, s32[1024]{0:T(1024)S(1)} %pad_clamp_fusion.2), kind=kCustom, calls=%fused_computation.clone.1 | custom fusion | bytes 16777248 | tf_op jit(solution)/shard_map/while/body/eval_jaxpr/gather | solution.py:30
  198.4 5.9 %convolution_bitcast_fusion.4 = f32[1,8,128,128]{2,3,1,0:T(8,128)S(1)} fusion(bf16[8,128,4096]{2,1,0:T(8,128)(2,1)} %gather_fusion, bf16[8,128,4096]{2,1,0:T(8,128)(2,1)} %get-tuple-element.90, s32[]{:T(128)} %get-tuple-element.80), kind=kOutput, calls=%fused_computation.1.clone.1 | convolution fusion | flops 1073741824 | bytes 9961984 | tf_op jit(solution)/shard_map/while/body/eval_jaxpr/rg,kqg->krq/dot_general | solution.py:31
  204.5 0.8 constant_dynamic-update-slice_fusion.2
  206.1 10.4 %gather_fusion = bf16[8,128,4096]{2,1,0:T(8,128)(2,1)} fusion(bf16[16,128,4096]{2,1,0:T(8,128)(2,1)} %get-tuple-element.89, s32[1024]{0:T(1024)S(1)} %pad_clamp_fusion.2), kind=kCustom, calls=%fused_computation.clone.1 | custom fusion | bytes 16777248 | tf_op jit(solution)/shard_map/while/body/eval_jaxpr/gather | solution.py:30
  216.5 5.9 %convolution_bitcast_fusion.4 = f32[1,8,128,128]{2,3,1,0:T(8,128)S(1)} fusion(bf16[8,128,4096]{2,1,0:T(8,128)(2,1)} %gather_fusion, bf16[8,128,4096]{2,1,0:T(8,128)(2,1)} %get-tuple-element.90, s32[]{:T(128)} %get-tuple-element.80), kind=kOutput, calls=%fused_computation.1.clone.1 | convolution fusion | flops 1073741824 | bytes 9961984 | tf_op jit(solution)/shard_map/while/body/eval_jaxpr/rg,kqg->krq/dot_general | solution.py:31
  222.6 0.8 constant_dynamic-update-slice_fusion.2
  224.2 10.4 %gather_fusion = bf16[8,128,4096]{2,1,0:T(8,128)(2,1)} fusion(bf16[16,128,4096]{2,1,0:T(8,128)(2,1)} %get-tuple-element.89, s32[1024]{0:T(1024)S(1)} %pad_clamp_fusion.2), kind=kCustom, calls=%fused_computation.clone.1 | custom fusion | bytes 16777248 | tf_op jit(solution)/shard_map/while/body/eval_jaxpr/gather | solution.py:30
  234.6 5.9 %convolution_bitcast_fusion.4 = f32[1,8,128,128]{2,3,1,0:T(8,128)S(1)} fusion(bf16[8,128,4096]{2,1,0:T(8,128)(2,1)} %gather_fusion, bf16[8,128,4096]{2,1,0:T(8,128)(2,1)} %get-tuple-element.90, s32[]{:T(128)} %get-tuple-element.80), kind=kOutput, calls=%fused_computation.1.clone.1 | convolution fusion | flops 1073741824 | bytes 9961984 | tf_op jit(solution)/shard_map/while/body/eval_jaxpr/rg,kqg->krq/dot_general | solution.py:31
  240.8 0.8 constant_dynamic-update-slice_fusion.2
  242.3 10.4 %gather_fusion = bf16[8,128,4096]{2,1,0:T(8,128)(2,1)} fusion(bf16[16,128,4096]{2,1,0:T(8,128)(2,1)} %get-tuple-element.89, s32[1024]{0:T(1024)S(1)} %pad_clamp_fusion.2), kind=kCustom, calls=%fused_computation.clone.1 | custom fusion | bytes 16777248 | tf_op jit(solution)/shard_map/while/body/eval_jaxpr/gather | solution.py:30
  252.7 5.9 %convolution_bitcast_fusion.4 = f32[1,8,128,128]{2,3,1,0:T(8,128)S(1)} fusion(bf16[8,128,4096]{2,1,0:T(8,128)(2,1)} %gather_fusion, bf16[8,128,4096]{2,1,0:T(8,128)(2,1)} %get-tuple-element.90, s32[]{:T(128)} %get-tuple-element.80), kind=kOutput, calls=%fused_computation.1.clone.1 | convolution fusion | flops 1073741824 | bytes 9961984 | tf_op jit(solution)/shard_map/while/body/eval_jaxpr/rg,kqg->krq/dot_general | solution.py:31
  258.9 0.8 constant_dynamic-update-slice_fusion.2
  260.4 10.4 %gather_fusion = bf16[8,128,4096]{2,1,0:T(8,128)(2,1)} fusion(bf16[16,128,4096]{2,1,0:T(8,128)(2,1)} %get-tuple-element.89, s32[1024]{0:T(1024)S(1)} %pad_clamp_fusion.2), kind=kCustom, calls=%fused_computation.clone.1 | custom fusion | bytes 16777248 | tf_op jit(solution)/shard_map/while/body/eval_jaxpr/gather | solution.py:30
  270.9 5.9 %convolution_bitcast_fusion.4 = f32[1,8,128,128]{2,3,1,0:T(8,128)S(1)} fusion(bf16[8,128,4096]{2,1,0:T(8,128)(2,1)} %gather_fusion, bf16[8,128,4096]{2,1,0:T(8,128)(2,1)} %get-tuple-element.90, s32[]{:T(128)} %get-tuple-element.80), kind=kOutput, calls=%fused_computation.1.clone.1 | convolution fusion | flops 1073741824 | bytes 9961984 | tf_op jit(solution)/shard_map/while/body/eval_jaxpr/rg,kqg->krq/dot_general | solution.py:31
  277.0 0.8 constant_dynamic-update-slice_fusion.2
  278.6 10.4 %gather_fusion = bf16[8,128,4096]{2,1,0:T(8,128)(2,1)} fusion(bf16[16,128,4096]{2,1,0:T(8,128)(2,1)} %get-tuple-element.89, s32[1024]{0:T(1024)S(1)} %pad_clamp_fusion.2), kind=kCustom, calls=%fused_computation.clone.1 | custom fusion | bytes 16777248 | tf_op jit(solution)/shard_map/while/body/eval_jaxpr/gather | solution.py:30
  289.0 5.9 %convolution_bitcast_fusion.4 = f32[1,8,128,128]{2,3,1,0:T(8,128)S(1)} fusion(bf16[8,128,4096]{2,1,0:T(8,128)(2,1)} %gather_fusion, bf16[8,128,4096]{2,1,0:T(8,128)(2,1)} %get-tuple-element.90, s32[]{:T(128)} %get-tuple-element.80), kind=kOutput, calls=%fused_computation.1.clone.1 | convolution fusion | flops 1073741824 | bytes 9961984 | tf_op jit(solution)/shard_map/while/body/eval_jaxpr/rg,kqg->krq/dot_general | solution.py:31
  295.1 0.8 constant_dynamic-update-slice_fusion.2
  296.7 10.4 %gather_fusion = bf16[8,128,4096]{2,1,0:T(8,128)(2,1)} fusion(bf16[16,128,4096]{2,1,0:T(8,128)(2,1)} %get-tuple-element.89, s32[1024]{0:T(1024)S(1)} %pad_clamp_fusion.2), kind=kCustom, calls=%fused_computation.clone.1 | custom fusion | bytes 16777248 | tf_op jit(solution)/shard_map/while/body/eval_jaxpr/gather | solution.py:30
  307.1 5.9 %convolution_bitcast_fusion.4 = f32[1,8,128,128]{2,3,1,0:T(8,128)S(1)} fusion(bf16[8,128,4096]{2,1,0:T(8,128)(2,1)} %gather_fusion, bf16[8,128,4096]{2,1,0:T(8,128)(2,1)} %get-tuple-element.90, s32[]{:T(128)} %get-tuple-element.80), kind=kOutput, calls=%fused_computation.1.clone.1 | convolution fusion | flops 1073741824 | bytes 9961984 | tf_op jit(solution)/shard_map/while/body/eval_jaxpr/rg,kqg->krq/dot_general | solution.py:31
  313.3 0.8 constant_dynamic-update-slice_fusion.2
  (29 shorter events, 7.2 us)
Async XLA Ops:
  6.5 1.7 copy-start
  6.5 141.2 %all-gather.2.cloned.1.call-start = ((), (), s32[]{:S(2)}) async-start(), calls=%async_computation | async-start | bytes 17825792 | tf_op jit(solution)/shard_map/all_gather | solution.py:24
Sparse Core Ops, SparseCore 0:
  14.6 133.0 all-gather.1
where the time goes:
time: 322 us; the launch traced here: 321 us
  waiting for transfers between devices  133 us (41%)
  local copies, waits for them, and re-layouts  115 us (36%)
  matrix products  53.7 us (17%)
  between operations  13.4 us (4%)
  other arithmetic  5.61 us (2%)
    all_gather x1, waiting for transfers between devices, local(): gathered = lax.all_gather(precond, 'rows', axis=0, tiled=True)  133 us
    gather x8, local copies, waits for them, and re-layouts, one_block(): chosen = qblocks[ids]  83.5 us
    dot_general x8, matrix products, one_block(): jnp.einsum('rg,kqg->krq', tblock, chosen, preferred_element_type=jnp.floa...  47.5 us
    all_gather x1, local copies, waits for them, and re-layouts, local(): gathered = lax.all_gather(precond, 'rows', axis=0, tiled=True)  21.4 us
    dynamic_update_slice x16, local copies, waits for them, and re-layouts, local(): partial_scores = lax.map(one_block, (tblocks, pair_query))  8.27 us
  transfers between devices with their start and end apart: 1, of which 1 were waited for; matrix products, arithmetic and copies ran while one was open for 0% of the time, Pallas kernels for 0%

commit v1 on v0

v1 whole, which is shorter than its diff:
```python
import functools

import jax
import jax.numpy as jnp
from jax import lax
from jax.experimental import pallas as pl
from jax.experimental.pallas import tpu as pltpu
from jax.sharding import PartitionSpec as P

PROJ = 16
BLK = 128
SLOT = PROJ * PROJ
F32 = jnp.float32
BF16 = jnp.bfloat16
NT = (((1,), (1,)), ((), ()))


def split3(x):
    one = x.astype(BF16)
    rest = x - one.astype(F32)
    two = rest.astype(BF16)
    three = (rest - two.astype(F32)).astype(BF16)
    return jnp.concatenate([one, two, three], axis=1)


def factor_kernel(layers, half, slot_ref, a_ref, b_ref, q_ref, high_ref, low_ref, ready_ref, xa, xb):
    row = lax.broadcasted_iota(jnp.int32, (3 * PROJ, SLOT), 0) % PROJ
    col = lax.broadcasted_iota(jnp.int32, (3 * PROJ, SLOT), 1)
    pick_i = jnp.where(col // PROJ == row, 1.0, 0.0).astype(BF16)
    pick_o = jnp.where(col % PROJ == row, 1.0, 0.0).astype(BF16)
    xa[...] = jnp.dot(split3(a_ref[...]), pick_i, preferred_element_type=F32)
    xb[...] = jnp.dot(split3(b_ref[...]), pick_o, preferred_element_type=F32)

    @pl.loop(0, layers)
    def _(layer):
        at = pl.multiple_of(layer * PROJ, PROJ)
        left = xa[pl.ds(at, PROJ), :]
        right = xb[pl.ds(at, PROJ), :]
        full = (left[:, None, :] * right[None, :, :]).reshape(SLOT, SLOT)
        high = full.astype(BF16)
        slot = slot_ref[layer]
        high_ref[slot] = high
        low_ref[slot] = (full - high.astype(F32)).astype(BF16)

    for s in range(layers // 2):
        x = q_ref[:, half + s * SLOT : half + (s + 1) * SLOT]
        y = jnp.dot(x, high_ref[layers // 2 + s], preferred_element_type=F32)
        y += jnp.dot(x, low_ref[layers // 2 + s], preferred_element_type=F32)
        ready_ref[:, s * SLOT : (s + 1) * SLOT] = y.astype(BF16)


def make_factors(layer_slot, in_factor, out_factor, query):
    layers = in_factor.shape[0]
    half = query.shape[1] // 2
    a_rows = jnp.swapaxes(in_factor, 1, 2).reshape(layers * PROJ, PROJ)
    b_rows = out_factor.reshape(layers * PROJ, PROJ)
    vmem = pl.BlockSpec(memory_space=pltpu.VMEM)
    return pl.pallas_call(
        functools.partial(factor_kernel, layers, half),
        out_shape=[
            jax.ShapeDtypeStruct((layers, SLOT, SLOT), BF16),
            jax.ShapeDtypeStruct((layers, SLOT, SLOT), BF16),
            jax.ShapeDtypeStruct((query.shape[0], half), BF16),
        ],
        in_specs=[pl.BlockSpec(memory_space=pltpu.SMEM)] + [vmem] * 3,
        out_specs=[vmem] * 3,
        scratch_shapes=[pltpu.VMEM((layers * PROJ, SLOT), F32)] * 2,
        compiler_params=pltpu.CompilerParams(vmem_limit_bytes=24 << 20),
        cost_estimate=pl.CostEstimate(flops=3 << 29, bytes_accessed=6 << 20, transcendentals=0),
        name="factors",
    )(layer_slot, a_rows, b_rows, query)


def score_kernel(jobs, n_raw, n_ready, has_acc, emit, aliased, half, *refs):
    refs = list(refs)
    table = refs.pop(0)
    train = refs.pop(0)
    raw = [refs.pop(0) for _ in range(n_raw)]
    high = refs.pop(0) if n_raw else None
    low = refs.pop(0) if n_raw else None
    ready = [refs.pop(0) for _ in range(n_ready)]
    acc = refs.pop(0) if has_acc else None
    if aliased:
        refs.pop(0)
    out = refs.pop(0)
    t_v, q_v, raw_v, high_v, low_v, acc_v, s_v, sems, out_sems = refs
    n = len(jobs)
    depth = t_v.shape[1]
    first = 0 if n_raw else half
    blocks = t_v.shape[0] // BLK
    half_slots = half // SLOT
    copies = []

    def begin(src, dst):
        copy = pltpu.make_async_copy(src, dst, sems.at[len(copies)])
        copy.start()
        copies.append(copy)
        return copy

    waits = []
    if n_raw:
        for j, ref in enumerate(raw):
            waits.append(begin(ref, raw_v.at[pl.ds(j * BLK, BLK)]))
        waits.append(begin(high.at[pl.ds(0, half_slots)], high_v))
        waits.append(begin(low.at[pl.ds(0, half_slots)], low_v))
    later = []
    for j, ref in enumerate(ready):
        later.append(begin(ref, q_v.at[pl.ds(j * BLK, BLK), pl.ds(depth - half, half)]))
    step = 2 * BLK
    loads = []
    for m in range(t_v.shape[0] // step):
        loads.append(begin(train.at[pl.ds(m * step, step), pl.ds(first, depth)], t_v.at[pl.ds(m * step, step)]))
    if has_acc:
        acc_load = begin(acc, acc_v)
    for copy in waits:
        copy.wait()
    if n_raw:
        for s in range(half_slots):
            cols = slice(s * SLOT, (s + 1) * SLOT)
            x = raw_v[:, cols]
            y = jnp.dot(x, high_v[s], preferred_element_type=F32)
            y += jnp.dot(x, low_v[s], preferred_element_type=F32)
            q_v[:, cols] = y.astype(BF16)
    for copy in later:
        copy.wait()
    if has_acc:
        acc_load.wait()

    def put(t, j):
        return pltpu.make_async_copy(s_v.at[t, j], out.at[t, jnp.maximum(table[t, jobs[j]], 0)], out_sems.at[t, j])

    for m in range(t_v.shape[0] // step):
        loads[m].wait()
        s = lax.dot_general(t_v[m * step : (m + 1) * step], q_v[...], NT, preferred_element_type=F32)
        for u in range(step // BLK):
            t = m * (step // BLK) + u
            for j in range(n):
                part = s[u * BLK : (u + 1) * BLK, j * BLK : (j + 1) * BLK]
                if has_acc:
                    part += acc_v[t, j]
                if not emit:
                    out[t, j] = part
                else:
                    s_v[t, j] = part

                    @pl.when(table[t, jobs[j]] >= 0)
                    def _(t=t, j=j):
                        put(t, j).start()

    if emit:
        for t in range(blocks):
            for j in range(n):

                @pl.when(table[t, jobs[j]] >= 0)
                def _(t=t, j=j):
                    put(t, j).wait()


def score(table, train, jobs, raw=(), ready=(), factors=None, acc=None, out=None, emit=True, name="score"):
    n = len(jobs)
    rows, width = train.shape
    half = width // 2
    blocks = rows // BLK
    depth = half * (bool(raw) + bool(ready))
    any_spec = pl.BlockSpec(memory_space=pl.ANY)
    args = [table, train, *raw]
    if raw:
        args += list(factors)
    args += list(ready)
    if acc is not None:
        args.append(acc)
    aliases = {}
    if out is not None:
        aliases = {len(args): 0}
        args.append(out)
    if emit:
        shape, out_spec = (blocks, table.shape[1] // 2, BLK, BLK), any_spec
    else:
        shape, out_spec = (blocks, n, BLK, BLK), pl.BlockSpec(memory_space=pltpu.VMEM)
    slots = half // SLOT if raw else 1
    flat = (slots, SLOT, SLOT) if raw else (1, 16, 128)
    small = (16, 128)
    scratch = [
        pltpu.VMEM((rows, depth), BF16),
        pltpu.VMEM((n * BLK, depth), BF16),
        pltpu.VMEM((n * BLK, half) if raw else small, BF16),
        pltpu.VMEM(flat, BF16),
        pltpu.VMEM(flat, BF16),
        pltpu.VMEM((blocks, n, BLK, BLK) if acc is not None else (1, 1, 8, 128), F32),
        pltpu.VMEM((blocks, n, BLK, BLK) if emit else (1, 1, 8, 128), F32),
        pltpu.SemaphoreType.DMA((len(raw) + len(ready) + 8 + rows // (2 * BLK),)),
        pltpu.SemaphoreType.DMA((blocks, n)),
    ]
    body = functools.partial(
        score_kernel, tuple(jobs), len(raw), len(ready), acc is not None, emit, out is not None, half
    )
    return pl.pallas_call(
        body,
        out_shape=jax.ShapeDtypeStruct(shape, F32),
        in_specs=[pl.BlockSpec(memory_space=pltpu.SMEM)] + [any_spec] * (len(args) - 1),
        out_specs=out_spec,
        scratch_shapes=scratch,
        input_output_aliases=aliases,
        compiler_params=pltpu.CompilerParams(vmem_limit_bytes=32 << 20),
        cost_estimate=pl.CostEstimate(
            flops=2 * rows * n * BLK * depth, bytes_accessed=2 * rows * depth, transcendentals=0
        ),
        name=name,
    )(*args)


def after(x, *deps):
    return lax.optimization_barrier((x, *deps))[0]


def local_rings(train_grads, query_grads, pair_query, layer_slot, in_factor, out_factor):
    count = lax.axis_size("rows")
    me = lax.axis_index("rows")
    core, col, layer = me % 2, me // 2 % 2, me // 4
    height = count // 4

    def index(z, y, c):
        return (z % height * 2 + y) * 2 + c

    def ring(move):
        return [(i, index(*move(i // 4, i // 2 % 2, i % 2))) for i in range(count)]

    down = ring(lambda z, y, c: (z - 1, y, c))
    up = ring(lambda z, y, c: (z + 1, y, c))
    across = ring(lambda z, y, c: (z, 1 - y, c))
    twin = ring(lambda z, y, c: (z, y, 1 - c))

    def send(x, perm):
        return lax.ppermute(x, "rows", perm)

    places = [(dz, dy) for dz in (0, 1, -1, 2) for dy in (0, 1)]
    ids = jnp.stack([index(layer + dz, (col + dy) % 2, (core + dc) % 2) for dz, dy in places for dc in (0, 1)])
    slots = jnp.arange(1, pair_query.shape[1] + 1, dtype=jnp.int32)
    named = pair_query[:, :, None] == ids[None, None, :]
    table = jnp.sum(jnp.where(named, slots[None, :, None], 0), axis=1) - 1
    job = {place: (2 * i, 2 * i + 1) for i, place in enumerate(places)}

    half = query_grads.shape[1] // 2
    raw = query_grads[:, :half]
    got = {"h0": raw}
    links = {
        "z": [("a0", "h0", down), ("b0", "h0", up), ("b1", "h1", up), ("f0", "a0", down), ("f1", "b1", up), ("a1", "h1", down), ("xa1", "y1", down)],
        "y": [("y0", "h0", across), ("y1", "h1", across), ("ya0", "a0", across), ("yb0", "b0", across), ("yb1", "b1", across), ("yf0", "f0", across), ("yf1", "f1", across)],
    }
    steps = len(links["z"])
    blocks = {
        (0, 0): ("h0", "h1"), (0, 1): ("y0", "y1"), (1, 0): ("a0", "a1"), (1, 1): ("ya0", "xa1"),
        (-1, 0): ("b0", "b1"), (-1, 1): ("yb0", "yb1"), (2, 0): ("f0", "f1"), (2, 1): ("yf0", "yf1"),
    }
    factors = None
    for s in range(steps):
        for way in ("z", "y"):
            name, source, perm = links[way][s]
            if source == "h1" and "h1" not in got:
                high, low, got["h1"] = make_factors(layer_slot, in_factor, out_factor, query_grads)
                factors = (high, low)
                for own in ("h0", "h1"):
                    got["c" + own] = send(got[own], twin)
            x = got[source]
            if s >= 2:
                past = [got[links[w][s - 2][0]] for w in ("z", "y")]
                x = after(x, *[v for v in past if v is not x])
            got[name] = send(x, perm)
            got["c" + name] = send(got[name], twin)

    def whole(place, out):
        first, second = blocks[place]
        return score(
            table, train_grads, job[place], raw=(got[first], got["c" + first]),
            ready=(got[second], got["c" + second]), factors=factors, out=out, name="score_pair",
        )

    out = None
    for place in ((0, 0), (0, 1), (-1, 0), (-1, 1), (2, 0), (1, 0)):
        out = whole(place, out)
    own = [job[(1, 1)][0], job[(2, 1)][0]]
    other = [job[(1, 1)][1], job[(2, 1)][1]]
    acc = [
        score(table, train_grads, jobs, raw=[got[p + n] for n in ("ya0", "yf0")], factors=factors, emit=False, name="score_first")
        for jobs, p in ((own, ""), (other, "c"))
    ]
    for jobs, p, part in ((own, "", acc[0]), (other, "c", acc[1])):
        out = score(table, train_grads, jobs, ready=[got[p + n] for n in ("xa1", "yf1")], acc=part, out=out, name="score_second")
    return out


def local(train_grads, query_grads, pair_query, layer_slot, in_factor, out_factor):
    dims_count = lax.axis_size("dims")
    dims_index = lax.axis_index("dims")
    width = query_grads.shape[1]
    local_layers = width // SLOT
    slots = dims_index * local_layers + jnp.arange(local_layers, dtype=jnp.int32)
    onehot = (slots[:, None] == layer_slot[None, :]).astype(F32)
    a_fac = jnp.einsum("sl,lij->sij", onehot, in_factor, precision=lax.Precision.HIGHEST)
    b_fac = jnp.einsum("sl,lij->sij", onehot, out_factor, precision=lax.Precision.HIGHEST)
    nrow = query_grads.shape[0]
    query = query_grads.astype(F32).reshape(nrow, local_layers, PROJ, PROJ)
    left = jnp.einsum("sia,rsab->rsib", a_fac, query, precision=lax.Precision.HIGHEST)
    both = jnp.einsum("rsib,sbo->rsio", left, b_fac, precision=lax.Precision.HIGHEST)
    precond = both.reshape(nrow, width).astype(BF16)
    gathered = lax.all_gather(precond, "rows", axis=0, tiled=True)
    qblocks = gathered.reshape(gathered.shape[0] // BLK, BLK, width)
    tblocks = train_grads.reshape(train_grads.shape[0] // BLK, BLK, width)

    def one_block(items):
        tblock, ids = items
        chosen = qblocks[ids]
        return jnp.einsum("rg,kqg->krq", tblock, chosen, preferred_element_type=F32)

    partial_scores = lax.map(one_block, (tblocks, pair_query))
    summed = lax.psum(partial_scores, "dims")
    share = BLK // dims_count
    return lax.dynamic_slice_in_dim(summed, dims_index * share, share, 2)


def solution(mesh):
    in_specs = (
        P(("shard", "rows"), "dims"),
        P(("shard", "rows"), "dims"),
        P(("shard", "rows"), None),
        P(),
        P(),
        P(),
    )
    out_specs = P(("shard", "rows"), None, "dims", None)
    four = mesh.shape["rows"] == 16 and mesh.shape["dims"] == 1
    body = local_rings if four else local
    return jax.shard_map(body, mesh=mesh, in_specs=in_specs, out_specs=out_specs, check_vma=False)
```

time: 322 us -> 175 us (0.54)
  local copies, waits for them, and re-layouts: 115 us -> 19.9 us
  waiting for transfers between devices: 133 us -> 43.2 us
  Pallas kernels: 0 us -> 70.9 us
  matrix products: 53.7 us -> 0 us
  starting transfers between devices: 0.01 us -> 39.1 us
  between operations: 13.4 us -> 0.57 us
  other arithmetic: 5.61 us -> 0.09 us
    all_gather x1 -> x0, waiting for transfers between devices: 133 us -> none  [local(): gathered = lax.all_gather(precond, 'rows', axis=0, tiled=True)]
    gather x8 -> x0, local copies, waits for them, and re-layouts: 83.5 us -> none  [one_block(): chosen = qblocks[ids]]
    pallas_call x0 -> x11, Pallas kernels: none -> 70.9 us  [the longest x10 68.8 us: score(): pl.pallas_call(body, out_shape=jax.ShapeDtypeStruct(shape, F32), in_specs...]
    dot_general x12 -> x0, matrix products: 53.7 us -> none  [the longest x8 47.5 us: one_block(): jnp.einsum('rg,kqg->krq', tblock, chosen, preferred_element_type=jnp.floa...]
    ppermute x0 -> x30, waiting for transfers between devices: none -> 43.2 us  [send(): return lax.ppermute(x, 'rows', perm)]
    ppermute x0 -> x30, starting transfers between devices: none -> 39.1 us  [send(): return lax.ppermute(x, 'rows', perm)]
    all_gather x1 -> x0, local copies, waits for them, and re-layouts: 21.4 us -> none  [local(): gathered = lax.all_gather(precond, 'rows', axis=0, tiled=True)]
    unnamed x3 -> x64, local copies, waits for them, and re-layouts: 1.65 us -> 18.7 us
  transfers between devices with their start and end apart: 1 -> 30, of which waited for: 1 -> 7; matrix products, arithmetic and copies ran while one was open for 0% -> 0% of each run, Pallas kernels for 0% -> 37%
where the time goes in v1:
time: 175 us; the launch traced here: 174 us
  Pallas kernels  70.9 us (41%)
  waiting for transfers between devices  43.2 us (25%)
  starting transfers between devices  39.1 us (22%)
  local copies, waits for them, and re-layouts  19.9 us (11%)
    pallas_call x10, Pallas kernels, score(): pl.pallas_call(body, out_shape=jax.ShapeDtypeStruct(shape, F32), in_specs...  68.8 us
    ppermute x30, waiting for transfers between devices, send(): return lax.ppermute(x, 'rows', perm)  43.2 us
    ppermute x30, starting transfers between devices, send(): return lax.ppermute(x, 'rows', perm)  39.1 us
    unnamed x64, local copies, waits for them, and re-layouts  18.7 us
  transfers between devices with their start and end apart: 30, of which 7 were waited for; matrix products, arithmetic and copies ran while one was open for 0% of the time, Pallas kernels for 37%

profile of v1, /device:TPU:0, one launch (start us, length us, event | category | flops | bytes accessed | tf_op | source)
XLA Modules:
  0.0 173.7 jit_solution(2937430190145291589)
XLA Ops:
  1.0 1.2 copy-done.27
  3.8 2.1 %factors.1 = (bf16[16,256,256]{2,1,0:T(8,128)(2,1)S(1)}, bf16[16,256,256]{2,1,0:T(8,128)(2,1)S(1)}, bf16[128,2048]{1,0:T(8,128)(2,1)S(1)}) custom-call(s32[16]{0:T(128)S(1)} %copy-done.30, f32[256,16]{1,0:T(8,128)S(1)} %bitcast.19, f32[256,16]{1,0:T(8,128)S(1)} %bitcast.20, bf16[128,4096]{1,0:T(8,128)(2,1)S(1)} %copy-done.27), custom_call_target="tpu_custom_call" | custom-call | flops 1610612736 | bytes 6291456 | tf_op jit(solution)/shard_map/factors/pallas_call | solution.py:58
  5.9 1.3 copy-done.2
  7.3 3.0 %collective-permute-start = (bf16[128,2048]{1,0:T(8,128)(2,1)S(1)}, bf16[128,2048]{1,0:T(8,128)(2,1)S(1)}, u32[]{:S(2)}, u32[]{:S(2)}) collective-permute-start(bf16[128,2048]{1,0:T(8,128)(2,1)S(1)} %get-tuple-element.28.refs_6_), channel_id=1, source_target_pairs={{0,2},{1,3},{2,0},{3,1},{4,6},{5,7},{6,4},{7,5},{8,10},{9,11},{10,... | collective-permute-start | bytes 1572872 | tf_op jit(solution)/shard_map/ppermute | solution.py:234
  10.4 4.1 %collective-permute-start.1 = (bf16[128,2048]{1,0:T(8,128)(2,1)S(1)}, bf16[128,2048]{1,0:T(8,128)(2,1)S(1)}, u32[]{:S(2)}, u32[]{:S(2)}) collective-permute-start(bf16[128,2048]{1,0:T(8,128)(2,1)S(1)} %slice.3.refs_2_), channel_id=1, source_target_pairs={{0,12},{1,13},{2,14},{3,15},{4,0},{5,1},{6,2},{7,3},{8,4},{9,5},{1... | collective-permute-start | bytes 1572872 | tf_op jit(solution)/shard_map/ppermute | solution.py:234
  15.0 8.0 %collective-permute-done.refs_6_ = bf16[128,2048]{1,0:T(8,128)(2,1)S(1)} collective-permute-done((bf16[128,2048]{1,0:T(8,128)(2,1)S(1)}, bf16[128,2048]{1,0:T(8,128)(2,1)S(1)}, u32[]{:S(2)}, u32[]{:S(2)}) %collective-permute-start) | collective-permute-done | bytes 524320 | tf_op jit(solution)/shard_map/ppermute | solution.py:234
  23.0 2.1 %collective-permute-start.12 = (bf16[128,2048]{1,0:T(8,128)(2,1)S(1)}, bf16[128,2048]{1,0:T(8,128)(2,1)S(1)}, u32[]{:S(2)}, u32[]{:S(2)}) collective-permute-start(bf16[128,2048]{1,0:T(8,128)(2,1)S(1)} %slice.3.refs_2_), channel_id=1, source_target_pairs={{0,4},{1,5},{2,6},{3,7},{4,8},{5,9},{6,10},{7,11},{8,12},{9,13},{1... | collective-permute-start | bytes 1572872 | tf_op jit(solution)/shard_map/ppermute | solution.py:234
  25.1 8.3 %collective-permute-done.2.refs_2_ = bf16[128,2048]{1,0:T(8,128)(2,1)S(1)} collective-permute-done((bf16[128,2048]{1,0:T(8,128)(2,1)S(1)}, bf16[128,2048]{1,0:T(8,128)(2,1)S(1)}, u32[]{:S(2)}, u32[]{:S(2)}) %collective-permute-start.2) | collective-permute-done | bytes 524320 | tf_op jit(solution)/shard_map/ppermute | solution.py:234
  35.5 1.8 %collective-permute-start.3 = (bf16[128,2048]{1,0:T(8,128)(2,1)S(1)}, bf16[128,2048]{1,0:T(8,128)(2,1)}, u32[]{:S(2)}, u32[]{:S(2)}) collective-permute-start(bf16[128,2048]{1,0:T(8,128)(2,1)S(1)} %get-tuple-element.28.refs_6_), channel_id=1, source_target_pairs={{0,4},{1,5},{2,6},{3,7},{4,8},{5,9},{6,10},{7,11},{8,12},{9,13},{1... | collective-permute-start | bytes 1572872 | tf_op jit(solution)/shard_map/ppermute | solution.py:234
  38.1 1.5 collective-permute-start.4
  42.7 2.0 %collective-permute-start.13 = (bf16[128,2048]{1,0:T(8,128)(2,1)S(1)}, bf16[128,2048]{1,0:T(8,128)(2,1)S(1)}, u32[]{:S(2)}, u32[]{:S(2)}) collective-permute-start(bf16[128,2048]{1,0:T(8,128)(2,1)S(1)} %collective-permute-done.1.refs_2_), channel_id=1, source_target_pairs={{0,12},{1,13},{2,14},{3,15},{4,0},{5,1},{6,2},{7,3},{8,4},{9,5},{1... | collective-permute-start | bytes 1572872 | tf_op jit(solution)/shard_map/ppermute | solution.py:234
  44.7 7.6 %collective-permute-done.3.refs_6_ = bf16[128,2048]{1,0:T(8,128)(2,1)} collective-permute-done((bf16[128,2048]{1,0:T(8,128)(2,1)S(1)}, bf16[128,2048]{1,0:T(8,128)(2,1)}, u32[]{:S(2)}, u32[]{:S(2)}) %collective-permute-start.3) | collective-permute-done | bytes 524320 | tf_op jit(solution)/shard_map/ppermute | solution.py:234
  54.6 1.6 collective-permute-start.6
  56.1 8.2 %collective-permute-done.14.refs_2_ = bf16[128,2048]{1,0:T(8,128)(2,1)} collective-permute-done((bf16[128,2048]{1,0:T(8,128)(2,1)S(1)}, bf16[128,2048]{1,0:T(8,128)(2,1)}, u32[]{:S(2)}, u32[]{:S(2)}) %collective-permute-start.14) | collective-permute-done | bytes 524320 | tf_op jit(solution)/shard_map/ppermute | solution.py:234
  64.3 1.6 collective-permute-start.5
  66.1 3.1 %collective-permute-start.18 = (bf16[128,2048]{1,0:T(8,128)(2,1)}, bf16[128,2048]{1,0:T(8,128)(2,1)S(1)}, u32[]{:S(2)}, u32[]{:S(2)}) collective-permute-start(bf16[128,2048]{1,0:T(8,128)(2,1)} %copy-done.9), channel_id=1, source_target_pairs={{0,12},{1,13},{2,14},{3,15},{4,0},{5,1},{6,2},{7,3},{8,4},{9,5},{1... | collective-permute-start | bytes 1572872 | tf_op jit(solution)/shard_map/ppermute | solution.py:234
  69.5 4.8 %collective-permute-done.6.refs_6_ = bf16[128,2048]{1,0:T(8,128)(2,1)} collective-permute-done((bf16[128,2048]{1,0:T(8,128)(2,1)}, bf16[128,2048]{1,0:T(8,128)(2,1)}, u32[]{:S(2)}, u32[]{:S(2)}) %collective-permute-start.6) | collective-permute-done | bytes 524320 | tf_op jit(solution)/shard_map/ppermute | solution.py:234
  74.3 1.5 collective-permute-start.15
  75.8 5.6 %collective-permute-done.5.refs_6_ = bf16[128,2048]{1,0:T(8,128)(2,1)} collective-permute-done((bf16[128,2048]{1,0:T(8,128)(2,1)}, bf16[128,2048]{1,0:T(8,128)(2,1)}, u32[]{:S(2)}, u32[]{:S(2)}) %collective-permute-start.5) | collective-permute-done | bytes 524320 | tf_op jit(solution)/shard_map/ppermute | solution.py:234
  81.4 3.4 %copy-done = bf16[1024,4096]{1,0:T(8,128)(2,1)S(1)} copy-done((bf16[1024,4096]{1,0:T(8,128)(2,1)S(1)}, bf16[1024,4096]{1,0:T(8,128)(2,1)}, u32[]{:S(2)}) %copy-start) | copy-done | bytes 8388632
  84.8 1.6 copy-done.3
  89.5 8.2 %score_pair.6.refs_8_ = f32[8,8,128,128]{3,2,1,0:T(8,128)} custom-call(s32[8,16]{1,0:T(8,128)S(1)} %broadcast_add_fusion.refs_0_, bf16[1024,4096]{1,0:T(8,128)(2,1)S(1)} %copy-done, bf16[128,2048]{1,0:T(8,128)(2,1)S(1)} %slice.3.refs_2_, bf16[128,2048]{1,0:T(8,128)(2,1)S(1)} %copy-done.22, bf16[16,256,256]{2,1,0:T(8,128)(2,1)S(1)} %get-tuple-element.26.refs_4_, ...), custom_call_target="tpu_custom_call" | custom-call | flops 2147483648 | bytes 8388608 | tf_op jit(solution)/shard_map/score_pair/pallas_call | solution.py:197
  97.7 12.9 %collective-permute-start.7 = (bf16[128,2048]{1,0:T(8,128)(2,1)S(1)}, bf16[128,2048]{1,0:T(8,128)(2,1)S(1)}, u32[]{:S(2)}, u32[]{:S(2)}) collective-permute-start(bf16[128,2048]{1,0:T(8,128)(2,1)S(1)} %copy-done.6), channel_id=1, source_target_pairs={{0,12},{1,13},{2,14},{3,15},{4,0},{5,1},{6,2},{7,3},{8,4},{9,5},{1... | collective-permute-start | bytes 1572872 | tf_op jit(solution)/shard_map/ppermute | solution.py:234
  110.7 7.6 %score_pair.7.refs_8_ = f32[8,8,128,128]{3,2,1,0:T(8,128)} custom-call(s32[8,16]{1,0:T(8,128)S(1)} %broadcast_add_fusion.refs_0_, bf16[1024,4096]{1,0:T(8,128)(2,1)S(1)} %copy-done.1, bf16[128,2048]{1,0:T(8,128)(2,1)S(1)} %copy-done.12, bf16[128,2048]{1,0:T(8,128)(2,1)S(1)} %copy-done.24, ...), custom_call_target="tpu_custom_call", output_to_operand_aliasing={{}: (8, {})} | custom-call | flops 2147483648 | bytes 8388608 | tf_op jit(solution)/shard_map/score_pair/pallas_call | solution.py:197
  119.2 8.1 %score_pair.8.refs_8_ = f32[8,8,128,128]{3,2,1,0:T(8,128)} custom-call(s32[8,16]{1,0:T(8,128)S(1)} %broadcast_add_fusion.refs_0_, bf16[1024,4096]{1,0:T(8,128)(2,1)S(1)} %copy-done.1, bf16[128,2048]{1,0:T(8,128)(2,1)S(1)} %copy-done.14, bf16[128,2048]{1,0:T(8,128)(2,1)S(1)} %copy-done.26, ...), custom_call_target="tpu_custom_call", output_to_operand_aliasing={{}: (8, {})} | custom-call | flops 2147483648 | bytes 8388608 | tf_op jit(solution)/shard_map/score_pair/pallas_call | solution.py:197
  127.3 5.1 %score_first.3.refs_4_ = f32[8,2,128,128]{3,2,1,0:T(8,128)S(1)} custom-call(s32[8,16]{1,0:T(8,128)S(1)} %broadcast_add_fusion.refs_0_, bf16[1024,4096]{1,0:T(8,128)(2,1)S(1)} %copy-done.1, bf16[128,2048]{1,0:T(8,128)(2,1)S(1)} %copy-done.8, bf16[128,2048]{1,0:T(8,128)(2,1)S(1)} %collective-permute-done.15.refs_3_, ...), custom_call_target="tpu_custom_call" | custom-call | flops 1073741824 | bytes 4194304 | tf_op jit(solution)/shard_map/score_first/pallas_call | solution.py:197
  133.0 8.5 %score_pair.9.refs_8_ = f32[8,8,128,128]{3,2,1,0:T(8,128)} custom-call(s32[8,16]{1,0:T(8,128)S(1)} %broadcast_add_fusion.refs_0_, bf16[1024,4096]{1,0:T(8,128)(2,1)S(1)} %copy-done.1, bf16[128,2048]{1,0:T(8,128)(2,1)} %collective-permute-done.14.refs_2_, bf16[128,2048]{1,0:T(8,128)(2,1)} %collective-permute-done.22.refs_3_, ...), custom_call_target="tpu_custom_call", output_to_operand_aliasing={{}: (8, {})} | custom-call | flops 2147483648 | bytes 8388608 | tf_op jit(solution)/shard_map/score_pair/pallas_call | solution.py:197
  142.1 8.3 %score_pair.10.refs_8_ = f32[8,8,128,128]{3,2,1,0:T(8,128)} custom-call(s32[8,16]{1,0:T(8,128)S(1)} %broadcast_add_fusion.refs_0_, bf16[1024,4096]{1,0:T(8,128)(2,1)S(1)} %copy-done.1, bf16[128,2048]{1,0:T(8,128)(2,1)S(1)} %copy-done.16, bf16[128,2048]{1,0:T(8,128)(2,1)S(1)} %collective-permute-done.20.refs_3_, ...), custom_call_target="tpu_custom_call", output_to_operand_aliasing={{}: (8, {})} | custom-call | flops 2147483648 | bytes 8388608 | tf_op jit(solution)/shard_map/score_pair/pallas_call | solution.py:197
  150.4 8.4 %score_pair.11.refs_5_ = f32[8,8,128,128]{3,2,1,0:T(8,128)} custom-call(s32[8,16]{1,0:T(8,128)S(1)} %broadcast_add_fusion.refs_0_, bf16[1024,4096]{1,0:T(8,128)(2,1)S(1)} %copy-done.1, bf16[128,2048]{1,0:T(8,128)(2,1)S(1)} %collective-permute-done.1.refs_2_, bf16[128,2048]{1,0:T(8,128)(2,1)} %collective-permute-done.17.refs_3_, ...), custom_call_target="tpu_custom_call", output_to_operand_aliasing={{}: (8, {})} | custom-call | flops 2147483648 | bytes 8388608 | tf_op jit(solution)/shard_map/score_pair/pallas_call | solution.py:197
  158.8 5.0 %score_second.2.refs_5_ = f32[8,8,128,128]{3,2,1,0:T(8,128)} custom-call(s32[8,16]{1,0:T(8,128)S(1)} %broadcast_add_fusion.refs_0_, bf16[1024,4096]{1,0:T(8,128)(2,1)S(1)} %copy-done.1, bf16[128,2048]{1,0:T(8,128)(2,1)S(1)} %collective-permute-done.7.refs_2_, bf16[128,2048]{1,0:T(8,128)(2,1)S(1)} %collective-permute-done.9.refs_3_, ...), custom_call_target="tpu_custom_call", output_to_operand_aliasing={{}: (5, {})} | custom-call | flops 1073741824 | bytes 4194304 | tf_op jit(solution)/shard_map/score_second/pallas_call | solution.py:197
  163.9 5.1 %score_first.2.refs_4_ = f32[8,2,128,128]{3,2,1,0:T(8,128)S(1)} custom-call(s32[8,16]{1,0:T(8,128)S(1)} %broadcast_add_fusion.refs_0_, bf16[1024,4096]{1,0:T(8,128)(2,1)S(1)} %copy-done.1, bf16[128,2048]{1,0:T(8,128)(2,1)S(1)} %collective-permute-done.11.refs_2_, bf16[128,2048]{1,0:T(8,128)(2,1)S(1)} %collective-permute-done.16.refs_3_, ...), custom_call_target="tpu_custom_call" | custom-call | flops 1073741824 | bytes 4194304 | tf_op jit(solution)/shard_map/score_first/pallas_call | solution.py:197
  169.1 4.4 %score_second.3 = f32[8,8,128,128]{3,2,1,0:T(8,128)} custom-call(s32[8,16]{1,0:T(8,128)S(1)} %broadcast_add_fusion.refs_0_, bf16[1024,4096]{1,0:T(8,128)(2,1)S(1)} %copy-done.1, bf16[128,2048]{1,0:T(8,128)(2,1)S(1)} %collective-permute-done.8.refs_2_, bf16[128,2048]{1,0:T(8,128)(2,1)S(1)} %collective-permute-done.10.refs_3_, ...), custom_call_target="tpu_custom_call", output_to_operand_aliasing={{}: (5, {})} | custom-call | flops 1073741824 | bytes 4194304 | tf_op jit(solution)/shard_map/score_second/pallas_call | solution.py:197
  (109 shorter events, 17.0 us)
Async XLA Ops:
  0.0 69.4 %copy-start.31 = (s32[8,8]{1,0:T(8,128)S(1)}, s32[8,8]{1,0:T(8,128)}, u32[]{:S(2)}) copy-start(s32[8,8]{1,0:T(8,128)} %param.8) | copy-start | bytes 772
  7.3 58.7 %copy-start.9 = (bf16[128,2048]{1,0:T(8,128)(2,1)}, bf16[128,2048]{1,0:T(8,128)(2,1)S(1)}, u32[]{:S(2)}) copy-start(bf16[128,2048]{1,0:T(8,128)(2,1)S(1)} %get-tuple-element.28.refs_6_) | copy-start | bytes 1572868
  7.3 15.7 %collective-permute-start = (bf16[128,2048]{1,0:T(8,128)(2,1)S(1)}, bf16[128,2048]{1,0:T(8,128)(2,1)S(1)}, u32[]{:S(2)}, u32[]{:S(2)}) collective-permute-start(bf16[128,2048]{1,0:T(8,128)(2,1)S(1)} %get-tuple-element.28.refs_6_), channel_id=1, source_target_pairs={{0,2},{1,3},{2,0},{3,1},{4,6},{5,7},{6,4},{7,5},{8,10},{9,11},{10,... | collective-permute-start | bytes 1572872 | tf_op jit(solution)/shard_map/ppermute | solution.py:234
  10.3 23.1 %collective-permute-start.2 = (bf16[128,2048]{1,0:T(8,128)(2,1)S(1)}, bf16[128,2048]{1,0:T(8,128)(2,1)S(1)}, u32[]{:S(2)}, u32[]{:S(2)}) collective-permute-start(bf16[128,2048]{1,0:T(8,128)(2,1)S(1)} %slice.3.refs_2_), channel_id=1, source_target_pairs={{0,2},{1,3},{2,0},{3,1},{4,6},{5,7},{6,4},{7,5},{8,10},{9,11},{10,... | collective-permute-start | bytes 1572872 | tf_op jit(solution)/shard_map/ppermute | solution.py:234
  10.4 23.0 %collective-permute-start.1 = (bf16[128,2048]{1,0:T(8,128)(2,1)S(1)}, bf16[128,2048]{1,0:T(8,128)(2,1)S(1)}, u32[]{:S(2)}, u32[]{:S(2)}) collective-permute-start(bf16[128,2048]{1,0:T(8,128)(2,1)S(1)} %slice.3.refs_2_), channel_id=1, source_target_pairs={{0,12},{1,13},{2,14},{3,15},{4,0},{5,1},{6,2},{7,3},{8,4},{9,5},{1... | collective-permute-start | bytes 1572872 | tf_op jit(solution)/shard_map/ppermute | solution.py:234
  14.5 20.3 %collective-permute-start.29 = (bf16[128,2048]{1,0:T(8,128)(2,1)S(1)}, bf16[128,2048]{1,0:T(8,128)(2,1)S(1)}, u32[]{:S(2)}, u32[]{:S(2)}) collective-permute-start(bf16[128,2048]{1,0:T(8,128)(2,1)S(1)} %get-tuple-element.28.refs_6_), channel_id=1, source_target_pairs={{0,1},{1,0},{2,3},{3,2},{4,5},{5,4},{6,7},{7,6},{8,9},{9,8},{10,11... | collective-permute-start | bytes 1572872 | tf_op jit(solution)/shard_map/ppermute | solution.py:234
  14.5 22.9 %collective-permute-start.28 = (bf16[128,2048]{1,0:T(8,128)(2,1)S(1)}, bf16[128,2048]{1,0:T(8,128)(2,1)S(1)}, u32[]{:S(2)}, u32[]{:S(2)}) collective-permute-start(bf16[128,2048]{1,0:T(8,128)(2,1)S(1)} %slice.3.refs_2_), channel_id=1, source_target_pairs={{0,1},{1,0},{2,3},{3,2},{4,5},{5,4},{6,7},{7,6},{8,9},{9,8},{10,11... | collective-permute-start | bytes 1572872 | tf_op jit(solution)/shard_map/ppermute | solution.py:234
  23.0 16.6 %collective-permute-start.12 = (bf16[128,2048]{1,0:T(8,128)(2,1)S(1)}, bf16[128,2048]{1,0:T(8,128)(2,1)S(1)}, u32[]{:S(2)}, u32[]{:S(2)}) collective-permute-start(bf16[128,2048]{1,0:T(8,128)(2,1)S(1)} %slice.3.refs_2_), channel_id=1, source_target_pairs={{0,4},{1,5},{2,6},{3,7},{4,8},{5,9},{6,10},{7,11},{8,12},{9,13},{1... | collective-permute-start | bytes 1572872 | tf_op jit(solution)/shard_map/ppermute | solution.py:234
  33.4 6.2 %collective-permute-start.27 = (bf16[128,2048]{1,0:T(8,128)(2,1)S(1)}, bf16[128,2048]{1,0:T(8,128)(2,1)S(1)}, u32[]{:S(2)}, u32[]{:S(2)}) collective-permute-start(bf16[128,2048]{1,0:T(8,128)(2,1)S(1)} %collective-permute-done.refs_6_), channel_id=1, source_target_pairs={{0,1},{1,0},{2,3},{3,2},{4,5},{5,4},{6,7},{7,6},{8,9},{9,8},{10,11... | collective-permute-start | bytes 1572872 | tf_op jit(solution)/shard_map/ppermute | solution.py:234
  33.4 8.4 %collective-permute-start.26 = (bf16[128,2048]{1,0:T(8,128)(2,1)S(1)}, bf16[128,2048]{1,0:T(8,128)(2,1)S(1)}, u32[]{:S(2)}, u32[]{:S(2)}) collective-permute-start(bf16[128,2048]{1,0:T(8,128)(2,1)S(1)} %collective-permute-done.2.refs_2_), channel_id=1, source_target_pairs={{0,1},{1,0},{2,3},{3,2},{4,5},{5,4},{6,7},{7,6},{8,9},{9,8},{10,11... | collective-permute-start | bytes 1572872 | tf_op jit(solution)/shard_map/ppermute | solution.py:234
  35.5 16.7 %collective-permute-start.3 = (bf16[128,2048]{1,0:T(8,128)(2,1)S(1)}, bf16[128,2048]{1,0:T(8,128)(2,1)}, u32[]{:S(2)}, u32[]{:S(2)}) collective-permute-start(bf16[128,2048]{1,0:T(8,128)(2,1)S(1)} %get-tuple-element.28.refs_6_), channel_id=1, source_target_pairs={{0,4},{1,5},{2,6},{3,7},{4,8},{5,9},{6,10},{7,11},{8,12},{9,13},{1... | collective-permute-start | bytes 1572872 | tf_op jit(solution)/shard_map/ppermute | solution.py:234
  38.1 14.8 %collective-permute-start.4 = (bf16[128,2048]{1,0:T(8,128)(2,1)S(1)}, bf16[128,2048]{1,0:T(8,128)(2,1)S(1)}, u32[]{:S(2)}, u32[]{:S(2)}) collective-permute-start(bf16[128,2048]{1,0:T(8,128)(2,1)S(1)} %collective-permute-done.1.refs_2_), channel_id=1, source_target_pairs={{0,2},{1,3},{2,0},{3,1},{4,6},{5,7},{6,4},{7,5},{8,10},{9,11},{10,... | collective-permute-start | bytes 1572872 | tf_op jit(solution)/shard_map/ppermute | solution.py:234
  39.7 14.1 %collective-permute-start.24 = (bf16[128,2048]{1,0:T(8,128)(2,1)S(1)}, bf16[128,2048]{1,0:T(8,128)(2,1)S(1)}, u32[]{:S(2)}, u32[]{:S(2)}) collective-permute-start(bf16[128,2048]{1,0:T(8,128)(2,1)S(1)} %collective-permute-done.12.refs_2_), channel_id=1, source_target_pairs={{0,1},{1,0},{2,3},{3,2},{4,5},{5,4},{6,7},{7,6},{8,9},{9,8},{10,11... | collective-permute-start | bytes 1572872 | tf_op jit(solution)/shard_map/ppermute | solution.py:234
  40.5 23.8 %collective-permute-start.14 = (bf16[128,2048]{1,0:T(8,128)(2,1)S(1)}, bf16[128,2048]{1,0:T(8,128)(2,1)}, u32[]{:S(2)}, u32[]{:S(2)}) collective-permute-start(bf16[128,2048]{1,0:T(8,128)(2,1)S(1)} %collective-permute-done.12.refs_2_), channel_id=1, source_target_pairs={{0,2},{1,3},{2,0},{3,1},{4,6},{5,7},{6,4},{7,5},{8,10},{9,11},{10,... | collective-permute-start | bytes 1572872 | tf_op jit(solution)/shard_map/ppermute | solution.py:234
  42.7 21.7 %collective-permute-start.13 = (bf16[128,2048]{1,0:T(8,128)(2,1)S(1)}, bf16[128,2048]{1,0:T(8,128)(2,1)S(1)}, u32[]{:S(2)}, u32[]{:S(2)}) collective-permute-start(bf16[128,2048]{1,0:T(8,128)(2,1)S(1)} %collective-permute-done.1.refs_2_), channel_id=1, source_target_pairs={{0,12},{1,13},{2,14},{3,15},{4,0},{5,1},{6,2},{7,3},{8,4},{9,5},{1... | collective-permute-start | bytes 1572872 | tf_op jit(solution)/shard_map/ppermute | solution.py:234
  52.2 13.8 %collective-permute-start.17 = (bf16[128,2048]{1,0:T(8,128)(2,1)S(1)}, bf16[128,2048]{1,0:T(8,128)(2,1)}, u32[]{:S(2)}, u32[]{:S(2)}) collective-permute-start(bf16[128,2048]{1,0:T(8,128)(2,1)S(1)} %collective-permute-done.1.refs_2_), channel_id=1, source_target_pairs={{0,1},{1,0},{2,3},{3,2},{4,5},{5,4},{6,7},{7,6},{8,9},{9,8},{10,11... | collective-permute-start | bytes 1572872 | tf_op jit(solution)/shard_map/ppermute | solution.py:234
  53.8 15.4 %collective-permute-start.25 = (bf16[128,2048]{1,0:T(8,128)(2,1)}, bf16[128,2048]{1,0:T(8,128)(2,1)}, u32[]{:S(2)}, u32[]{:S(2)}) collective-permute-start(bf16[128,2048]{1,0:T(8,128)(2,1)} %collective-permute-done.3.refs_6_), channel_id=1, source_target_pairs={{0,1},{1,0},{2,3},{3,2},{4,5},{5,4},{6,7},{7,6},{8,9},{9,8},{10,11... | collective-permute-start | bytes 1572872 | tf_op jit(solution)/shard_map/ppermute | solution.py:234
  54.6 19.7 %collective-permute-start.6 = (bf16[128,2048]{1,0:T(8,128)(2,1)}, bf16[128,2048]{1,0:T(8,128)(2,1)}, u32[]{:S(2)}, u32[]{:S(2)}) collective-permute-start(bf16[128,2048]{1,0:T(8,128)(2,1)} %collective-permute-done.3.refs_6_), channel_id=1, source_target_pairs={{0,2},{1,3},{2,0},{3,1},{4,6},{5,7},{6,4},{7,5},{8,10},{9,11},{10,... | collective-permute-start | bytes 1572872 | tf_op jit(solution)/shard_map/ppermute | solution.py:234
  64.3 11.5 %collective-permute-start.22 = (bf16[128,2048]{1,0:T(8,128)(2,1)}, bf16[128,2048]{1,0:T(8,128)(2,1)}, u32[]{:S(2)}, u32[]{:S(2)}) collective-permute-start(bf16[128,2048]{1,0:T(8,128)(2,1)} %collective-permute-done.14.refs_2_), channel_id=1, source_target_pairs={{0,1},{1,0},{2,3},{3,2},{4,5},{5,4},{6,7},{7,6},{8,9},{9,8},{10,11... | collective-permute-start | bytes 1572872 | tf_op jit(solution)/shard_map/ppermute | solution.py:234
  64.3 17.1 %collective-permute-start.5 = (bf16[128,2048]{1,0:T(8,128)(2,1)}, bf16[128,2048]{1,0:T(8,128)(2,1)}, u32[]{:S(2)}, u32[]{:S(2)}) collective-permute-start(bf16[128,2048]{1,0:T(8,128)(2,1)} %collective-permute-done.3.refs_6_), channel_id=1, source_target_pairs={{0,4},{1,5},{2,6},{3,7},{4,8},{5,9},{6,10},{7,11},{8,12},{9,13},{1... | collective-permute-start | bytes 1572872 | tf_op jit(solution)/shard_map/ppermute | solution.py:234
  66.1 44.6 %collective-permute-start.18 = (bf16[128,2048]{1,0:T(8,128)(2,1)}, bf16[128,2048]{1,0:T(8,128)(2,1)S(1)}, u32[]{:S(2)}, u32[]{:S(2)}) collective-permute-start(bf16[128,2048]{1,0:T(8,128)(2,1)} %copy-done.9), channel_id=1, source_target_pairs={{0,12},{1,13},{2,14},{3,15},{4,0},{5,1},{6,2},{7,3},{8,4},{9,5},{1... | collective-permute-start | bytes 1572872 | tf_op jit(solution)/shard_map/ppermute | solution.py:234
  69.2 28.6 %collective-permute-start.20 = (bf16[128,2048]{1,0:T(8,128)(2,1)}, bf16[128,2048]{1,0:T(8,128)(2,1)S(1)}, u32[]{:S(2)}, u32[]{:S(2)}) collective-permute-start(bf16[128,2048]{1,0:T(8,128)(2,1)} %copy-done.15), channel_id=1, source_target_pairs={{0,1},{1,0},{2,3},{3,2},{4,5},{5,4},{6,7},{7,6},{8,9},{9,8},{10,11... | collective-permute-start | bytes 1572872 | tf_op jit(solution)/shard_map/ppermute | solution.py:234
  74.3 44.1 %collective-permute-start.15 = (bf16[128,2048]{1,0:T(8,128)(2,1)}, bf16[128,2048]{1,0:T(8,128)(2,1)S(1)}, u32[]{:S(2)}, u32[]{:S(2)}) collective-permute-start(bf16[128,2048]{1,0:T(8,128)(2,1)} %copy-done.15), channel_id=1, source_target_pairs={{0,2},{1,3},{2,0},{3,1},{4,6},{5,7},{6,4},{7,5},{8,10},{9,11},{10,... | collective-permute-start | bytes 1572872 | tf_op jit(solution)/shard_map/ppermute | solution.py:234
  75.8 56.6 %collective-permute-start.23 = (bf16[128,2048]{1,0:T(8,128)(2,1)}, bf16[128,2048]{1,0:T(8,128)(2,1)S(1)}, u32[]{:S(2)}, u32[]{:S(2)}) collective-permute-start(bf16[128,2048]{1,0:T(8,128)(2,1)} %collective-permute-done.6.refs_6_), channel_id=1, source_target_pairs={{0,1},{1,0},{2,3},{3,2},{4,5},{5,4},{6,7},{7,6},{8,9},{9,8},{10,11... | collective-permute-start | bytes 1572872 | tf_op jit(solution)/shard_map/ppermute | solution.py:234
  81.4 51.1 %collective-permute-start.21 = (bf16[128,2048]{1,0:T(8,128)(2,1)}, bf16[128,2048]{1,0:T(8,128)(2,1)S(1)}, u32[]{:S(2)}, u32[]{:S(2)}) collective-permute-start(bf16[128,2048]{1,0:T(8,128)(2,1)} %collective-permute-done.5.refs_6_), channel_id=1, source_target_pairs={{0,1},{1,0},{2,3},{3,2},{4,5},{5,4},{6,7},{7,6},{8,9},{9,8},{10,11... | collective-permute-start | bytes 1572872 | tf_op jit(solution)/shard_map/ppermute | solution.py:234
  97.7 43.8 %collective-permute-start.7 = (bf16[128,2048]{1,0:T(8,128)(2,1)S(1)}, bf16[128,2048]{1,0:T(8,128)(2,1)S(1)}, u32[]{:S(2)}, u32[]{:S(2)}) collective-permute-start(bf16[128,2048]{1,0:T(8,128)(2,1)S(1)} %copy-done.6), channel_id=1, source_target_pairs={{0,12},{1,13},{2,14},{3,15},{4,0},{5,1},{6,2},{7,3},{8,4},{9,5},{1... | collective-permute-start | bytes 1572872 | tf_op jit(solution)/shard_map/ppermute | solution.py:234
  110.7 31.0 %collective-permute-start.9 = (bf16[128,2048]{1,0:T(8,128)(2,1)}, bf16[128,2048]{1,0:T(8,128)(2,1)S(1)}, u32[]{:S(2)}, u32[]{:S(2)}) collective-permute-start(bf16[128,2048]{1,0:T(8,128)(2,1)} %collective-permute-done.5.refs_6_), channel_id=1, source_target_pairs={{0,2},{1,3},{2,0},{3,1},{4,6},{5,7},{6,4},{7,5},{8,10},{9,11},{10,... | collective-permute-start | bytes 1572872 | tf_op jit(solution)/shard_map/ppermute | solution.py:234
  118.3 32.1 %collective-permute-start.19 = (bf16[128,2048]{1,0:T(8,128)(2,1)S(1)}, bf16[128,2048]{1,0:T(8,128)(2,1)S(1)}, u32[]{:S(2)}, u32[]{:S(2)}) collective-permute-start(bf16[128,2048]{1,0:T(8,128)(2,1)S(1)} %collective-permute-done.18.refs_6_), channel_id=1, source_target_pairs={{0,1},{1,0},{2,3},{3,2},{4,5},{5,4},{6,7},{7,6},{8,9},{9,8},{10,11... | collective-permute-start | bytes 1572872 | tf_op jit(solution)/shard_map/ppermute | solution.py:234
  132.4 31.5 %collective-permute-start.11 = (bf16[128,2048]{1,0:T(8,128)(2,1)S(1)}, bf16[128,2048]{1,0:T(8,128)(2,1)S(1)}, u32[]{:S(2)}, u32[]{:S(2)}) collective-permute-start(bf16[128,2048]{1,0:T(8,128)(2,1)S(1)} %copy-done.8), channel_id=1, source_target_pairs={{0,1},{1,0},{2,3},{3,2},{4,5},{5,4},{6,7},{7,6},{8,9},{9,8},{10,11... | collective-permute-start | bytes 1572872 | tf_op jit(solution)/shard_map/ppermute | solution.py:234
  132.5 31.4 %collective-permute-start.16 = (bf16[128,2048]{1,0:T(8,128)(2,1)S(1)}, bf16[128,2048]{1,0:T(8,128)(2,1)S(1)}, u32[]{:S(2)}, u32[]{:S(2)}) collective-permute-start(bf16[128,2048]{1,0:T(8,128)(2,1)S(1)} %collective-permute-done.15.refs_3_), channel_id=1, source_target_pairs={{0,1},{1,0},{2,3},{3,2},{4,5},{5,4},{6,7},{7,6},{8,9},{9,8},{10,11... | collective-permute-start | bytes 1572872 | tf_op jit(solution)/shard_map/ppermute | solution.py:234
  141.5 27.6 %collective-permute-start.8 = (bf16[128,2048]{1,0:T(8,128)(2,1)S(1)}, bf16[128,2048]{1,0:T(8,128)(2,1)S(1)}, u32[]{:S(2)}, u32[]{:S(2)}) collective-permute-start(bf16[128,2048]{1,0:T(8,128)(2,1)S(1)} %collective-permute-done.7.refs_2_), channel_id=1, source_target_pairs={{0,1},{1,0},{2,3},{3,2},{4,5},{5,4},{6,7},{7,6},{8,9},{9,8},{10,11... | collective-permute-start | bytes 1572872 | tf_op jit(solution)/shard_map/ppermute | solution.py:234
  141.7 27.4 %collective-permute-start.10 = (bf16[128,2048]{1,0:T(8,128)(2,1)S(1)}, bf16[128,2048]{1,0:T(8,128)(2,1)S(1)}, u32[]{:S(2)}, u32[]{:S(2)}) collective-permute-start(bf16[128,2048]{1,0:T(8,128)(2,1)S(1)} %collective-permute-done.9.refs_3_), channel_id=1, source_target_pairs={{0,1},{1,0},{2,3},{3,2},{4,5},{5,4},{6,7},{7,6},{8,9},{9,8},{10,11... | collective-permute-start | bytes 1572872 | tf_op jit(solution)/shard_map/ppermute | solution.py:234
  (30 other events, 227.7 us)

commit v2 on v0

v2 whole, which is shorter than its diff:
```python
import functools

import jax
import jax.numpy as jnp
from jax import lax
from jax.experimental import pallas as pl
from jax.experimental.pallas import tpu as pltpu
from jax.sharding import PartitionSpec as P

PROJ = 16
BLK = 128
SLOT = PROJ * PROJ
F32 = jnp.float32
BF16 = jnp.bfloat16
NT = (((1,), (1,)), ((), ()))
SMALL = pl.CostEstimate(flops=1, bytes_accessed=1, transcendentals=0)


def split3(x):
    one = x.astype(BF16)
    rest = x - one.astype(F32)
    two = rest.astype(BF16)
    three = (rest - two.astype(F32)).astype(BF16)
    return jnp.concatenate([one, two, three], axis=1)


def split3(x):
    one = x.astype(BF16)
    rest = x - one.astype(F32)
    two = rest.astype(BF16)
    three = (rest - two.astype(F32)).astype(BF16)
    return one, two, three


def precondition(x_refs, y_refs, high, low, skip):
    rows = x_refs[0].shape[0]
    for s in range(x_refs[0].shape[1] // SLOT):
        cols = slice(s * SLOT, (s + 1) * SLOT)
        x = jnp.concatenate([ref[:, cols] for ref in x_refs], axis=0)
        y = jnp.dot(x, high[skip + s], preferred_element_type=F32)
        y += jnp.dot(x, low[skip + s], preferred_element_type=F32)
        for i, ref in enumerate(y_refs):
            ref[:, cols] = y[i * rows : (i + 1) * rows].astype(BF16)


def prepare_kernel(
    layers, slot_ref, pair_ref, a_ref, b_ref, x0, x1, train, high_ref, low_ref, y0, y1, keep, away, table, xa, xb, sems
):
    me = lax.axis_index("rows")
    core = me & 1
    half = keep.shape[1]
    mine = pl.multiple_of(core * half, half)
    other = pl.multiple_of((1 - core) * half, half)
    loads = [
        pltpu.make_async_copy(train.at[:, pl.ds(other, half)], away, sems.at[0]),
        pltpu.make_async_copy(train.at[:, pl.ds(mine, half)], keep, sems.at[1]),
    ]
    for load in loads:
        load.start()
    row = lax.broadcasted_iota(jnp.int32, (PROJ, SLOT), 0)
    col = lax.broadcasted_iota(jnp.int32, (PROJ, SLOT), 1)
    pick_i = jnp.where(col // PROJ == row, 1.0, 0.0).astype(BF16)
    pick_o = jnp.where(col % PROJ == row, 1.0, 0.0).astype(BF16)
    total = 0.0
    for part in split3(b_ref[...]):
        total += jnp.dot(part, pick_o, preferred_element_type=F32)
    xb[...] = total
    for layer in range(layers):
        at = slice(layer * PROJ, (layer + 1) * PROJ)
        total = 0.0
        for part in split3(a_ref[at]):
            total += lax.dot_general(part, pick_i, (((0,), (0,)), ((), ())), preferred_element_type=F32)
        xa[at] = total

    @pl.loop(0, layers)
    def _(layer):
        slot = slot_ref[layer] - core * (layers // 2)

        @pl.when((slot >= 0) & (slot < layers // 2))
        def _():
            at = pl.multiple_of(layer * PROJ, PROJ)
            left = xa[pl.ds(at, PROJ), :]
            right = xb[pl.ds(at, PROJ), :]
            full = (left[:, None, :] * right[None, :, :]).reshape(SLOT, SLOT)
            high = full.astype(BF16)
            high_ref[slot] = high
            low_ref[slot] = (full - high.astype(F32)).astype(BF16)

    precondition([x0, x1], [y0, y1], high_ref, low_ref)
    blocks, slots = pair_ref.shape
    for t in range(blocks):
        for j in range(table.shape[1]):
            table[t, j] = -1
    for t in range(blocks):
        for k in range(slots):
            q = pair_ref[t, k]
            table[t, (((q >> 2) - (me >> 2)) & 3) * 4 + ((q ^ me) & 3)] = k
    for load in loads:
        load.wait()


def prepare(layer_slot, pair_query, in_factor, out_factor, x0, x1, train, jobs):
    layers = in_factor.shape[0]
    a_rows = in_factor.reshape(layers * PROJ, PROJ)
    b_rows = out_factor.reshape(layers * PROJ, PROJ)
    vmem = pl.BlockSpec(memory_space=pltpu.VMEM)
    smem = pl.BlockSpec(memory_space=pltpu.SMEM)
    side = jax.ShapeDtypeStruct((train.shape[0], train.shape[1] // 2), BF16)
    factor = jax.ShapeDtypeStruct((layers // 2, SLOT, SLOT), BF16)
    piece = jax.ShapeDtypeStruct(x0.shape, BF16)
    return pl.pallas_call(
        functools.partial(prepare_kernel, layers),
        out_shape=[factor, factor, piece, piece, side, side, jax.ShapeDtypeStruct((pair_query.shape[0], jobs), jnp.int32)],
        in_specs=[smem] * 2 + [vmem] * 4 + [pl.BlockSpec(memory_space=pl.ANY)],
        out_specs=[vmem] * 6 + [smem],
        scratch_shapes=[
            pltpu.VMEM((layers * PROJ, SLOT), F32),
            pltpu.VMEM((layers * PROJ, SLOT), F32),
            pltpu.SemaphoreType.DMA((2,)),
        ],
        compiler_params=pltpu.CompilerParams(vmem_limit_bytes=40 << 20),
        cost_estimate=SMALL,
        name="prepare",
    )(layer_slot, pair_query, a_rows, b_rows, x0, x1, train)


def precondition(x_refs, y_refs, high, low):
    rows = x_refs[0].shape[0]
    for s in range(x_refs[0].shape[1] // SLOT):
        cols = slice(s * SLOT, (s + 1) * SLOT)
        x = jnp.concatenate([ref[:, cols] for ref in x_refs], axis=0)
        y = jnp.dot(x, high[s], preferred_element_type=F32)
        y += jnp.dot(x, low[s], preferred_element_type=F32)
        for i, ref in enumerate(y_refs):
            ref[:, cols] = y[i * rows : (i + 1) * rows].astype(BF16)


def ready_kernel(x0, x1, high, low, y0, y1):
    precondition([x0, x1], [y0, y1], high, low)


def make_ready(x0, x1, high, low):
    return pl.pallas_call(
        ready_kernel,
        out_shape=[jax.ShapeDtypeStruct(x0.shape, BF16)] * 2,
        compiler_params=pltpu.CompilerParams(vmem_limit_bytes=10 << 20),
        cost_estimate=SMALL,
        name="ready",
    )(x0, x1, high, low)


def stage_kernel(adds, n_sums, n_train, n_pieces, aliased, *refs):
    refs = list(refs)
    table = refs.pop(0)
    sums = [refs.pop(0) for _ in range(n_sums)]
    trains = [refs.pop(0) for _ in range(n_train)]
    pieces = [refs.pop(0) for _ in range(n_pieces)]
    if aliased:
        refs.pop(0)
    token = refs.pop(0)
    out = refs.pop(0) if adds else None
    parts = [refs.pop(0) for _ in range(n_train)]
    token[...] = jnp.zeros_like(token)
    puts = []
    if adds:
        s_v, sems = refs
        for i, (job, ours, j, theirs, k) in enumerate(adds):
            for t in range(table.shape[0]):
                slot = table[t, job]
                copy = pltpu.make_async_copy(s_v.at[t, i], out.at[t, jnp.maximum(slot, 0)], sems.at[t, i])
                puts.append((slot >= 0, copy))
                s_v[t, i] = sums[ours][t, j] + sums[theirs][t, k]

                @pl.when(slot >= 0)
                def _(copy=copy):
                    copy.start()

    step = 2 * BLK
    for train, part in zip(trains, parts):
        for m in range(train.shape[0] // step):
            for h in range(0, n_pieces, 2):
                q = jnp.concatenate([ref[...] for ref in pieces[h : h + 2]], axis=0)
                s = lax.dot_general(train[m * step : (m + 1) * step], q, NT, preferred_element_type=F32)
                for u in range(step // BLK):
                    for j in range(2):
                        part[m * (step // BLK) + u, h + j] = s[u * BLK : (u + 1) * BLK, j * BLK : (j + 1) * BLK]

    for named, copy in puts:

        @pl.when(named)
        def _(copy=copy):
            copy.wait()


def stage(table, adds, trains, pieces, out, slots, cost=0):
    any_spec = pl.BlockSpec(memory_space=pl.ANY)
    vmem = pl.BlockSpec(memory_space=pltpu.VMEM)
    sums, spots = [], []
    for job, *pair in adds:
        spot = [job]
        for array, column in pair:
            at = next((i for i, other in enumerate(sums) if other is array), len(sums))
            if at == len(sums):
                sums.append(array)
            spot += [at, column]
        spots.append(tuple(spot))
    args = [table, *sums, *trains, *pieces]
    specs = [pl.BlockSpec(memory_space=pltpu.SMEM)] + [vmem] * (len(args) - 1)
    aliases = {}
    if adds and out is not None:
        aliases = {len(args): 1}
        args.append(out)
        specs.append(any_spec)
    blocks = table.shape[0]
    shapes, out_specs, scratch = [jax.ShapeDtypeStruct((8, 128), F32)], [vmem], []
    if adds:
        shapes.append(jax.ShapeDtypeStruct((blocks, slots, BLK, BLK), F32))
        out_specs.append(any_spec)
        scratch = [pltpu.VMEM((blocks, len(adds), BLK, BLK), F32), pltpu.SemaphoreType.DMA((blocks, len(adds)))]
    for _ in trains:
        shapes.append(jax.ShapeDtypeStruct((blocks, len(pieces), BLK, BLK), F32))
        out_specs.append(vmem)
    body = functools.partial(stage_kernel, tuple(spots), len(sums), len(trains), len(pieces), bool(aliases))
    token, *rest = pl.pallas_call(
        body,
        out_shape=shapes,
        in_specs=specs,
        out_specs=out_specs,
        scratch_shapes=scratch,
        input_output_aliases=aliases,
        compiler_params=pltpu.CompilerParams(vmem_limit_bytes=20 << 20),
        cost_estimate=pl.CostEstimate(flops=cost * 10**9, bytes_accessed=1, transcendentals=0),
        name="stage",
    )(*args)
    if adds:
        out = rest.pop(0)
    return token, out, rest


def after(x, *deps):
    return lax.optimization_barrier((x, *deps))[0]


def local_rings(train_grads, query_grads, pair_query, layer_slot, in_factor, out_factor):
    count = lax.axis_size("rows")
    height = count // 4

    def index(z, y, c):
        return (z % height * 2 + y) * 2 + c

    def ring(move):
        return [(i, index(*move(i // 4, i // 2 % 2, i % 2))) for i in range(count)]

    down = ring(lambda z, y, c: (z - 1, y, c))
    up = ring(lambda z, y, c: (z + 1, y, c))
    across = ring(lambda z, y, c: (z, 1 - y, c))
    twin = ring(lambda z, y, c: (z, y, 1 - c))

    def send(x, perm, name):
        with jax.named_scope("send_" + name):
            return lax.ppermute(x, "rows", perm)

    job = {}
    for letter, dz, dy in (("h", 0, 0), ("y", 0, 1), ("a", 1, 0), ("ya", 1, 1), ("f", 2, 0), ("yf", 2, 1), ("b", 3, 0), ("yb", 3, 1)):
        for dc in (0, 1):
            job[letter + str(dc)] = (dz * 2 + dy) * 2 + dc
    job["xa1"] = job.pop("ya1")
    other_name = {n: ("xa1" if n == "ya0" else "ya0" if n == "xa1" else n[:-1] + "10"[int(n[-1])]) for n in job}
    plan = [
        (("a0", "h0", down), ("y0", "h0", across)),
        (("b0", "h0", up), ("y1", "h1", across)),
        (("b1", "h1", up), ("ya0", "a0", across)),
        (("f0", "a0", down), ("yb0", "b0", across)),
        (("f1", "b1", up), ("yb1", "b1", across)),
        (("a1", "h1", down), ("yf0", "f0", across)),
        (("xa1", "y1", down), ("yf1", "f1", across)),
    ]
    work = {4: ["h0", "h1", "a0", "y0"], 5: ["b0", "y1", "b1", "ya0"], 6: ["f0", "yb0", "f1", "yb1"], 7: ["a1", "yf0"]}
    adding = {4: 6, 5: 7, 6: 8, 7: 8}
    cost = {4: 1, 5: 1, 6: 1, 7: 8}
    slots = pair_query.shape[1]
    half = query_grads.shape[1] // 2
    core = lax.axis_index("rows") % 2
    low_half, high_half = query_grads[:, :half], query_grads[:, half:]
    raw = {"h0": jnp.where(core == 0, low_half, high_half)}
    raw["h1"] = send(jnp.where(core == 0, high_half, low_half), twin, "h1")
    for step in plan[:2]:
        for name, source, perm in step:
            raw[name] = send(raw[source], perm, name)
    high, low, own0, own1, keep, away, table = prepare(
        layer_slot, pair_query, in_factor, out_factor, raw["h0"], raw["h1"], train_grads, 2 * 8
    )
    got = {"h0": own0, "h1": own1}
    trains = (keep, send(away, twin, "train"))
    ours, theirs, open_jobs = {}, {}, list(other_name)
    out, tokens = None, []

    def ready_adds():
        done = [n for n in open_jobs if n in ours and other_name[n] in theirs]
        for n in done:
            open_jobs.remove(n)
        return [(job[n], ours[n], theirs[other_name[n]]) for n in done]

    arriving = {}
    for s in range(2, len(plan) + 1):
        names = [name for name, _, _ in plan[s - 2]]
        if s < 4:
            got[names[0]], got[names[1]] = make_ready(raw[names[0]], raw[names[1]], high, low)
        past = [got[name] for name in names] + tokens
        if s < len(plan):
            for name, source, perm in plan[s]:
                deps = [v for v in past if v is not got[source]]
                got[name] = send(after(got[source], *deps), perm, name)
        if s not in work:
            continue
        for part in arriving.pop(s, []):
            theirs.update(part)
        pieces = [got[n] for n in work[s]]
        pieces[0] = after(pieces[0], *[got[name] for name in names if name not in work[s][:1]])
        token, out, (mine, away) = stage(table, ready_adds(), trains, pieces, out, slots, cost[s])
        tokens = [token]
        away = send(away, twin, "part" + str(s))
        ours.update({n: (mine, i) for i, n in enumerate(work[s])})
        arriving.setdefault(adding[s], []).append({n: (away, i) for i, n in enumerate(work[s])})
    names = [name for name, _, _ in plan[-1]]
    pieces = [after(got[names[0]], *tokens), got[names[1]]]
    _, _, (away,) = stage(table, [], trains[1:], pieces, out, slots)
    away = send(away, twin, "part")
    for part in arriving.pop(8, []):
        theirs.update(part)
    _, out, (mine,) = stage(table, ready_adds(), trains[:1], pieces, out, slots)
    ours.update({n: (mine, i) for i, n in enumerate(names)})
    theirs.update({n: (away, i) for i, n in enumerate(names)})
    _, out, _ = stage(table, ready_adds(), [], [], out, slots)
    return out


def local(train_grads, query_grads, pair_query, layer_slot, in_factor, out_factor):
    dims_count = lax.axis_size("dims")
    dims_index = lax.axis_index("dims")
    width = query_grads.shape[1]
    local_layers = width // SLOT
    slots = dims_index * local_layers + jnp.arange(local_layers, dtype=jnp.int32)
    onehot = (slots[:, None] == layer_slot[None, :]).astype(F32)
    a_fac = jnp.einsum("sl,lij->sij", onehot, in_factor, precision=lax.Precision.HIGHEST)
    b_fac = jnp.einsum("sl,lij->sij", onehot, out_factor, precision=lax.Precision.HIGHEST)
    nrow = query_grads.shape[0]
    query = query_grads.astype(F32).reshape(nrow, local_layers, PROJ, PROJ)
    left = jnp.einsum("sia,rsab->rsib", a_fac, query, precision=lax.Precision.HIGHEST)
    both = jnp.einsum("rsib,sbo->rsio", left, b_fac, precision=lax.Precision.HIGHEST)
    precond = both.reshape(nrow, width).astype(BF16)
    gathered = lax.all_gather(precond, "rows", axis=0, tiled=True)
    qblocks = gathered.reshape(gathered.shape[0] // BLK, BLK, width)
    tblocks = train_grads.reshape(train_grads.shape[0] // BLK, BLK, width)

    def one_block(items):
        tblock, ids = items
        chosen = qblocks[ids]
        return jnp.einsum("rg,kqg->krq", tblock, chosen, preferred_element_type=F32)

    partial_scores = lax.map(one_block, (tblocks, pair_query))
    summed = lax.psum(partial_scores, "dims")
    share = BLK // dims_count
    return lax.dynamic_slice_in_dim(summed, dims_index * share, share, 2)


def solution(mesh):
    in_specs = (
        P(("shard", "rows"), "dims"),
        P(("shard", "rows"), "dims"),
        P(("shard", "rows"), None),
        P(),
        P(),
        P(),
    )
    out_specs = P(("shard", "rows"), None, "dims", None)
    four = mesh.shape["rows"] == 16 and mesh.shape["dims"] == 1
    body = local_rings if four else local
    return jax.shard_map(body, mesh=mesh, in_specs=in_specs, out_specs=out_specs, check_vma=False)
```

time: 322 us -> 117 us (0.36)
  local copies, waits for them, and re-layouts: 115 us -> 0.01 us
  waiting for transfers between devices: 133 us -> 57.4 us
  matrix products: 53.7 us -> 0 us
  Pallas kernels: 0 us -> 37.4 us
  starting transfers between devices: 0.01 us -> 20.2 us
  between operations: 13.4 us -> 0.27 us
  other arithmetic: 5.61 us -> 1.31 us
    all_gather x1 -> x0, waiting for transfers between devices: 133 us -> none  [local(): gathered = lax.all_gather(precond, 'rows', axis=0, tiled=True)]
    gather x8 -> x0, local copies, waits for them, and re-layouts: 83.5 us -> none  [one_block(): chosen = qblocks[ids]]
    ppermute x0 -> x21, waiting for transfers between devices: none -> 57.4 us  [send(): return lax.ppermute(x, 'rows', perm)]
    dot_general x12 -> x0, matrix products: 53.7 us -> none  [the longest x8 47.5 us: one_block(): jnp.einsum('rg,kqg->krq', tblock, chosen, preferred_element_type=jnp.floa...]
    pallas_call x0 -> x10, Pallas kernels: none -> 37.4 us  [the longest x7 31.1 us: stage(): pl.pallas_call(body, out_shape=shapes, in_specs=specs, out_specs=out_spec...]
    all_gather x1 -> x0, local copies, waits for them, and re-layouts: 21.4 us -> none  [local(): gathered = lax.all_gather(precond, 'rows', axis=0, tiled=True)]
    ppermute x0 -> x21, starting transfers between devices: none -> 20.2 us  [send(): return lax.ppermute(x, 'rows', perm)]
    dynamic_update_slice x16 -> x0, local copies, waits for them, and re-layouts: 8.27 us -> none  [local(): partial_scores = lax.map(one_block, (tblocks, pair_query))]
  transfers between devices with their start and end apart: 1 -> 21, of which waited for: 1 -> 13; matrix products, arithmetic and copies ran while one was open for 0% -> 0% of each run, Pallas kernels for 0% -> 26%
where the time goes in v2:
time: 117 us
  waiting for transfers between devices  57.4 us (49%)
  Pallas kernels  37.4 us (32%)
  starting transfers between devices  20.2 us (17%)
  other arithmetic  1.31 us (1%)
    ppermute x21, waiting for transfers between devices, send(): return lax.ppermute(x, 'rows', perm)  57.4 us
    pallas_call x7, Pallas kernels, stage(): pl.pallas_call(body, out_shape=shapes, in_specs=specs, out_specs=out_spec...  31.1 us
    ppermute x21, starting transfers between devices, send(): return lax.ppermute(x, 'rows', perm)  20.2 us
    pallas_call x1, Pallas kernels, prepare(): pl.pallas_call(functools.partial(prepare_kernel, layers), out_shape=[fact...  4.92 us
  transfers between devices with their start and end apart: 21, of which 13 were waited for; matrix products, arithmetic and copies ran while one was open for 0% of the time, Pallas kernels for 26%

profile of v2, /device:TPU:0, one launch (start us, length us, event | category | flops | bytes accessed | tf_op | source)
XLA Modules:
  0.0 116.6 jit_solution(2558920001003306455)
XLA Ops:
  0.0 1.3 %broadcast_select_fusion = (bf16[128,2048]{1,0:T(8,128)(2,1)S(1)}, bf16[128,2048]{1,0:T(8,128)(2,1)S(1)}) fusion(pred[]{:T(512)S(6)} %eq.6, bf16[128,4096]{1,0:T(8,128)(2,1)} %param.7), kind=kLoop, calls=%fused_computation | loop fusion | flops 524288 | bytes 2097153 | tf_op jit(solution)/shard_map/jit(_where)/select_n | solution.py:286
  1.9 1.5 %collective-permute-done.x1 = bf16[128,2048]{1,0:T(8,128)(2,1)S(1)} collective-permute-done((bf16[128,2048]{1,0:T(8,128)(2,1)S(1)}, bf16[128,2048]{1,0:T(8,128)(2,1)S(1)}, u32[]{:S(2)}, u32[]{:S(2)}) %collective-permute-start) | collective-permute-done | bytes 524320 | tf_op jit(solution)/shard_map/send_h1/ppermute | solution.py:261
  3.4 4.9 %prepare.1 = (bf16[8,256,256]{2,1,0:T(8,128)(2,1)S(1)}, bf16[8,256,256]{2,1,0:T(8,128)(2,1)S(1)}, bf16[128,2048]{1,0:T(8,128)(2,1)S(1)}, bf16[128,2048]{1,0:T(8,...) custom-call(s32[16]{0:T(128)S(1)} %copy-done.3, ...), custom_call_target="tpu_custom_call" | custom-call | flops 1 | bytes 1 | tf_op jit(solution)/shard_map/prepare/pallas_call | solution.py:111
  8.8 4.7 %collective-permute-start.4 = (bf16[128,2048]{1,0:T(8,128)(2,1)S(1)}, bf16[128,2048]{1,0:T(8,128)(2,1)S(1)}, u32[]{:S(2)}, u32[]{:S(2)}) collective-permute-start(bf16[128,2048]{1,0:T(8,128)(2,1)S(1)} %get-tuple-element.84.x0), channel_id=1, source_target_pairs={{0,12},{1,13},{2,14},{3,15},{4,0},{5,1},{6,2},{7,3},{8,4},{9,5},{1... | collective-permute-start | bytes 1572872 | tf_op jit(solution)/shard_map/send_a0/ppermute | solution.py:261
  13.5 1.5 %collective-permute-start.5 = (bf16[128,2048]{1,0:T(8,128)(2,1)S(1)}, bf16[128,2048]{1,0:T(8,128)(2,1)S(1)}, u32[]{:S(2)}, u32[]{:S(2)}) collective-permute-start(bf16[128,2048]{1,0:T(8,128)(2,1)S(1)} %get-tuple-element.84.x0), channel_id=1, source_target_pairs={{0,2},{1,3},{2,0},{3,1},{4,6},{5,7},{6,4},{7,5},{8,10},{9,11},{10,... | collective-permute-start | bytes 1572872 | tf_op jit(solution)/shard_map/send_y0/ppermute | solution.py:261
  15.6 10.3 %collective-permute-done.4.x0 = bf16[128,2048]{1,0:T(8,128)(2,1)S(1)} collective-permute-done((bf16[128,2048]{1,0:T(8,128)(2,1)S(1)}, bf16[128,2048]{1,0:T(8,128)(2,1)S(1)}, u32[]{:S(2)}, u32[]{:S(2)}) %collective-permute-start.4) | collective-permute-done | bytes 524320 | tf_op jit(solution)/shard_map/send_a0/ppermute | solution.py:261
  25.8 2.5 %collective-permute-done.5.x1 = bf16[128,2048]{1,0:T(8,128)(2,1)S(1)} collective-permute-done((bf16[128,2048]{1,0:T(8,128)(2,1)S(1)}, bf16[128,2048]{1,0:T(8,128)(2,1)S(1)}, u32[]{:S(2)}, u32[]{:S(2)}) %collective-permute-start.5) | collective-permute-done | bytes 524320 | tf_op jit(solution)/shard_map/send_y0/ppermute | solution.py:261
  28.3 0.7 ready.3
  29.1 1.6 %collective-permute-start.9 = (bf16[128,2048]{1,0:T(8,128)(2,1)S(1)}, bf16[128,2048]{1,0:T(8,128)(2,1)S(1)}, u32[]{:S(2)}, u32[]{:S(2)}) collective-permute-start(bf16[128,2048]{1,0:T(8,128)(2,1)S(1)} %get-tuple-element.53.refs_5_), channel_id=1, source_target_pairs={{0,2},{1,3},{2,0},{3,1},{4,6},{5,7},{6,4},{7,5},{8,10},{9,11},{10,... | collective-permute-start | bytes 1572872 | tf_op jit(solution)/shard_map/send_ya0/ppermute | solution.py:261
  30.7 7.2 %collective-permute-done.2.x0 = bf16[128,2048]{1,0:T(8,128)(2,1)S(1)} collective-permute-done((bf16[128,2048]{1,0:T(8,128)(2,1)S(1)}, bf16[128,2048]{1,0:T(8,128)(2,1)S(1)}, u32[]{:S(2)}, u32[]{:S(2)}) %collective-permute-start.2) | collective-permute-done | bytes 524320 | tf_op jit(solution)/shard_map/send_b0/ppermute | solution.py:261
  37.9 1.6 %collective-permute-done.3.x1 = bf16[128,2048]{1,0:T(8,128)(2,1)S(1)} collective-permute-done((bf16[128,2048]{1,0:T(8,128)(2,1)S(1)}, bf16[128,2048]{1,0:T(8,128)(2,1)S(1)}, u32[]{:S(2)}, u32[]{:S(2)}) %collective-permute-start.3) | collective-permute-done | bytes 524320 | tf_op jit(solution)/shard_map/send_y1/ppermute | solution.py:261
  39.6 0.7 ready.2
  40.3 1.4 %collective-permute-start.6 = (bf16[128,2048]{1,0:T(8,128)(2,1)S(1)}, bf16[128,2048]{1,0:T(8,128)(2,1)S(1)}, u32[]{:S(2)}, u32[]{:S(2)}) collective-permute-start(bf16[128,2048]{1,0:T(8,128)(2,1)S(1)} %get-tuple-element.53.refs_5_), channel_id=1, source_target_pairs={{0,12},{1,13},{2,14},{3,15},{4,0},{5,1},{6,2},{7,3},{8,4},{9,5},{1... | collective-permute-start | bytes 1572872 | tf_op jit(solution)/shard_map/send_f0/ppermute | solution.py:261
  41.7 1.1 collective-permute-start.7
  42.9 6.4 %collective-permute-done.8.refs_5_ = bf16[128,2048]{1,0:T(8,128)(2,1)S(1)} collective-permute-done((bf16[128,2048]{1,0:T(8,128)(2,1)S(1)}, bf16[128,2048]{1,0:T(8,128)(2,1)S(1)}, u32[]{:S(2)}, u32[]{:S(2)}) %collective-permute-start.8) | collective-permute-done | bytes 524320 | tf_op jit(solution)/shard_map/send_b1/ppermute | solution.py:261
  49.2 1.6 %collective-permute-done.9.refs_6_ = bf16[128,2048]{1,0:T(8,128)(2,1)S(1)} collective-permute-done((bf16[128,2048]{1,0:T(8,128)(2,1)S(1)}, bf16[128,2048]{1,0:T(8,128)(2,1)S(1)}, u32[]{:S(2)}, u32[]{:S(2)}) %collective-permute-start.9) | collective-permute-done | bytes 524320 | tf_op jit(solution)/shard_map/send_ya0/ppermute | solution.py:261
  50.8 5.6 %stage.9 = (f32[8,128]{1,0:T(8,128)}, f32[8,4,128,128]{3,2,1,0:T(8,128)S(1)}, f32[8,4,128,128]{3,2,1,0:T(8,128)S(1)}) custom-call(s32[8,16]{1,0:T(8,128)S(1)} %get-tuple-element.45.refs_0_, bf16[1024,2048]{1,0:T(8,128)(2,1)S(1)} %get-tuple-element.46.refs_1_.refs_4_.refs_7_, bf16[1024,2048]{1,0:T(8,128)(2,1)S(1)} %collective-permute-done.1.refs_2_.refs_1_.refs_5_, ...), custom_call_target="tpu_custom_call" | custom-call | flops 1000000000 | bytes 1 | tf_op jit(solution)/shard_map/stage/pallas_call | solution.py:224
  56.4 3.5 %collective-permute-done.6.refs_6_ = bf16[128,2048]{1,0:T(8,128)(2,1)S(1)} collective-permute-done((bf16[128,2048]{1,0:T(8,128)(2,1)S(1)}, bf16[128,2048]{1,0:T(8,128)(2,1)S(1)}, u32[]{:S(2)}, u32[]{:S(2)}) %collective-permute-start.6) | collective-permute-done | bytes 524320 | tf_op jit(solution)/shard_map/send_f0/ppermute | solution.py:261
  59.9 1.3 %collective-permute-done.7.refs_7_ = bf16[128,2048]{1,0:T(8,128)(2,1)S(1)} collective-permute-done((bf16[128,2048]{1,0:T(8,128)(2,1)S(1)}, bf16[128,2048]{1,0:T(8,128)(2,1)S(1)}, u32[]{:S(2)}, u32[]{:S(2)}) %collective-permute-start.7) | collective-permute-done | bytes 524320 | tf_op jit(solution)/shard_map/send_yb0/ppermute | solution.py:261
  61.2 5.6 %stage.7 = (f32[8,128]{1,0:T(8,128)}, f32[8,4,128,128]{3,2,1,0:T(8,128)S(1)}, f32[8,4,128,128]{3,2,1,0:T(8,128)S(1)}) custom-call(s32[8,16]{1,0:T(8,128)S(1)} %get-tuple-element.45.refs_0_, bf16[1024,2048]{1,0:T(8,128)(2,1)S(1)} %get-tuple-element.46.refs_1_.refs_4_.refs_7_, bf16[1024,2048]{1,0:T(8,128)(2,1)S(1)} %collective-permute-done.1.refs_2_.refs_1_.refs_5_, ...), custom_call_target="tpu_custom_call" | custom-call | flops 1000000000 | bytes 1 | tf_op jit(solution)/shard_map/stage/pallas_call | solution.py:224
  66.7 1.5 %collective-permute-start.11 = (bf16[128,2048]{1,0:T(8,128)(2,1)S(1)}, bf16[128,2048]{1,0:T(8,128)(2,1)S(1)}, u32[]{:S(2)}, u32[]{:S(2)}) collective-permute-start(bf16[128,2048]{1,0:T(8,128)(2,1)S(1)} %collective-permute-done.8.refs_5_), channel_id=1, source_target_pairs={{0,2},{1,3},{2,0},{3,1},{4,6},{5,7},{6,4},{7,5},{8,10},{9,11},{10,... | collective-permute-start | bytes 1572872 | tf_op jit(solution)/shard_map/send_yb1/ppermute | solution.py:261
  68.8 14.1 %collective-permute-done.10.refs_8_ = bf16[128,2048]{1,0:T(8,128)(2,1)S(1)} collective-permute-done((bf16[128,2048]{1,0:T(8,128)(2,1)S(1)}, bf16[128,2048]{1,0:T(8,128)(2,1)S(1)}, u32[]{:S(2)}, u32[]{:S(2)}) %collective-permute-start.10) | collective-permute-done | bytes 524320 | tf_op jit(solution)/shard_map/send_f1/ppermute | solution.py:261
  83.2 6.7 %stage.10 = (f32[8,128]{1,0:T(8,128)}, f32[8,8,128,128]{3,2,1,0:T(8,128)}, f32[8,4,128,128]{3,2,1,0:T(8,128)S(1)}, f32[8,4,128,128]{3,2,1,0:T(8,128)S(1)}) custom-call(s32[8,16]{1,0:T(8,128)S(1)} %get-tuple-element.45.refs_0_, f32[8,4,128,128]{3,2,1,0:T(8,128)S(1)} %get-tuple-element.66.refs_1_, ...), custom_call_target="tpu_custom_call" | custom-call | flops 1000000000 | bytes 1 | tf_op jit(solution)/shard_map/stage/pallas_call | solution.py:224
  90.0 1.6 %collective-permute-start.13 = (bf16[128,2048]{1,0:T(8,128)(2,1)S(1)}, bf16[128,2048]{1,0:T(8,128)(2,1)S(1)}, u32[]{:S(2)}, u32[]{:S(2)}) collective-permute-start(bf16[128,2048]{1,0:T(8,128)(2,1)S(1)} %collective-permute-done.10.refs_8_), channel_id=1, source_target_pairs={{0,2},{1,3},{2,0},{3,1},{4,6},{5,7},{6,4},{7,5},{8,10},{9,11},{10,... | collective-permute-start | bytes 1572872 | tf_op jit(solution)/shard_map/send_yf1/ppermute | solution.py:261
  91.6 0.7 collective-permute-done.17.refs_7_
  92.3 4.1 %collective-permute-start.12 = (bf16[128,2048]{1,0:T(8,128)(2,1)S(1)}, bf16[128,2048]{1,0:T(8,128)(2,1)S(1)}, u32[]{:S(2)}, u32[]{:S(2)}) collective-permute-start(bf16[128,2048]{1,0:T(8,128)(2,1)S(1)} %get-tuple-element.61.refs_4_), channel_id=1, source_target_pairs={{0,12},{1,13},{2,14},{3,15},{4,0},{5,1},{6,2},{7,3},{8,4},{9,5},{1... | collective-permute-start | bytes 1572872 | tf_op jit(solution)/shard_map/send_xa1/ppermute | solution.py:261
  96.4 1.3 %collective-permute-done.16.refs_6_ = bf16[128,2048]{1,0:T(8,128)(2,1)S(1)} collective-permute-done((bf16[128,2048]{1,0:T(8,128)(2,1)S(1)}, bf16[128,2048]{1,0:T(8,128)(2,1)S(1)}, u32[]{:S(2)}, u32[]{:S(2)}) %collective-permute-start.16) | collective-permute-done | bytes 524320 | tf_op jit(solution)/shard_map/send_a1/ppermute | solution.py:261
  97.7 4.5 %stage.11 = (f32[8,128]{1,0:T(8,128)}, f32[8,8,128,128]{3,2,1,0:T(8,128)}, f32[8,2,128,128]{3,2,1,0:T(8,128)S(1)}, f32[8,2,128,128]{3,2,1,0:T(8,128)S(1)}) custom-call(s32[8,16]{1,0:T(8,128)S(1)} %get-tuple-element.45.refs_0_, f32[8,4,128,128]{3,2,1,0:T(8,128)S(1)} %get-tuple-element.66.refs_1_, ...), custom_call_target="tpu_custom_call", output_to_operand_aliasing={{1}: (8, {})} | custom-call | flops 8000000000 | bytes 1 | tf_op jit(solution)/shard_map/stage/pallas_call | solution.py:224
  102.3 5.4 %collective-permute-done.12.refs_2_.refs_8_ = bf16[128,2048]{1,0:T(8,128)(2,1)S(1)} collective-permute-done((bf16[128,2048]{1,0:T(8,128)(2,1)S(1)}, bf16[128,2048]{1,0:T(8,128)(2,1)S(1)}, u32[]{:S(2)}, u32[]{:S(2)}) %collective-permute-start.12) | collective-permute-done | bytes 524320 | tf_op jit(solution)/shard_map/send_xa1/ppermute | solution.py:261
  107.7 2.3 %stage.8 = (f32[8,128]{1,0:T(8,128)}, f32[8,2,128,128]{3,2,1,0:T(8,128)S(1)}) custom-call(s32[8,16]{1,0:T(8,128)S(1)} %get-tuple-element.45.refs_0_, bf16[1024,2048]{1,0:T(8,128)(2,1)S(1)} %collective-permute-done.1.refs_2_.refs_1_.refs_5_, bf16[128,2048]{1,0:T(8,128)(2,1)S(1)} %collective-permute-done.12.refs_2_.refs_8_, ...), custom_call_target="tpu_custom_call" | custom-call | bytes 1 | tf_op jit(solution)/shard_map/stage/pallas_call | solution.py:224
  110.0 3.9 %stage.12 = (f32[8,128]{1,0:T(8,128)}, f32[8,8,128,128]{3,2,1,0:T(8,128)}, f32[8,2,128,128]{3,2,1,0:T(8,128)S(1)}) custom-call(s32[8,16]{1,0:T(8,128)S(1)} %get-tuple-element.45.refs_0_, f32[8,4,128,128]{3,2,1,0:T(8,128)S(1)} %get-tuple-element.66.refs_1_, ...), custom_call_target="tpu_custom_call", output_to_operand_aliasing={{1}: (10, {})} | custom-call | bytes 1 | tf_op jit(solution)/shard_map/stage/pallas_call | solution.py:224
  113.9 2.5 %stage.13 = (f32[8,128]{1,0:T(8,128)}, f32[8,8,128,128]{3,2,1,0:T(8,128)}) custom-call(s32[8,16]{1,0:T(8,128)S(1)} %get-tuple-element.45.refs_0_, f32[8,4,128,128]{3,2,1,0:T(8,128)S(1)} %get-tuple-element.58.refs_3_.refs_1_, f32[8,2,128,128]{3,2,1,0:T(8,128)S(1)} %collective-permute-done.14.refs_2_, ...), custom_call_target="tpu_custom_call", output_to_operand_aliasing={{1}: (7, {})} | custom-call | bytes 1 | tf_op jit(solution)/shard_map/stage/pallas_call | solution.py:224
  (29 shorter events, 2.6 us)
Async XLA Ops:
  0.0 3.4 %copy-start = (f32[16,16,16]{2,1,0:T(8,128)S(1)}, f32[16,16,16]{2,1,0:T(8,128)}, u32[]{:S(2)}) copy-start(f32[16,16,16]{2,1,0:T(8,128)} %param.10) | copy-start | bytes 49156
  0.0 3.4 %copy-start.1 = (f32[16,16,16]{2,1,0:T(8,128)S(1)}, f32[16,16,16]{2,1,0:T(8,128)}, u32[]{:S(2)}) copy-start(f32[16,16,16]{2,1,0:T(8,128)} %param.11) | copy-start | bytes 49156
  0.0 3.4 %copy-start.2 = (s32[8,8]{1,0:T(8,128)S(1)}, s32[8,8]{1,0:T(8,128)}, u32[]{:S(2)}) copy-start(s32[8,8]{1,0:T(8,128)} %pair_ref.1) | copy-start | bytes 772
  0.0 3.4 %copy-start.3 = (s32[16]{0:T(128)S(1)}, s32[16]{0:T(128)}, u32[]{:S(2)}) copy-start(s32[16]{0:T(128)} %slot_ref.1) | copy-start | bytes 196
  1.3 2.1 %collective-permute-start = (bf16[128,2048]{1,0:T(8,128)(2,1)S(1)}, bf16[128,2048]{1,0:T(8,128)(2,1)S(1)}, u32[]{:S(2)}, u32[]{:S(2)}) collective-permute-start(bf16[128,2048]{1,0:T(8,128)(2,1)S(1)} %get-tuple-element.83), channel_id=1, source_target_pairs={{0,1},{1,0},{2,3},{3,2},{4,5},{5,4},{6,7},{7,6},{8,9},{9,8},{10,11... | collective-permute-start | bytes 1572872 | tf_op jit(solution)/shard_map/send_h1/ppermute | solution.py:261
  8.4 42.4 %collective-permute-start.1 = (bf16[1024,2048]{1,0:T(8,128)(2,1)S(1)}, bf16[1024,2048]{1,0:T(8,128)(2,1)S(1)}, u32[]{:S(2)}, u32[]{:S(2)}) collective-permute-start(bf16[1024,2048]{1,0:T(8,128)(2,1)S(1)} %get-tuple-element.47), channel_id=1, source_target_pairs={{0,1},{1,0},{2,3},{3,2},{4,5},{5,4},{6,7},{7,6},{8,9},{9,8},{10,11... | collective-permute-start | bytes 12582920 | tf_op jit(solution)/shard_map/send_train/ppermute | solution.py:261
  8.8 17.0 %collective-permute-start.4 = (bf16[128,2048]{1,0:T(8,128)(2,1)S(1)}, bf16[128,2048]{1,0:T(8,128)(2,1)S(1)}, u32[]{:S(2)}, u32[]{:S(2)}) collective-permute-start(bf16[128,2048]{1,0:T(8,128)(2,1)S(1)} %get-tuple-element.84.x0), channel_id=1, source_target_pairs={{0,12},{1,13},{2,14},{3,15},{4,0},{5,1},{6,2},{7,3},{8,4},{9,5},{1... | collective-permute-start | bytes 1572872 | tf_op jit(solution)/shard_map/send_a0/ppermute | solution.py:261
  13.5 14.8 %collective-permute-start.5 = (bf16[128,2048]{1,0:T(8,128)(2,1)S(1)}, bf16[128,2048]{1,0:T(8,128)(2,1)S(1)}, u32[]{:S(2)}, u32[]{:S(2)}) collective-permute-start(bf16[128,2048]{1,0:T(8,128)(2,1)S(1)} %get-tuple-element.84.x0), channel_id=1, source_target_pairs={{0,2},{1,3},{2,0},{3,1},{4,6},{5,7},{6,4},{7,5},{8,10},{9,11},{10,... | collective-permute-start | bytes 1572872 | tf_op jit(solution)/shard_map/send_y0/ppermute | solution.py:261
  15.1 22.9 %collective-permute-start.2 = (bf16[128,2048]{1,0:T(8,128)(2,1)S(1)}, bf16[128,2048]{1,0:T(8,128)(2,1)S(1)}, u32[]{:S(2)}, u32[]{:S(2)}) collective-permute-start(bf16[128,2048]{1,0:T(8,128)(2,1)S(1)} %get-tuple-element.84.x0), channel_id=1, source_target_pairs={{0,4},{1,5},{2,6},{3,7},{4,8},{5,9},{6,10},{7,11},{8,12},{9,13},{1... | collective-permute-start | bytes 1572872 | tf_op jit(solution)/shard_map/send_b0/ppermute | solution.py:261
  15.1 24.5 %collective-permute-start.3 = (bf16[128,2048]{1,0:T(8,128)(2,1)S(1)}, bf16[128,2048]{1,0:T(8,128)(2,1)S(1)}, u32[]{:S(2)}, u32[]{:S(2)}) collective-permute-start(bf16[128,2048]{1,0:T(8,128)(2,1)S(1)} %collective-permute-done.x1), channel_id=1, source_target_pairs={{0,2},{1,3},{2,0},{3,1},{4,6},{5,7},{6,4},{7,5},{8,10},{9,11},{10,... | collective-permute-start | bytes 1572872 | tf_op jit(solution)/shard_map/send_y1/ppermute | solution.py:261
  29.0 20.2 %collective-permute-start.8 = (bf16[128,2048]{1,0:T(8,128)(2,1)S(1)}, bf16[128,2048]{1,0:T(8,128)(2,1)S(1)}, u32[]{:S(2)}, u32[]{:S(2)}) collective-permute-start(bf16[128,2048]{1,0:T(8,128)(2,1)S(1)} %get-tuple-element.69.refs_4_), channel_id=1, source_target_pairs={{0,4},{1,5},{2,6},{3,7},{4,8},{5,9},{6,10},{7,11},{8,12},{9,13},{1... | collective-permute-start | bytes 1572872 | tf_op jit(solution)/shard_map/send_b1/ppermute | solution.py:261
  29.1 21.7 %collective-permute-start.9 = (bf16[128,2048]{1,0:T(8,128)(2,1)S(1)}, bf16[128,2048]{1,0:T(8,128)(2,1)S(1)}, u32[]{:S(2)}, u32[]{:S(2)}) collective-permute-start(bf16[128,2048]{1,0:T(8,128)(2,1)S(1)} %get-tuple-element.53.refs_5_), channel_id=1, source_target_pairs={{0,2},{1,3},{2,0},{3,1},{4,6},{5,7},{6,4},{7,5},{8,10},{9,11},{10,... | collective-permute-start | bytes 1572872 | tf_op jit(solution)/shard_map/send_ya0/ppermute | solution.py:261
  40.3 19.6 %collective-permute-start.6 = (bf16[128,2048]{1,0:T(8,128)(2,1)S(1)}, bf16[128,2048]{1,0:T(8,128)(2,1)S(1)}, u32[]{:S(2)}, u32[]{:S(2)}) collective-permute-start(bf16[128,2048]{1,0:T(8,128)(2,1)S(1)} %get-tuple-element.53.refs_5_), channel_id=1, source_target_pairs={{0,12},{1,13},{2,14},{3,15},{4,0},{5,1},{6,2},{7,3},{8,4},{9,5},{1... | collective-permute-start | bytes 1572872 | tf_op jit(solution)/shard_map/send_f0/ppermute | solution.py:261
  41.7 19.4 %collective-permute-start.7 = (bf16[128,2048]{1,0:T(8,128)(2,1)S(1)}, bf16[128,2048]{1,0:T(8,128)(2,1)S(1)}, u32[]{:S(2)}, u32[]{:S(2)}) collective-permute-start(bf16[128,2048]{1,0:T(8,128)(2,1)S(1)} %get-tuple-element.54.refs_3_), channel_id=1, source_target_pairs={{0,2},{1,3},{2,0},{3,1},{4,6},{5,7},{6,4},{7,5},{8,10},{9,11},{10,... | collective-permute-start | bytes 1572872 | tf_op jit(solution)/shard_map/send_yb0/ppermute | solution.py:261
  56.4 26.8 %collective-permute-start.18 = (f32[8,4,128,128]{3,2,1,0:T(8,128)S(1)}, f32[8,4,128,128]{3,2,1,0:T(8,128)S(1)}, u32[]{:S(2)}, u32[]{:S(2)}) collective-permute-start(f32[8,4,128,128]{3,2,1,0:T(8,128)S(1)} %get-tuple-element.72), channel_id=1, source_target_pairs={{0,1},{1,0},{2,3},{3,2},{4,5},{5,4},{6,7},{7,6},{8,9},{9,8},{10,11... | collective-permute-start | bytes 6291464 | tf_op jit(solution)/shard_map/send_part4/ppermute | solution.py:261
  66.7 31.0 %collective-permute-start.15 = (f32[8,4,128,128]{3,2,1,0:T(8,128)S(1)}, f32[8,4,128,128]{3,2,1,0:T(8,128)S(1)}, u32[]{:S(2)}, u32[]{:S(2)}) collective-permute-start(f32[8,4,128,128]{3,2,1,0:T(8,128)S(1)} %get-tuple-element.67), channel_id=1, source_target_pairs={{0,1},{1,0},{2,3},{3,2},{4,5},{5,4},{6,7},{7,6},{8,9},{9,8},{10,11... | collective-permute-start | bytes 6291464 | tf_op jit(solution)/shard_map/send_part5/ppermute | solution.py:261
  66.7 16.1 %collective-permute-start.10 = (bf16[128,2048]{1,0:T(8,128)(2,1)S(1)}, bf16[128,2048]{1,0:T(8,128)(2,1)S(1)}, u32[]{:S(2)}, u32[]{:S(2)}) collective-permute-start(bf16[128,2048]{1,0:T(8,128)(2,1)S(1)} %collective-permute-done.8.refs_5_), channel_id=1, source_target_pairs={{0,4},{1,5},{2,6},{3,7},{4,8},{5,9},{6,10},{7,11},{8,12},{9,13},{1... | collective-permute-start | bytes 1572872 | tf_op jit(solution)/shard_map/send_f1/ppermute | solution.py:261
  66.7 16.5 %collective-permute-start.11 = (bf16[128,2048]{1,0:T(8,128)(2,1)S(1)}, bf16[128,2048]{1,0:T(8,128)(2,1)S(1)}, u32[]{:S(2)}, u32[]{:S(2)}) collective-permute-start(bf16[128,2048]{1,0:T(8,128)(2,1)S(1)} %collective-permute-done.8.refs_5_), channel_id=1, source_target_pairs={{0,2},{1,3},{2,0},{3,1},{4,6},{5,7},{6,4},{7,5},{8,10},{9,11},{10,... | collective-permute-start | bytes 1572872 | tf_op jit(solution)/shard_map/send_yb1/ppermute | solution.py:261
  68.2 24.1 %collective-permute-start.17 = (bf16[128,2048]{1,0:T(8,128)(2,1)S(1)}, bf16[128,2048]{1,0:T(8,128)(2,1)S(1)}, u32[]{:S(2)}, u32[]{:S(2)}) collective-permute-start(bf16[128,2048]{1,0:T(8,128)(2,1)S(1)} %collective-permute-done.6.refs_6_), channel_id=1, source_target_pairs={{0,2},{1,3},{2,0},{3,1},{4,6},{5,7},{6,4},{7,5},{8,10},{9,11},{10,... | collective-permute-start | bytes 1572872 | tf_op jit(solution)/shard_map/send_yf0/ppermute | solution.py:261
  82.9 14.8 %collective-permute-start.16 = (bf16[128,2048]{1,0:T(8,128)(2,1)S(1)}, bf16[128,2048]{1,0:T(8,128)(2,1)S(1)}, u32[]{:S(2)}, u32[]{:S(2)}) collective-permute-start(bf16[128,2048]{1,0:T(8,128)(2,1)S(1)} %get-tuple-element.69.refs_4_), channel_id=1, source_target_pairs={{0,12},{1,13},{2,14},{3,15},{4,0},{5,1},{6,2},{7,3},{8,4},{9,5},{1... | collective-permute-start | bytes 1572872 | tf_op jit(solution)/shard_map/send_a1/ppermute | solution.py:261
  89.9 20.0 %collective-permute-start.20 = (f32[8,4,128,128]{3,2,1,0:T(8,128)S(1)}, f32[8,4,128,128]{3,2,1,0:T(8,128)S(1)}, u32[]{:S(2)}, u32[]{:S(2)}) collective-permute-start(f32[8,4,128,128]{3,2,1,0:T(8,128)S(1)} %get-tuple-element.78), channel_id=1, source_target_pairs={{0,1},{1,0},{2,3},{3,2},{4,5},{5,4},{6,7},{7,6},{8,9},{9,8},{10,11... | collective-permute-start | bytes 6291464 | tf_op jit(solution)/shard_map/send_part6/ppermute | solution.py:261
  90.0 17.6 %collective-permute-start.13 = (bf16[128,2048]{1,0:T(8,128)(2,1)S(1)}, bf16[128,2048]{1,0:T(8,128)(2,1)S(1)}, u32[]{:S(2)}, u32[]{:S(2)}) collective-permute-start(bf16[128,2048]{1,0:T(8,128)(2,1)S(1)} %collective-permute-done.10.refs_8_), channel_id=1, source_target_pairs={{0,2},{1,3},{2,0},{3,1},{4,6},{5,7},{6,4},{7,5},{8,10},{9,11},{10,... | collective-permute-start | bytes 1572872 | tf_op jit(solution)/shard_map/send_yf1/ppermute | solution.py:261
  92.3 15.3 %collective-permute-start.12 = (bf16[128,2048]{1,0:T(8,128)(2,1)S(1)}, bf16[128,2048]{1,0:T(8,128)(2,1)S(1)}, u32[]{:S(2)}, u32[]{:S(2)}) collective-permute-start(bf16[128,2048]{1,0:T(8,128)(2,1)S(1)} %get-tuple-element.61.refs_4_), channel_id=1, source_target_pairs={{0,12},{1,13},{2,14},{3,15},{4,0},{5,1},{6,2},{7,3},{8,4},{9,5},{1... | collective-permute-start | bytes 1572872 | tf_op jit(solution)/shard_map/send_xa1/ppermute | solution.py:261
  102.2 7.8 %collective-permute-start.19 = (f32[8,2,128,128]{3,2,1,0:T(8,128)S(1)}, f32[8,2,128,128]{3,2,1,0:T(8,128)S(1)}, u32[]{:S(2)}, u32[]{:S(2)}) collective-permute-start(f32[8,2,128,128]{3,2,1,0:T(8,128)S(1)} %get-tuple-element.76), channel_id=1, source_target_pairs={{0,1},{1,0},{2,3},{3,2},{4,5},{5,4},{6,7},{7,6},{8,9},{9,8},{10,11... | collective-permute-start | bytes 3145736 | tf_op jit(solution)/shard_map/send_part7/ppermute | solution.py:261
  110.0 3.9 %collective-permute-start.14 = (f32[8,2,128,128]{3,2,1,0:T(8,128)S(1)}, f32[8,2,128,128]{3,2,1,0:T(8,128)S(1)}, u32[]{:S(2)}, u32[]{:S(2)}) collective-permute-start(f32[8,2,128,128]{3,2,1,0:T(8,128)S(1)} %get-tuple-element.63), channel_id=1, source_target_pairs={{0,1},{1,0},{2,3},{3,2},{4,5},{5,4},{6,7},{7,6},{8,9},{9,8},{10,11... | collective-permute-start | bytes 3145736 | tf_op jit(solution)/shard_map/send_part/ppermute | solution.py:261

commit v3 on v2

--- a/solution.py
+++ b/solution.py
@@ -11,9 +11,10 @@
 BLK = 128
 SLOT = PROJ * PROJ
 F32 = jnp.float32
+HALVES_LIMIT = 44
 BF16 = jnp.bfloat16
 NT = (((1,), (1,)), ((), ()))
-SMALL = pl.CostEstimate(flops=1, bytes_accessed=1, transcendentals=0)
+SMALL = pl.CostEstimate(flops=10**9, bytes_accessed=1, transcendentals=0)
 
 
 def split3(x):
@@ -30,6 +31,37 @@
     two = rest.astype(BF16)
     three = (rest - two.astype(F32)).astype(BF16)
     return one, two, three
+
+
+def halves_kernel(train, twin_train, keep, rest, theirs, token, sems):
+    token[...] = jnp.zeros_like(token)
+    half = keep.shape[1]
+    core = lax.axis_index("rows") & 1
+    mine = pl.ds(pl.multiple_of(core * half, half), half)
+    other = pl.ds(pl.multiple_of((1 - core) * half, half), half)
+    copies = [
+        pltpu.make_async_copy(train.at[:, mine], keep, sems.at[0]),
+        pltpu.make_async_copy(twin_train.at[:, mine], theirs, sems.at[1]),
+        pltpu.make_async_copy(train.at[:, other], rest, sems.at[2]),
+    ]
+    for copy in copies:
+        copy.start()
+    for copy in copies:
+        copy.wait()
+
+
+def make_halves(train, twin_train):
+    side = jax.ShapeDtypeStruct((train.shape[0], train.shape[1] // 2), BF16)
+    return pl.pallas_call(
+        halves_kernel,
+        out_shape=[side] * 3 + [jax.ShapeDtypeStruct((8, 128), F32)],
+        in_specs=[pl.BlockSpec(memory_space=pl.ANY)] * 2,
+        out_specs=[pl.BlockSpec(memory_space=pltpu.VMEM)] * 4,
+        scratch_shapes=[pltpu.SemaphoreType.DMA((3,))],
+        compiler_params=pltpu.CompilerParams(vmem_limit_bytes=HALVES_LIMIT << 20),
+        cost_estimate=SMALL,
+        name="halves",
+    )(train, twin_train)
 
 
 def precondition(x_refs, y_refs, high, low, skip):
@@ -43,20 +75,9 @@
             ref[:, cols] = y[i * rows : (i + 1) * rows].astype(BF16)
 
 
-def prepare_kernel(
-    layers, slot_ref, pair_ref, a_ref, b_ref, x0, x1, train, high_ref, low_ref, y0, y1, keep, away, table, xa, xb, sems
-):
+def prepare_kernel(layers, slot_ref, pair_ref, a_ref, b_ref, x0, x1, high_ref, low_ref, y0, y1, table, xa, xb):
     me = lax.axis_index("rows")
     core = me & 1
-    half = keep.shape[1]
-    mine = pl.multiple_of(core * half, half)
-    other = pl.multiple_of((1 - core) * half, half)
-    loads = [
-        pltpu.make_async_copy(train.at[:, pl.ds(other, half)], away, sems.at[0]),
-        pltpu.make_async_copy(train.at[:, pl.ds(mine, half)], keep, sems.at[1]),
-    ]
-    for load in loads:
-        load.start()
     row = lax.broadcasted_iota(jnp.int32, (PROJ, SLOT), 0)
     col = lax.broadcasted_iota(jnp.int32, (PROJ, SLOT), 1)
     pick_i = jnp.where(col // PROJ == row, 1.0, 0.0).astype(BF16)
@@ -95,33 +116,60 @@
         for k in range(slots):
             q = pair_ref[t, k]
             table[t, (((q >> 2) - (me >> 2)) & 3) * 4 + ((q ^ me) & 3)] = k
-    for load in loads:
-        load.wait()
-
-
-def prepare(layer_slot, pair_query, in_factor, out_factor, x0, x1, train, jobs):
+
+
+def prepare(layer_slot, pair_query, in_factor, out_factor, x0, x1, jobs):
     layers = in_factor.shape[0]
     a_rows = in_factor.reshape(layers * PROJ, PROJ)
     b_rows = out_factor.reshape(layers * PROJ, PROJ)
     vmem = pl.BlockSpec(memory_space=pltpu.VMEM)
     smem = pl.BlockSpec(memory_space=pltpu.SMEM)
-    side = jax.ShapeDtypeStruct((train.shape[0], train.shape[1] // 2), BF16)
     factor = jax.ShapeDtypeStruct((layers // 2, SLOT, SLOT), BF16)
     piece = jax.ShapeDtypeStruct(x0.shape, BF16)
     return pl.pallas_call(
         functools.partial(prepare_kernel, layers),
-        out_shape=[factor, factor, piece, piece, side, side, jax.ShapeDtypeStruct((pair_query.shape[0], jobs), jnp.int32)],
-        in_specs=[smem] * 2 + [vmem] * 4 + [pl.BlockSpec(memory_space=pl.ANY)],
-        out_specs=[vmem] * 6 + [smem],
+        out_shape=[factor, factor, piece, piece, jax.ShapeDtypeStruct((pair_query.shape[0], jobs), jnp.int32)],
+        in_specs=[smem] * 2 + [vmem] * 4,
+        out_specs=[vmem] * 4 + [smem],
         scratch_shapes=[
             pltpu.VMEM((layers * PROJ, SLOT), F32),
             pltpu.VMEM((layers * PROJ, SLOT), F32),
-            pltpu.SemaphoreType.DMA((2,)),
         ],
-        compiler_params=pltpu.CompilerParams(vmem_limit_bytes=40 << 20),
+        compiler_params=pltpu.CompilerParams(vmem_limit_bytes=16 << 20),
         cost_estimate=SMALL,
         name="prepare",
-    )(layer_slot, pair_query, a_rows, b_rows, x0, x1, train)
+    )(layer_slot, pair_query, a_rows, b_rows, x0, x1)
+
+
+def halves_kernel(train, twin_train, keep, rest, theirs, token, sems):
+    token[...] = jnp.zeros_like(token)
+    half = keep.shape[1]
+    core = lax.axis_index("rows") & 1
+    mine = pl.ds(pl.multiple_of(core * half, half), half)
+    other = pl.ds(pl.multiple_of((1 - core) * half, half), half)
+    copies = [
+        pltpu.make_async_copy(train.at[:, mine], keep, sems.at[0]),
+        pltpu.make_async_copy(twin_train.at[:, mine], theirs, sems.at[1]),
+        pltpu.make_async_copy(train.at[:, other], rest, sems.at[2]),
+    ]
+    for copy in copies:
+        copy.start()
+    for copy in copies:
+        copy.wait()
+
+
+def make_halves(train, twin_train):
+    side = jax.ShapeDtypeStruct((train.shape[0], train.shape[1] // 2), BF16)
+    return pl.pallas_call(
+        halves_kernel,
+        out_shape=[side] * 3 + [jax.ShapeDtypeStruct((8, 128), F32)],
+        in_specs=[pl.BlockSpec(memory_space=pl.ANY)] * 2,
+        out_specs=[pl.BlockSpec(memory_space=pltpu.VMEM)] * 4,
+        scratch_shapes=[pltpu.SemaphoreType.DMA((3,))],
+        compiler_params=pltpu.CompilerParams(vmem_limit_bytes=HALVES_LIMIT << 20),
+        cost_estimate=SMALL,
+        name="halves",
+    )(train, twin_train)
 
 
 def precondition(x_refs, y_refs, high, low):
@@ -149,92 +197,126 @@
     )(x0, x1, high, low)
 
 
-def stage_kernel(adds, n_sums, n_train, n_pieces, aliased, *refs):
-    refs = list(refs)
-    table = refs.pop(0)
-    sums = [refs.pop(0) for _ in range(n_sums)]
-    trains = [refs.pop(0) for _ in range(n_train)]
-    pieces = [refs.pop(0) for _ in range(n_pieces)]
-    if aliased:
-        refs.pop(0)
+def stage_kernel(adds, products, n_arrays, n_idle, *refs):
+    table, arrays, refs = refs[0], refs[1 : 1 + n_arrays], list(refs[1 + n_arrays + n_idle :])
     token = refs.pop(0)
-    out = refs.pop(0) if adds else None
-    parts = [refs.pop(0) for _ in range(n_train)]
+    puts = len(adds) + sum(len(product[2]) for product in products)
+    out = refs.pop(0) if puts else None
+    parts = [None if product[2] else refs.pop(0) for product in products]
     token[...] = jnp.zeros_like(token)
-    puts = []
-    if adds:
+    started = []
+
+    def put(t, job, value):
         s_v, sems = refs
-        for i, (job, ours, j, theirs, k) in enumerate(adds):
-            for t in range(table.shape[0]):
-                slot = table[t, job]
-                copy = pltpu.make_async_copy(s_v.at[t, i], out.at[t, jnp.maximum(slot, 0)], sems.at[t, i])
-                puts.append((slot >= 0, copy))
-                s_v[t, i] = sums[ours][t, j] + sums[theirs][t, k]
-
-                @pl.when(slot >= 0)
-                def _(copy=copy):
-                    copy.start()
+        at = len(started)
+        i, j = at // table.shape[0], at % table.shape[0]
+        slot = table[t, job]
+        copy = pltpu.make_async_copy(s_v.at[i, j], out.at[t, jnp.maximum(slot, 0)], sems.at[i, j])
+        s_v[i, j] = value
+        started.append((slot >= 0, copy))
+
+        @pl.when(slot >= 0)
+        def _():
+            copy.start()
+
+    for job, ours, j, theirs, k in adds:
+        for t in range(table.shape[0]):
+            put(t, job, arrays[ours][t, j] + arrays[theirs][t, k])
 
     step = 2 * BLK
-    for train, part in zip(trains, parts):
+    for (train, pieces, sums, before), part in zip(products, parts):
+        skip = 0
+        if before is not None:
+            skip = arrays[before].shape[1]
+            part[:, :skip] = arrays[before][...]
+        train = arrays[train]
         for m in range(train.shape[0] // step):
-            for h in range(0, n_pieces, 2):
-                q = jnp.concatenate([ref[...] for ref in pieces[h : h + 2]], axis=0)
+            for h in range(0, len(pieces), 2):
+                q = jnp.concatenate([arrays[i][...] for i in pieces[h : h + 2]], axis=0)
                 s = lax.dot_general(train[m * step : (m + 1) * step], q, NT, preferred_element_type=F32)
                 for u in range(step // BLK):
                     for j in range(2):
-                        part[m * (step // BLK) + u, h + j] = s[u * BLK : (u + 1) * BLK, j * BLK : (j + 1) * BLK]
-
-    for named, copy in puts:
+                        t = m * (step // BLK) + u
+                        value = s[u * BLK : (u + 1) * BLK, j * BLK : (j + 1) * BLK]
+                        if sums:
+                            job, at, column = sums[h + j]
+                            put(t, job, value + arrays[at][t, column])
+                        else:
+                            part[t, skip + h + j] = value
+
+    for named, copy in started:
 
         @pl.when(named)
         def _(copy=copy):
             copy.wait()
 
 
-def stage(table, adds, trains, pieces, out, slots, cost=0):
-    any_spec = pl.BlockSpec(memory_space=pl.ANY)
+def stage(table, adds, products, out, slots, cost=0, wait=()):
     vmem = pl.BlockSpec(memory_space=pltpu.VMEM)
-    sums, spots = [], []
-    for job, *pair in adds:
-        spot = [job]
-        for array, column in pair:
-            at = next((i for i, other in enumerate(sums) if other is array), len(sums))
-            if at == len(sums):
-                sums.append(array)
-            spot += [at, column]
-        spots.append(tuple(spot))
-    args = [table, *sums, *trains, *pieces]
-    specs = [pl.BlockSpec(memory_space=pltpu.SMEM)] + [vmem] * (len(args) - 1)
-    aliases = {}
-    if adds and out is not None:
-        aliases = {len(args): 1}
+    arrays = []
+
+    def index(array):
+        for i, other in enumerate(arrays):
+            if other is array:
+                return i
+        arrays.append(array)
+        return len(arrays) - 1
+
+    blocks = table.shape[0]
+    adds = tuple((job, index(a), i, index(b), j) for job, (a, i), (b, j) in adds)
+    shapes, out_specs, scratch = [jax.ShapeDtypeStruct((8, 128), F32)], [vmem], []
+    puts = len(adds) + sum(len(product[2]) for product in products)
+    if puts:
+        shapes.append(jax.ShapeDtypeStruct((blocks, slots, BLK, BLK), F32))
+        out_specs.append(pl.BlockSpec(memory_space=pl.ANY))
+        scratch = [pltpu.VMEM((puts, blocks, BLK, BLK), F32), pltpu.SemaphoreType.DMA((puts, blocks))]
+    spots = []
+    for train, pieces, sums, before in products:
+        if not sums:
+            width = len(pieces) + (0 if before is None else before.shape[1])
+            shapes.append(jax.ShapeDtypeStruct((blocks, width, BLK, BLK), F32))
+            out_specs.append(vmem)
+        spots.append((
+            index(train), tuple(index(piece) for piece in pieces),
+            tuple((job, index(array), i) for job, (array, i) in sums), None if before is None else index(before),
+        ))
+    args = [table, *arrays]
+    specs = [pl.BlockSpec(memory_space=pltpu.SMEM)] + [vmem] * len(arrays)
+    args += wait
+    specs += [pl.BlockSpec(memory_space=pl.ANY)] * len(wait)
+    aliased = bool(puts) and out is not None
+    if aliased:
         args.append(out)
-        specs.append(any_spec)
-    blocks = table.shape[0]
-    shapes, out_specs, scratch = [jax.ShapeDtypeStruct((8, 128), F32)], [vmem], []
-    if adds:
-        shapes.append(jax.ShapeDtypeStruct((blocks, slots, BLK, BLK), F32))
-        out_specs.append(any_spec)
-        scratch = [pltpu.VMEM((blocks, len(adds), BLK, BLK), F32), pltpu.SemaphoreType.DMA((blocks, len(adds)))]
-    for _ in trains:
-        shapes.append(jax.ShapeDtypeStruct((blocks, len(pieces), BLK, BLK), F32))
-        out_specs.append(vmem)
-    body = functools.partial(stage_kernel, tuple(spots), len(sums), len(trains), len(pieces), bool(aliases))
+        specs.append(pl.BlockSpec(memory_space=pl.ANY))
+    body = functools.partial(stage_kernel, adds, tuple(spots), len(arrays), len(wait) + aliased)
     token, *rest = pl.pallas_call(
         body,
         out_shape=shapes,
         in_specs=specs,
         out_specs=out_specs,
         scratch_shapes=scratch,
-        input_output_aliases=aliases,
+        input_output_aliases={len(args) - 1: 1} if aliased else {},
         compiler_params=pltpu.CompilerParams(vmem_limit_bytes=20 << 20),
-        cost_estimate=pl.CostEstimate(flops=cost * 10**9, bytes_accessed=1, transcendentals=0),
+        cost_estimate=pl.CostEstimate(flops=int(cost * 1.15e9), bytes_accessed=1, transcendentals=0),
         name="stage",
     )(*args)
-    if adds:
+    if puts:
         out = rest.pop(0)
     return token, out, rest
+
+
+def pass_kernel(x_ref, y_ref):
+    y_ref[...] = x_ref[...]
+
+
+def stand(token, cost):
+    return pl.pallas_call(
+        pass_kernel,
+        out_shape=jax.ShapeDtypeStruct(token.shape, token.dtype),
+        compiler_params=pltpu.CompilerParams(vmem_limit_bytes=1 << 20),
+        cost_estimate=pl.CostEstimate(flops=int(cost * 1.15e9), bytes_accessed=1, transcendentals=0),
+        name="stand",
+    )(token)
 
 
 def after(x, *deps):
@@ -275,9 +357,10 @@
         (("a1", "h1", down), ("yf0", "f0", across)),
         (("xa1", "y1", down), ("yf1", "f1", across)),
     ]
-    work = {4: ["h0", "h1", "a0", "y0"], 5: ["b0", "y1", "b1", "ya0"], 6: ["f0", "yb0", "f1", "yb1"], 7: ["a1", "yf0"]}
-    adding = {4: 6, 5: 7, 6: 8, 7: 8}
-    cost = {4: 1, 5: 1, 6: 1, 7: 8}
+    work = {3: ["h0", "h1", "a0", "y0"], 4: ["b0", "y1", "b1", "ya0"], 5: ["f0", "yb0"], 6: ["f1", "yb1"], 7: ["a1", "yf0"]}
+    exchange = (4, 6, 7)
+    cost = {3: 1, 4: 1, 5: 1, 6: 1, 7: 1, 8: 12, 9: 1}
+    stand_cost = 60
     slots = pair_query.shape[1]
     half = query_grads.shape[1] // 2
     core = lax.axis_index("rows") % 2
@@ -287,11 +370,11 @@
     for step in plan[:2]:
         for name, source, perm in step:
             raw[name] = send(raw[source], perm, name)
-    high, low, own0, own1, keep, away, table = prepare(
-        layer_slot, pair_query, in_factor, out_factor, raw["h0"], raw["h1"], train_grads, 2 * 8
+    high, low, own0, own1, table = prepare(
+        layer_slot, pair_query, in_factor, out_factor, raw["h0"], raw["h1"], 2 * 8
     )
     got = {"h0": own0, "h1": own1}
-    trains = (keep, send(away, twin, "train"))
+    keep, rest, their_train, halves_token = make_halves(train_grads, send(train_grads, twin, "train"))
     ours, theirs, open_jobs = {}, {}, list(other_name)
     out, tokens = None, []
 
@@ -301,37 +384,40 @@
             open_jobs.remove(n)
         return [(job[n], ours[n], theirs[other_name[n]]) for n in done]
 
-    arriving = {}
+    held, columns = None, []
     for s in range(2, len(plan) + 1):
         names = [name for name, _, _ in plan[s - 2]]
         if s < 4:
             got[names[0]], got[names[1]] = make_ready(raw[names[0]], raw[names[1]], high, low)
-        past = [got[name] for name in names] + tokens
+        past = [got[name] for name in names] + (tokens if s > 3 else [halves_token] * (s == 2))
         if s < len(plan):
             for name, source, perm in plan[s]:
                 deps = [v for v in past if v is not got[source]]
                 got[name] = send(after(got[source], *deps), perm, name)
         if s not in work:
             continue
-        for part in arriving.pop(s, []):
-            theirs.update(part)
         pieces = [got[n] for n in work[s]]
-        pieces[0] = after(pieces[0], *[got[name] for name in names if name not in work[s][:1]])
-        token, out, (mine, away) = stage(table, ready_adds(), trains, pieces, out, slots, cost[s])
+        products = [(keep, pieces, (), None), (their_train, pieces, (), held)]
+        token, _, (mine, held) = stage(table, [], products, None, slots, cost[s], tokens)
         tokens = [token]
-        away = send(away, twin, "part" + str(s))
         ours.update({n: (mine, i) for i, n in enumerate(work[s])})
-        arriving.setdefault(adding[s], []).append({n: (away, i) for i, n in enumerate(work[s])})
+        columns += work[s]
+        if s in exchange:
+            part = send(held, twin, "part" + str(s))
+            theirs.update({n: (part, i) for i, n in enumerate(columns)})
+            held, columns = None, []
+    late = {n: theirs.pop(n) for n in work[len(plan)]}
+    adds = ready_adds()
+    token, out, _ = stage(table, adds, [], None, slots, 1, [stand(tokens[0], stand_cost)])
+    theirs.update(late)
     names = [name for name, _, _ in plan[-1]]
-    pieces = [after(got[names[0]], *tokens), got[names[1]]]
-    _, _, (away,) = stage(table, [], trains[1:], pieces, out, slots)
-    away = send(away, twin, "part")
-    for part in arriving.pop(8, []):
-        theirs.update(part)
-    _, out, (mine,) = stage(table, ready_adds(), trains[:1], pieces, out, slots)
+    pieces = [got[name] for name in names]
+    twins = [send(after(piece, token), twin, "c" + name) for piece, name in zip(pieces, names)]
+    _, _, (mine,) = stage(table, [], [(keep, pieces, (), None)], None, slots, cost[8], [token])
     ours.update({n: (mine, i) for i, n in enumerate(names)})
-    theirs.update({n: (away, i) for i, n in enumerate(names)})
-    _, out, _ = stage(table, ready_adds(), [], [], out, slots)
+    adds = ready_adds()
+    sums = tuple((job[other_name[name]], ours[other_name[name]]) for name in names)
+    _, out, _ = stage(table, adds, [(rest, twins, sums, None)], out, slots, cost[9])
     return out
 
 

time: 117 us -> 105 us (0.90)
  waiting for transfers between devices: 57.4 us -> 15.9 us
  starting transfers between devices: 20.2 us -> 42.5 us
  local copies, waits for them, and re-layouts: 0.01 us -> 5.34 us
  Pallas kernels: 37.4 us -> 39.6 us
    ppermute x21, waiting for transfers between devices: 57.4 us -> 15.9 us  [send(): return lax.ppermute(x, 'rows', perm)]
    ppermute x21, starting transfers between devices: 20.2 us -> 42.5 us  [send(): return lax.ppermute(x, 'rows', perm)]
    pallas_call x0 -> x2, Pallas kernels: none -> 6.71 us  [the longest x1 6.71 us: make_halves(): pl.pallas_call(halves_kernel, out_shape=[side] * 3 + [jax.ShapeDtypeStruc...]
    unnamed x8 -> x10, local copies, waits for them, and re-layouts: 0.01 us -> 5.34 us
    pallas_call x7 -> x8, Pallas kernels: 31.1 us -> 28.2 us  [stage(): pl.pallas_call(body, out_shape=shapes, in_specs=specs, out_specs=out_spec...]
    pallas_call x1, Pallas kernels: 4.92 us -> 3.24 us  [prepare(): pl.pallas_call(functools.partial(prepare_kernel, layers), out_shape=[fact...]
  transfers between devices with their start and end apart: 21 -> 21, of which waited for: 13 -> 6; matrix products, arithmetic and copies ran while one was open for 0% -> 1% of each run, Pallas kernels for 26% -> 34%
where the time goes in v3:
time: 105 us
  starting transfers between devices  42.5 us (40%)
  Pallas kernels  39.6 us (38%)
  waiting for transfers between devices  15.9 us (15%)
  local copies, waits for them, and re-layouts  5.34 us (5%)
  other arithmetic  1.27 us (1%)
    ppermute x21, starting transfers between devices, send(): return lax.ppermute(x, 'rows', perm)  42.5 us
    pallas_call x8, Pallas kernels, stage(): pl.pallas_call(body, out_shape=shapes, in_specs=specs, out_specs=out_spec...  28.2 us
    ppermute x21, waiting for transfers between devices, send(): return lax.ppermute(x, 'rows', perm)  15.9 us
    pallas_call x1, Pallas kernels, make_halves(): pl.pallas_call(halves_kernel, out_shape=[side] * 3 + [jax.ShapeDtypeStruc...  6.71 us
    unnamed x10, local copies, waits for them, and re-layouts  5.34 us
    pallas_call x1, Pallas kernels, prepare(): pl.pallas_call(functools.partial(prepare_kernel, layers), out_shape=[fact...  3.24 us
  transfers between devices with their start and end apart: 21, of which 6 were waited for; matrix products, arithmetic and copies ran while one was open for 1% of the time, Pallas kernels for 34%

profile of v3, /device:TPU:0, one launch (start us, length us, event | category | flops | bytes accessed | tf_op | source)
XLA Modules:
  0.0 104.8 jit_solution(2991859664692797799)
XLA Ops:
  0.5 1.3 %broadcast_select_fusion = (bf16[128,2048]{1,0:T(8,128)(2,1)S(1)}, bf16[128,2048]{1,0:T(8,128)(2,1)S(1)}) fusion(pred[]{:T(512)S(6)} %eq.6, bf16[128,4096]{1,0:T(8,128)(2,1)} %param.7), kind=kLoop, calls=%fused_computation | loop fusion | flops 524288 | bytes 2097153 | tf_op jit(solution)/shard_map/jit(_where)/select_n | solution.py:369
  1.9 3.0 %collective-permute-start.3 = (bf16[128,2048]{1,0:T(8,128)(2,1)S(1)}, bf16[128,2048]{1,0:T(8,128)(2,1)S(1)}, u32[]{:S(2)}, u32[]{:S(2)}) collective-permute-start(bf16[128,2048]{1,0:T(8,128)(2,1)S(1)} %get-tuple-element.91.x0), channel_id=1, source_target_pairs={{0,2},{1,3},{2,0},{3,1},{4,6},{5,7},{6,4},{7,5},{8,10},{9,11},{10,... | collective-permute-start | bytes 1572872 | tf_op jit(solution)/shard_map/send_y0/ppermute | solution.py:343
  4.8 3.6 %collective-permute-start.2 = (bf16[128,2048]{1,0:T(8,128)(2,1)S(1)}, bf16[128,2048]{1,0:T(8,128)(2,1)S(1)}, u32[]{:S(2)}, u32[]{:S(2)}) collective-permute-start(bf16[128,2048]{1,0:T(8,128)(2,1)S(1)} %get-tuple-element.91.x0), channel_id=1, source_target_pairs={{0,12},{1,13},{2,14},{3,15},{4,0},{5,1},{6,2},{7,3},{8,4},{9,5},{1... | collective-permute-start | bytes 1572872 | tf_op jit(solution)/shard_map/send_a0/ppermute | solution.py:343
  8.4 5.6 %collective-permute-done.x1 = bf16[128,2048]{1,0:T(8,128)(2,1)S(1)} collective-permute-done((bf16[128,2048]{1,0:T(8,128)(2,1)S(1)}, bf16[128,2048]{1,0:T(8,128)(2,1)S(1)}, u32[]{:S(2)}, u32[]{:S(2)}) %collective-permute-start) | collective-permute-done | bytes 524320 | tf_op jit(solution)/shard_map/send_h1/ppermute | solution.py:343
  14.0 2.9 %collective-permute-start.5 = (bf16[128,2048]{1,0:T(8,128)(2,1)S(1)}, bf16[128,2048]{1,0:T(8,128)(2,1)S(1)}, u32[]{:S(2)}, u32[]{:S(2)}) collective-permute-start(bf16[128,2048]{1,0:T(8,128)(2,1)S(1)} %collective-permute-done.x1), channel_id=1, source_target_pairs={{0,2},{1,3},{2,0},{3,1},{4,6},{5,7},{6,4},{7,5},{8,10},{9,11},{10,... | collective-permute-start | bytes 1572872 | tf_op jit(solution)/shard_map/send_y1/ppermute | solution.py:343
  16.9 0.9 copy-done.1
  17.8 0.9 copy-done.2
  18.7 0.7 copy-done.3
  20.0 3.2 %prepare.1 = (bf16[8,256,256]{2,1,0:T(8,128)(2,1)S(1)}, bf16[8,256,256]{2,1,0:T(8,128)(2,1)S(1)}, bf16[128,2048]{1,0:T(8,128)(2,1)S(1)}, bf16[128,2048]{1,0:T(8,128)(2,1)S(1)}, s32[8,16]{1,0:T(8,128)S(1)}) custom-call(s32[16]{0:T(128)S(1)} %copy-done.4, s32[8,8]{1,0:T(8,128)S(1)} %copy-done.3, f32[256,16]{1,0:T(8,128)S(1)} %bitcast.2, ...), custom_call_target="tpu_custom_call" | custom-call | flops 1000000000 | bytes 1 | tf_op jit(solution)/shard_map/prepare/pallas_call | solution.py:129
  23.3 0.7 ready.2
  24.0 6.7 %halves.1 = (bf16[1024,2048]{1,0:T(8,128)(2,1)S(1)}, bf16[1024,2048]{1,0:T(8,128)(2,1)S(1)}, bf16[1024,2048]{1,0:T(8,128)(2,1)}, f32[8,128]{1,0:T(8,128)}) custom-call(bf16[1024,4096]{1,0:T(8,128)(2,1)} %train.1, bf16[1024,4096]{1,0:T(8,128)(2,1)} %collective-permute-done.1.twin_train), custom_call_target="tpu_custom_call" | custom-call | flops 1000000000 | bytes 1 | tf_op jit(solution)/shard_map/halves/pallas_call | solution.py:163
  30.7 1.6 %collective-permute-start.8 = (bf16[128,2048]{1,0:T(8,128)(2,1)S(1)}, bf16[128,2048]{1,0:T(8,128)(2,1)S(1)}, u32[]{:S(2)}, u32[]{:S(2)}) collective-permute-start(bf16[128,2048]{1,0:T(8,128)(2,1)S(1)} %get-tuple-element.67.refs_3_), channel_id=1, source_target_pairs={{0,4},{1,5},{2,6},{3,7},{4,8},{5,9},{6,10},{7,11},{8,12},{9,13},{1... | collective-permute-start | bytes 1572872 | tf_op jit(solution)/shard_map/send_b1/ppermute | solution.py:343
  32.9 0.7 ready.3
  33.6 2.2 %collective-permute-start.6 = (bf16[128,2048]{1,0:T(8,128)(2,1)S(1)}, bf16[128,2048]{1,0:T(8,128)(2,1)S(1)}, u32[]{:S(2)}, u32[]{:S(2)}) collective-permute-start(bf16[128,2048]{1,0:T(8,128)(2,1)S(1)} %get-tuple-element.63.refs_4_), channel_id=1, source_target_pairs={{0,12},{1,13},{2,14},{3,15},{4,0},{5,1},{6,2},{7,3},{8,4},{9,5},{1... | collective-permute-start | bytes 1572872 | tf_op jit(solution)/shard_map/send_f0/ppermute | solution.py:343
  35.8 1.7 %collective-permute-start.7 = (bf16[128,2048]{1,0:T(8,128)(2,1)S(1)}, bf16[128,2048]{1,0:T(8,128)(2,1)S(1)}, u32[]{:S(2)}, u32[]{:S(2)}) collective-permute-start(bf16[128,2048]{1,0:T(8,128)(2,1)S(1)} %get-tuple-element.58.refs_2_), channel_id=1, source_target_pairs={{0,2},{1,3},{2,0},{3,1},{4,6},{5,7},{6,4},{7,5},{8,10},{9,11},{10,... | collective-permute-start | bytes 1572872 | tf_op jit(solution)/shard_map/send_yb0/ppermute | solution.py:343
  37.4 2.2 %copy-done = bf16[1024,2048]{1,0:T(8,128)(2,1)S(1)} copy-done((bf16[1024,2048]{1,0:T(8,128)(2,1)S(1)}, bf16[1024,2048]{1,0:T(8,128)(2,1)}, u32[]{:S(2)}) %copy-start) | copy-done | bytes 4194328
  39.6 5.1 %stage.8 = (f32[8,128]{1,0:T(8,128)S(1)}, f32[8,4,128,128]{3,2,1,0:T(8,128)S(1)}, f32[8,4,128,128]{3,2,1,0:T(8,128)S(1)}) custom-call(s32[8,16]{1,0:T(8,128)S(1)} %get-tuple-element.48.refs_0_, bf16[1024,2048]{1,0:T(8,128)(2,1)S(1)} %get-tuple-element.49.refs_1_, bf16[128,2048]{1,0:T(8,128)(2,1)S(1)} %get-tuple-element.50.refs_2_, ...), custom_call_target="tpu_custom_call" | custom-call | flops 1150000000 | bytes 1 | tf_op jit(solution)/shard_map/stage/pallas_call | solution.py:292
  44.8 2.7 %collective-permute-done.8.refs_4_ = bf16[128,2048]{1,0:T(8,128)(2,1)S(1)} collective-permute-done((bf16[128,2048]{1,0:T(8,128)(2,1)S(1)}, bf16[128,2048]{1,0:T(8,128)(2,1)S(1)}, u32[]{:S(2)}, u32[]{:S(2)}) %collective-permute-start.8) | collective-permute-done | bytes 524320 | tf_op jit(solution)/shard_map/send_b1/ppermute | solution.py:343
  47.7 1.6 %collective-permute-start.12 = (bf16[128,2048]{1,0:T(8,128)(2,1)S(1)}, bf16[128,2048]{1,0:T(8,128)(2,1)S(1)}, u32[]{:S(2)}, u32[]{:S(2)}) collective-permute-start(bf16[128,2048]{1,0:T(8,128)(2,1)S(1)} %collective-permute-done.8.refs_4_), channel_id=1, source_target_pairs={{0,4},{1,5},{2,6},{3,7},{4,8},{5,9},{6,10},{7,11},{8,12},{9,13},{1... | collective-permute-start | bytes 1572872 | tf_op jit(solution)/shard_map/send_f1/ppermute | solution.py:343
  49.3 5.2 %stage.9 = (f32[8,128]{1,0:T(8,128)S(1)}, f32[8,4,128,128]{3,2,1,0:T(8,128)S(1)}, f32[8,8,128,128]{3,2,1,0:T(8,128)S(1)}) custom-call(s32[8,16]{1,0:T(8,128)S(1)} %get-tuple-element.48.refs_0_, bf16[1024,2048]{1,0:T(8,128)(2,1)S(1)} %get-tuple-element.49.refs_1_, bf16[128,2048]{1,0:T(8,128)(2,1)S(1)} %get-tuple-element.58.refs_2_, ...), custom_call_target="tpu_custom_call" | custom-call | flops 1150000000 | bytes 1 | tf_op jit(solution)/shard_map/stage/pallas_call | solution.py:292
  54.5 4.1 %collective-permute-done.6.refs_2_ = bf16[128,2048]{1,0:T(8,128)(2,1)S(1)} collective-permute-done((bf16[128,2048]{1,0:T(8,128)(2,1)S(1)}, bf16[128,2048]{1,0:T(8,128)(2,1)S(1)}, u32[]{:S(2)}, u32[]{:S(2)}) %collective-permute-start.6) | collective-permute-done | bytes 524320 | tf_op jit(solution)/shard_map/send_f0/ppermute | solution.py:343
  58.6 5.7 %collective-permute-start.10 = (bf16[128,2048]{1,0:T(8,128)(2,1)S(1)}, bf16[128,2048]{1,0:T(8,128)(2,1)S(1)}, u32[]{:S(2)}, u32[]{:S(2)}) collective-permute-start(bf16[128,2048]{1,0:T(8,128)(2,1)S(1)} %get-tuple-element.67.refs_3_), channel_id=1, source_target_pairs={{0,12},{1,13},{2,14},{3,15},{4,0},{5,1},{6,2},{7,3},{8,4},{9,5},{1... | collective-permute-start | bytes 1572872 | tf_op jit(solution)/shard_map/send_a1/ppermute | solution.py:343
  64.3 1.5 %collective-permute-start.11 = (bf16[128,2048]{1,0:T(8,128)(2,1)S(1)}, bf16[128,2048]{1,0:T(8,128)(2,1)S(1)}, u32[]{:S(2)}, u32[]{:S(2)}) collective-permute-start(bf16[128,2048]{1,0:T(8,128)(2,1)S(1)} %collective-permute-done.6.refs_2_), channel_id=1, source_target_pairs={{0,2},{1,3},{2,0},{3,1},{4,6},{5,7},{6,4},{7,5},{8,10},{9,11},{10,... | collective-permute-start | bytes 1572872 | tf_op jit(solution)/shard_map/send_yf0/ppermute | solution.py:343
  65.8 3.0 %stage.10 = (f32[8,128]{1,0:T(8,128)S(1)}, f32[8,2,128,128]{3,2,1,0:T(8,128)S(1)}, f32[8,2,128,128]{3,2,1,0:T(8,128)S(1)}) custom-call(s32[8,16]{1,0:T(8,128)S(1)} %get-tuple-element.48.refs_0_, bf16[1024,2048]{1,0:T(8,128)(2,1)S(1)} %get-tuple-element.49.refs_1_, bf16[128,2048]{1,0:T(8,128)(2,1)S(1)} %collective-permute-done.6.refs_2_, ...), custom_call_target="tpu_custom_call" | custom-call | flops 1150000000 | bytes 1 | tf_op jit(solution)/shard_map/stage/pallas_call | solution.py:292
  68.8 0.9 collective-permute-done.13.refs_3_
  69.7 2.0 %collective-permute-done.12.refs_2_ = bf16[128,2048]{1,0:T(8,128)(2,1)S(1)} collective-permute-done((bf16[128,2048]{1,0:T(8,128)(2,1)S(1)}, bf16[128,2048]{1,0:T(8,128)(2,1)S(1)}, u32[]{:S(2)}, u32[]{:S(2)}) %collective-permute-start.12) | collective-permute-done | bytes 524320 | tf_op jit(solution)/shard_map/send_f1/ppermute | solution.py:343
  71.7 15.7 %collective-permute-start.15 = (bf16[128,2048]{1,0:T(8,128)(2,1)S(1)}, bf16[128,2048]{1,0:T(8,128)(2,1)S(1)}, u32[]{:S(2)}, u32[]{:S(2)}) collective-permute-start(bf16[128,2048]{1,0:T(8,128)(2,1)S(1)} %get-tuple-element.74.refs_3_), channel_id=1, source_target_pairs={{0,12},{1,13},{2,14},{3,15},{4,0},{5,1},{6,2},{7,3},{8,4},{9,5},{1... | collective-permute-start | bytes 1572872 | tf_op jit(solution)/shard_map/send_xa1/ppermute | solution.py:343
  87.9 3.0 %stage.11 = (f32[8,128]{1,0:T(8,128)S(1)}, f32[8,2,128,128]{3,2,1,0:T(8,128)S(1)}, f32[8,4,128,128]{3,2,1,0:T(8,128)S(1)}) custom-call(s32[8,16]{1,0:T(8,128)S(1)} %get-tuple-element.48.refs_0_, bf16[1024,2048]{1,0:T(8,128)(2,1)S(1)} %get-tuple-element.49.refs_1_, bf16[128,2048]{1,0:T(8,128)(2,1)S(1)} %collective-permute-done.12.refs_2_, ...), custom_call_target="tpu_custom_call" | custom-call | flops 1150000000 | bytes 1 | tf_op jit(solution)/shard_map/stage/pallas_call | solution.py:292
  91.0 3.0 %stage.12 = (f32[8,128]{1,0:T(8,128)S(1)}, f32[8,2,128,128]{3,2,1,0:T(8,128)S(1)}, f32[8,2,128,128]{3,2,1,0:T(8,128)S(1)}) custom-call(s32[8,16]{1,0:T(8,128)S(1)} %get-tuple-element.48.refs_0_, bf16[1024,2048]{1,0:T(8,128)(2,1)S(1)} %get-tuple-element.49.refs_1_, bf16[128,2048]{1,0:T(8,128)(2,1)S(1)} %collective-permute-done.10.refs_2_, ...), custom_call_target="tpu_custom_call" | custom-call | flops 1150000000 | bytes 1 | tf_op jit(solution)/shard_map/stage/pallas_call | solution.py:292
  95.1 2.9 %stage.13 = (f32[8,128]{1,0:T(8,128)S(1)}, f32[8,8,128,128]{3,2,1,0:T(8,128)}) custom-call(s32[8,16]{1,0:T(8,128)S(1)} %get-tuple-element.48.refs_0_, f32[8,4,128,128]{3,2,1,0:T(8,128)S(1)} %get-tuple-element.57.refs_1_, f32[8,8,128,128]{3,2,1,0:T(8,128)S(1)} %collective-permute-done.17.refs_2_.refs_4_, ...), custom_call_target="tpu_custom_call" | custom-call | flops 1150000000 | bytes 1 | tf_op jit(solution)/shard_map/stage/pallas_call | solution.py:292
  98.6 2.3 %stage.14 = (f32[8,128]{1,0:T(8,128)}, f32[8,2,128,128]{3,2,1,0:T(8,128)S(1)}) custom-call(s32[8,16]{1,0:T(8,128)S(1)} %get-tuple-element.48.refs_0_, bf16[1024,2048]{1,0:T(8,128)(2,1)S(1)} %get-tuple-element.49.refs_1_, bf16[128,2048]{1,0:T(8,128)(2,1)S(1)} %collective-permute-done.15.refs_2_, bf16[128,2048]{1,0:T(8,128)(2,1)S(1)} %collective-permute-done.16.refs_3_, ...), custom_call_target="tpu_custom_call" | custom-call | flops 13799999488 | bytes 1 | tf_op jit(solution)/shard_map/stage/pallas_call | solution.py:292
  100.9 3.7 %stage.15 = (f32[8,128]{1,0:T(8,128)}, f32[8,8,128,128]{3,2,1,0:T(8,128)}) custom-call(s32[8,16]{1,0:T(8,128)S(1)} %get-tuple-element.48.refs_0_, f32[8,4,128,128]{3,2,1,0:T(8,128)S(1)} %get-tuple-element.57.refs_1_, f32[8,2,128,128]{3,2,1,0:T(8,128)S(1)} %collective-permute-done.14.refs_2_, ...), custom_call_target="tpu_custom_call", output_to_operand_aliasing={{1}: (10, {})} | custom-call | flops 1150000000 | bytes 1 | tf_op jit(solution)/shard_map/stage/pallas_call | solution.py:292
  (34 shorter events, 4.4 us)
Async XLA Ops:
  0.0 24.0 %collective-permute-start.1 = (bf16[1024,4096]{1,0:T(8,128)(2,1)}, bf16[1024,4096]{1,0:T(8,128)(2,1)}, u32[]{:S(2)}, u32[]{:S(2)}) collective-permute-start(bf16[1024,4096]{1,0:T(8,128)(2,1)} %train.1), channel_id=1, source_target_pairs={{0,1},{1,0},{2,3},{3,2},{4,5},{5,4},{6,7},{7,6},{8,9},{9,8},{10,11... | collective-permute-start | bytes 25165832 | tf_op jit(solution)/shard_map/send_train/ppermute | solution.py:343
  1.7 12.3 %collective-permute-start = (bf16[128,2048]{1,0:T(8,128)(2,1)S(1)}, bf16[128,2048]{1,0:T(8,128)(2,1)S(1)}, u32[]{:S(2)}, u32[]{:S(2)}) collective-permute-start(bf16[128,2048]{1,0:T(8,128)(2,1)S(1)} %get-tuple-element.90), channel_id=1, source_target_pairs={{0,1},{1,0},{2,3},{3,2},{4,5},{5,4},{6,7},{7,6},{8,9},{9,8},{10,11... | collective-permute-start | bytes 1572872 | tf_op jit(solution)/shard_map/send_h1/ppermute | solution.py:343
  1.9 21.4 %collective-permute-start.3 = (bf16[128,2048]{1,0:T(8,128)(2,1)S(1)}, bf16[128,2048]{1,0:T(8,128)(2,1)S(1)}, u32[]{:S(2)}, u32[]{:S(2)}) collective-permute-start(bf16[128,2048]{1,0:T(8,128)(2,1)S(1)} %get-tuple-element.91.x0), channel_id=1, source_target_pairs={{0,2},{1,3},{2,0},{3,1},{4,6},{5,7},{6,4},{7,5},{8,10},{9,11},{10,... | collective-permute-start | bytes 1572872 | tf_op jit(solution)/shard_map/send_y0/ppermute | solution.py:343
  4.8 18.5 %collective-permute-start.2 = (bf16[128,2048]{1,0:T(8,128)(2,1)S(1)}, bf16[128,2048]{1,0:T(8,128)(2,1)S(1)}, u32[]{:S(2)}, u32[]{:S(2)}) collective-permute-start(bf16[128,2048]{1,0:T(8,128)(2,1)S(1)} %get-tuple-element.91.x0), channel_id=1, source_target_pairs={{0,12},{1,13},{2,14},{3,15},{4,0},{5,1},{6,2},{7,3},{8,4},{9,5},{1... | collective-permute-start | bytes 1572872 | tf_op jit(solution)/shard_map/send_a0/ppermute | solution.py:343
  8.4 24.5 %collective-permute-start.4 = (bf16[128,2048]{1,0:T(8,128)(2,1)S(1)}, bf16[128,2048]{1,0:T(8,128)(2,1)S(1)}, u32[]{:S(2)}, u32[]{:S(2)}) collective-permute-start(bf16[128,2048]{1,0:T(8,128)(2,1)S(1)} %get-tuple-element.91.x0), channel_id=1, source_target_pairs={{0,4},{1,5},{2,6},{3,7},{4,8},{5,9},{6,10},{7,11},{8,12},{9,13},{1... | collective-permute-start | bytes 1572872 | tf_op jit(solution)/shard_map/send_b0/ppermute | solution.py:343
  14.0 18.9 %collective-permute-start.5 = (bf16[128,2048]{1,0:T(8,128)(2,1)S(1)}, bf16[128,2048]{1,0:T(8,128)(2,1)S(1)}, u32[]{:S(2)}, u32[]{:S(2)}) collective-permute-start(bf16[128,2048]{1,0:T(8,128)(2,1)S(1)} %collective-permute-done.x1), channel_id=1, source_target_pairs={{0,2},{1,3},{2,0},{3,1},{4,6},{5,7},{6,4},{7,5},{8,10},{9,11},{10,... | collective-permute-start | bytes 1572872 | tf_op jit(solution)/shard_map/send_y1/ppermute | solution.py:343
  16.9 0.9 copy-start.1
  17.8 0.9 copy-start.2
  18.7 0.7 copy-start.3
  19.4 0.7 copy-start.4
  30.7 16.7 %collective-permute-start.8 = (bf16[128,2048]{1,0:T(8,128)(2,1)S(1)}, bf16[128,2048]{1,0:T(8,128)(2,1)S(1)}, u32[]{:S(2)}, u32[]{:S(2)}) collective-permute-start(bf16[128,2048]{1,0:T(8,128)(2,1)S(1)} %get-tuple-element.67.refs_3_), channel_id=1, source_target_pairs={{0,4},{1,5},{2,6},{3,7},{4,8},{5,9},{6,10},{7,11},{8,12},{9,13},{1... | collective-permute-start | bytes 1572872 | tf_op jit(solution)/shard_map/send_b1/ppermute | solution.py:343
  32.4 15.1 %collective-permute-start.9 = (bf16[128,2048]{1,0:T(8,128)(2,1)S(1)}, bf16[128,2048]{1,0:T(8,128)(2,1)S(1)}, u32[]{:S(2)}, u32[]{:S(2)}) collective-permute-start(bf16[128,2048]{1,0:T(8,128)(2,1)S(1)} %get-tuple-element.63.refs_4_), channel_id=1, source_target_pairs={{0,2},{1,3},{2,0},{3,1},{4,6},{5,7},{6,4},{7,5},{8,10},{9,11},{10,... | collective-permute-start | bytes 1572872 | tf_op jit(solution)/shard_map/send_ya0/ppermute | solution.py:343
  33.6 25.0 %collective-permute-start.6 = (bf16[128,2048]{1,0:T(8,128)(2,1)S(1)}, bf16[128,2048]{1,0:T(8,128)(2,1)S(1)}, u32[]{:S(2)}, u32[]{:S(2)}) collective-permute-start(bf16[128,2048]{1,0:T(8,128)(2,1)S(1)} %get-tuple-element.63.refs_4_), channel_id=1, source_target_pairs={{0,12},{1,13},{2,14},{3,15},{4,0},{5,1},{6,2},{7,3},{8,4},{9,5},{1... | collective-permute-start | bytes 1572872 | tf_op jit(solution)/shard_map/send_f0/ppermute | solution.py:343
  35.8 22.8 %collective-permute-start.7 = (bf16[128,2048]{1,0:T(8,128)(2,1)S(1)}, bf16[128,2048]{1,0:T(8,128)(2,1)S(1)}, u32[]{:S(2)}, u32[]{:S(2)}) collective-permute-start(bf16[128,2048]{1,0:T(8,128)(2,1)S(1)} %get-tuple-element.58.refs_2_), channel_id=1, source_target_pairs={{0,2},{1,3},{2,0},{3,1},{4,6},{5,7},{6,4},{7,5},{8,10},{9,11},{10,... | collective-permute-start | bytes 1572872 | tf_op jit(solution)/shard_map/send_yb0/ppermute | solution.py:343
  37.4 2.2 %copy-start = (bf16[1024,2048]{1,0:T(8,128)(2,1)S(1)}, bf16[1024,2048]{1,0:T(8,128)(2,1)}, u32[]{:S(2)}) copy-start(bf16[1024,2048]{1,0:T(8,128)(2,1)} %get-tuple-element.56.refs_6_.refs_4_) | copy-start | bytes 12582916
  47.4 22.3 %collective-permute-start.13 = (bf16[128,2048]{1,0:T(8,128)(2,1)S(1)}, bf16[128,2048]{1,0:T(8,128)(2,1)S(1)}, u32[]{:S(2)}, u32[]{:S(2)}) collective-permute-start(bf16[128,2048]{1,0:T(8,128)(2,1)S(1)} %collective-permute-done.8.refs_4_), channel_id=1, source_target_pairs={{0,2},{1,3},{2,0},{3,1},{4,6},{5,7},{6,4},{7,5},{8,10},{9,11},{10,... | collective-permute-start | bytes 1572872 | tf_op jit(solution)/shard_map/send_yb1/ppermute | solution.py:343
  47.7 24.0 %collective-permute-start.12 = (bf16[128,2048]{1,0:T(8,128)(2,1)S(1)}, bf16[128,2048]{1,0:T(8,128)(2,1)S(1)}, u32[]{:S(2)}, u32[]{:S(2)}) collective-permute-start(bf16[128,2048]{1,0:T(8,128)(2,1)S(1)} %collective-permute-done.8.refs_4_), channel_id=1, source_target_pairs={{0,4},{1,5},{2,6},{3,7},{4,8},{5,9},{6,10},{7,11},{8,12},{9,13},{1... | collective-permute-start | bytes 1572872 | tf_op jit(solution)/shard_map/send_f1/ppermute | solution.py:343
  58.6 32.3 %collective-permute-start.10 = (bf16[128,2048]{1,0:T(8,128)(2,1)S(1)}, bf16[128,2048]{1,0:T(8,128)(2,1)S(1)}, u32[]{:S(2)}, u32[]{:S(2)}) collective-permute-start(bf16[128,2048]{1,0:T(8,128)(2,1)S(1)} %get-tuple-element.67.refs_3_), channel_id=1, source_target_pairs={{0,12},{1,13},{2,14},{3,15},{4,0},{5,1},{6,2},{7,3},{8,4},{9,5},{1... | collective-permute-start | bytes 1572872 | tf_op jit(solution)/shard_map/send_a1/ppermute | solution.py:343
  64.3 26.6 %collective-permute-start.11 = (bf16[128,2048]{1,0:T(8,128)(2,1)S(1)}, bf16[128,2048]{1,0:T(8,128)(2,1)S(1)}, u32[]{:S(2)}, u32[]{:S(2)}) collective-permute-start(bf16[128,2048]{1,0:T(8,128)(2,1)S(1)} %collective-permute-done.6.refs_2_), channel_id=1, source_target_pairs={{0,2},{1,3},{2,0},{3,1},{4,6},{5,7},{6,4},{7,5},{8,10},{9,11},{10,... | collective-permute-start | bytes 1572872 | tf_op jit(solution)/shard_map/send_yf0/ppermute | solution.py:343
  65.8 29.3 %collective-permute-start.17 = (f32[8,8,128,128]{3,2,1,0:T(8,128)S(1)}, f32[8,8,128,128]{3,2,1,0:T(8,128)S(1)}, u32[]{:S(2)}, u32[]{:S(2)}) collective-permute-start(f32[8,8,128,128]{3,2,1,0:T(8,128)S(1)} %get-tuple-element.76), channel_id=1, source_target_pairs={{0,1},{1,0},{2,3},{3,2},{4,5},{5,4},{6,7},{7,6},{8,9},{9,8},{10,11... | collective-permute-start | bytes 12582920 | tf_op jit(solution)/shard_map/send_part4/ppermute | solution.py:343
  71.7 26.3 %collective-permute-start.15 = (bf16[128,2048]{1,0:T(8,128)(2,1)S(1)}, bf16[128,2048]{1,0:T(8,128)(2,1)S(1)}, u32[]{:S(2)}, u32[]{:S(2)}) collective-permute-start(bf16[128,2048]{1,0:T(8,128)(2,1)S(1)} %get-tuple-element.74.refs_3_), channel_id=1, source_target_pairs={{0,12},{1,13},{2,14},{3,15},{4,0},{5,1},{6,2},{7,3},{8,4},{9,5},{1... | collective-permute-start | bytes 1572872 | tf_op jit(solution)/shard_map/send_xa1/ppermute | solution.py:343
  87.4 10.6 %collective-permute-start.16 = (bf16[128,2048]{1,0:T(8,128)(2,1)S(1)}, bf16[128,2048]{1,0:T(8,128)(2,1)S(1)}, u32[]{:S(2)}, u32[]{:S(2)}) collective-permute-start(bf16[128,2048]{1,0:T(8,128)(2,1)S(1)} %collective-permute-done.12.refs_2_), channel_id=1, source_target_pairs={{0,2},{1,3},{2,0},{3,1},{4,6},{5,7},{6,4},{7,5},{8,10},{9,11},{10,... | collective-permute-start | bytes 1572872 | tf_op jit(solution)/shard_map/send_yf1/ppermute | solution.py:343
  90.9 4.2 %collective-permute-start.18 = (f32[8,4,128,128]{3,2,1,0:T(8,128)S(1)}, f32[8,4,128,128]{3,2,1,0:T(8,128)S(1)}, u32[]{:S(2)}, u32[]{:S(2)}) collective-permute-start(f32[8,4,128,128]{3,2,1,0:T(8,128)S(1)} %get-tuple-element.80), channel_id=1, source_target_pairs={{0,1},{1,0},{2,3},{3,2},{4,5},{5,4},{6,7},{7,6},{8,9},{9,8},{10,11... | collective-permute-start | bytes 6291464 | tf_op jit(solution)/shard_map/send_part6/ppermute | solution.py:343
  94.0 6.9 %collective-permute-start.14 = (f32[8,2,128,128]{3,2,1,0:T(8,128)S(1)}, f32[8,2,128,128]{3,2,1,0:T(8,128)S(1)}, u32[]{:S(2)}, u32[]{:S(2)}) collective-permute-start(f32[8,2,128,128]{3,2,1,0:T(8,128)S(1)} %get-tuple-element.73), channel_id=1, source_target_pairs={{0,1},{1,0},{2,3},{3,2},{4,5},{5,4},{6,7},{7,6},{8,9},{9,8},{10,11... | collective-permute-start | bytes 3145736 | tf_op jit(solution)/shard_map/send_part7/ppermute | solution.py:343
  98.0 2.9 %collective-permute-start.19 = (bf16[128,2048]{1,0:T(8,128)(2,1)S(1)}, bf16[128,2048]{1,0:T(8,128)(2,1)S(1)}, u32[]{:S(2)}, u32[]{:S(2)}) collective-permute-start(bf16[128,2048]{1,0:T(8,128)(2,1)S(1)} %collective-permute-done.15.refs_2_), channel_id=1, source_target_pairs={{0,1},{1,0},{2,3},{3,2},{4,5},{5,4},{6,7},{7,6},{8,9},{9,8},{10,11... | collective-permute-start | bytes 1572872 | tf_op jit(solution)/shard_map/send_cxa1/ppermute | solution.py:343
  98.2 2.7 %collective-permute-start.20 = (bf16[128,2048]{1,0:T(8,128)(2,1)S(1)}, bf16[128,2048]{1,0:T(8,128)(2,1)S(1)}, u32[]{:S(2)}, u32[]{:S(2)}) collective-permute-start(bf16[128,2048]{1,0:T(8,128)(2,1)S(1)} %collective-permute-done.16.refs_3_), channel_id=1, source_target_pairs={{0,1},{1,0},{2,3},{3,2},{4,5},{5,4},{6,7},{7,6},{8,9},{9,8},{10,11... | collective-permute-start | bytes 1572872 | tf_op jit(solution)/shard_map/send_cyf1/ppermute | solution.py:343

commit v4 on v3

--- a/solution.py
+++ b/solution.py
@@ -367,6 +367,7 @@
     low_half, high_half = query_grads[:, :half], query_grads[:, half:]
     raw = {"h0": jnp.where(core == 0, low_half, high_half)}
     raw["h1"] = send(jnp.where(core == 0, high_half, low_half), twin, "h1")
+    raw["h1"], train_later = lax.optimization_barrier((raw["h1"], train_grads))
     for step in plan[:2]:
         for name, source, perm in step:
             raw[name] = send(raw[source], perm, name)
@@ -374,7 +375,7 @@
         layer_slot, pair_query, in_factor, out_factor, raw["h0"], raw["h1"], 2 * 8
     )
     got = {"h0": own0, "h1": own1}
-    keep, rest, their_train, halves_token = make_halves(train_grads, send(train_grads, twin, "train"))
+    keep, rest, their_train, halves_token = make_halves(train_grads, send(train_later, twin, "train"))
     ours, theirs, open_jobs = {}, {}, list(other_name)
     out, tokens = None, []
 
@@ -384,14 +385,17 @@
             open_jobs.remove(n)
         return [(job[n], ours[n], theirs[other_name[n]]) for n in done]
 
-    held, columns = None, []
+    held, columns, last_send = None, [], None
     for s in range(2, len(plan) + 1):
         names = [name for name, _, _ in plan[s - 2]]
         if s < 4:
             got[names[0]], got[names[1]] = make_ready(raw[names[0]], raw[names[1]], high, low)
-        past = [got[name] for name in names] + (tokens if s > 3 else [halves_token] * (s == 2))
+        past = [got[name] for name in names] + (tokens if s > 3 else [halves_token] * (s == 3))
         if s < len(plan):
             for name, source, perm in plan[s]:
+                if name == "xa1":
+                    last_send = (name, source, perm, past)
+                    continue
                 deps = [v for v in past if v is not got[source]]
                 got[name] = send(after(got[source], *deps), perm, name)
         if s not in work:
@@ -400,6 +404,9 @@
         products = [(keep, pieces, (), None), (their_train, pieces, (), held)]
         token, _, (mine, held) = stage(table, [], products, None, slots, cost[s], tokens)
         tokens = [token]
+        if s == len(plan) - 1:
+            name, source, perm, past = last_send
+            got[name] = send(after(got[source], *past, token), perm, name)
         ours.update({n: (mine, i) for i, n in enumerate(work[s])})
         columns += work[s]
         if s in exchange:

time: 105 us -> 96.2 us (0.916)
  starting transfers between devices: 42.5 us -> 21 us
  waiting for transfers between devices: 15.9 us -> 28.6 us
    ppermute x21, starting transfers between devices: 42.5 us -> 21 us  [send(): return lax.ppermute(x, 'rows', perm)]
    ppermute x21, waiting for transfers between devices: 15.9 us -> 28.6 us  [send(): return lax.ppermute(x, 'rows', perm)]
  transfers between devices with their start and end apart: 21 -> 21, of which waited for: 6 -> 11; matrix products, arithmetic and copies ran while one was open for 1% -> 0% of each run, Pallas kernels for 34% -> 37%
where the time goes in v4:
time: 96.2 us; the launch traced here: 96 us
  Pallas kernels  39.4 us (41%)
  waiting for transfers between devices  28.6 us (30%)
  starting transfers between devices  21 us (22%)
  local copies, waits for them, and re-layouts  5.34 us (6%)
  other arithmetic  1.27 us (1%)
    ppermute x21, waiting for transfers between devices, send(): return lax.ppermute(x, 'rows', perm)  28.6 us
    pallas_call x8, Pallas kernels, stage(): pl.pallas_call(body, out_shape=shapes, in_specs=specs, out_specs=out_spec...  28.1 us
    ppermute x21, starting transfers between devices, send(): return lax.ppermute(x, 'rows', perm)  21 us
    pallas_call x1, Pallas kernels, make_halves(): pl.pallas_call(halves_kernel, out_shape=[side] * 3 + [jax.ShapeDtypeStruc...  6.71 us
    unnamed x10, local copies, waits for them, and re-layouts  5.34 us
    pallas_call x1, Pallas kernels, prepare(): pl.pallas_call(functools.partial(prepare_kernel, layers), out_shape=[fact...  3.21 us
  transfers between devices with their start and end apart: 21, of which 11 were waited for; matrix products, arithmetic and copies ran while one was open for 0% of the time, Pallas kernels for 37%

profile of v4, /device:TPU:0, one launch (start us, length us, event | category | flops | bytes accessed | tf_op | source)
XLA Modules:
  0.0 96.0 jit_solution(15838839741496573142)
XLA Ops:
  0.0 1.3 %broadcast_select_fusion = (bf16[128,2048]{1,0:T(8,128)(2,1)S(1)}, bf16[128,2048]{1,0:T(8,128)(2,1)S(1)}) fusion(pred[]{:T(512)S(6)} %eq.6, bf16[128,4096]{1,0:T(8,128)(2,1)} %param.7), kind=kLoop, calls=%fused_computation | loop fusion | flops 524288 | bytes 2097153 | tf_op jit(solution)/shard_map/jit(_where)/select_n | solution.py:369
  1.8 1.5 %collective-permute-done.x1 = bf16[128,2048]{1,0:T(8,128)(2,1)S(1)} collective-permute-done((bf16[128,2048]{1,0:T(8,128)(2,1)S(1)}, bf16[128,2048]{1,0:T(8,128)(2,1)S(1)}, u32[]{:S(2)}, u32[]{:S(2)}) %collective-permute-start) | collective-permute-done | bytes 524320 | tf_op jit(solution)/shard_map/send_h1/ppermute | solution.py:343
  3.7 4.7 %collective-permute-start.2 = (bf16[128,2048]{1,0:T(8,128)(2,1)S(1)}, bf16[128,2048]{1,0:T(8,128)(2,1)S(1)}, u32[]{:S(2)}, u32[]{:S(2)}) collective-permute-start(bf16[128,2048]{1,0:T(8,128)(2,1)S(1)} %get-tuple-element.95.x0), channel_id=1, source_target_pairs={{0,12},{1,13},{2,14},{3,15},{4,0},{5,1},{6,2},{7,3},{8,4},{9,5},{1... | collective-permute-start | bytes 1572872 | tf_op jit(solution)/shard_map/send_a0/ppermute | solution.py:343
  8.5 1.5 %collective-permute-start.3 = (bf16[128,2048]{1,0:T(8,128)(2,1)S(1)}, bf16[128,2048]{1,0:T(8,128)(2,1)S(1)}, u32[]{:S(2)}, u32[]{:S(2)}) collective-permute-start(bf16[128,2048]{1,0:T(8,128)(2,1)S(1)} %get-tuple-element.95.x0), channel_id=1, source_target_pairs={{0,2},{1,3},{2,0},{3,1},{4,6},{5,7},{6,4},{7,5},{8,10},{9,11},{10,... | collective-permute-start | bytes 1572872 | tf_op jit(solution)/shard_map/send_y0/ppermute | solution.py:343
  13.6 3.2 %prepare.1 = (bf16[8,256,256]{2,1,0:T(8,128)(2,1)S(1)}, bf16[8,256,256]{2,1,0:T(8,128)(2,1)S(1)}, bf16[128,2048]{1,0:T(8,128)(2,1)S(1)}, bf16[128,2048]{1,0:T(8,128)(2,1)S(1)}, s32[8,16]{1,0:T(8,128)S(1)}) custom-call(s32[16]{0:T(128)S(1)} %copy-done.4, s32[8,8]{1,0:T(8,128)S(1)} %copy-done.3, f32[256,16]{1,0:T(8,128)S(1)} %bitcast.2, ...), custom_call_target="tpu_custom_call" | custom-call | flops 1000000000 | bytes 1 | tf_op jit(solution)/shard_map/prepare/pallas_call | solution.py:129
  16.9 3.9 %collective-permute-done.2.x0 = bf16[128,2048]{1,0:T(8,128)(2,1)S(1)} collective-permute-done((bf16[128,2048]{1,0:T(8,128)(2,1)S(1)}, bf16[128,2048]{1,0:T(8,128)(2,1)S(1)}, u32[]{:S(2)}, u32[]{:S(2)}) %collective-permute-start.2) | collective-permute-done | bytes 524320 | tf_op jit(solution)/shard_map/send_a0/ppermute | solution.py:343
  20.8 2.5 %collective-permute-done.3.x1 = bf16[128,2048]{1,0:T(8,128)(2,1)S(1)} collective-permute-done((bf16[128,2048]{1,0:T(8,128)(2,1)S(1)}, bf16[128,2048]{1,0:T(8,128)(2,1)S(1)}, u32[]{:S(2)}, u32[]{:S(2)}) %collective-permute-start.3) | collective-permute-done | bytes 524320 | tf_op jit(solution)/shard_map/send_y0/ppermute | solution.py:343
  24.0 1.6 %collective-permute-start.9 = (bf16[128,2048]{1,0:T(8,128)(2,1)S(1)}, bf16[128,2048]{1,0:T(8,128)(2,1)S(1)}, u32[]{:S(2)}, u32[]{:S(2)}) collective-permute-start(bf16[128,2048]{1,0:T(8,128)(2,1)S(1)} %get-tuple-element.65.refs_4_), channel_id=1, source_target_pairs={{0,2},{1,3},{2,0},{3,1},{4,6},{5,7},{6,4},{7,5},{8,10},{9,11},{10,... | collective-permute-start | bytes 1572872 | tf_op jit(solution)/shard_map/send_ya0/ppermute | solution.py:343
  25.6 7.2 %collective-permute-done.4.x0 = bf16[128,2048]{1,0:T(8,128)(2,1)S(1)} collective-permute-done((bf16[128,2048]{1,0:T(8,128)(2,1)S(1)}, bf16[128,2048]{1,0:T(8,128)(2,1)S(1)}, u32[]{:S(2)}, u32[]{:S(2)}) %collective-permute-start.4) | collective-permute-done | bytes 524320 | tf_op jit(solution)/shard_map/send_b0/ppermute | solution.py:343
  32.9 1.6 %collective-permute-done.5.x1 = bf16[128,2048]{1,0:T(8,128)(2,1)S(1)} collective-permute-done((bf16[128,2048]{1,0:T(8,128)(2,1)S(1)}, bf16[128,2048]{1,0:T(8,128)(2,1)S(1)}, u32[]{:S(2)}, u32[]{:S(2)}) %collective-permute-start.5) | collective-permute-done | bytes 524320 | tf_op jit(solution)/shard_map/send_y1/ppermute | solution.py:343
  35.2 6.7 %halves.1 = (bf16[1024,2048]{1,0:T(8,128)(2,1)S(1)}, bf16[1024,2048]{1,0:T(8,128)(2,1)S(1)}, bf16[1024,2048]{1,0:T(8,128)(2,1)}, f32[8,128]{1,0:T(8,128)}) custom-call(bf16[1024,4096]{1,0:T(8,128)(2,1)} %train.1, bf16[1024,4096]{1,0:T(8,128)(2,1)} %collective-permute-done.1.twin_train), custom_call_target="tpu_custom_call" | custom-call | flops 1000000000 | bytes 1 | tf_op jit(solution)/shard_map/halves/pallas_call | solution.py:163
  41.9 1.4 %collective-permute-start.6 = (bf16[128,2048]{1,0:T(8,128)(2,1)S(1)}, bf16[128,2048]{1,0:T(8,128)(2,1)S(1)}, u32[]{:S(2)}, u32[]{:S(2)}) collective-permute-start(bf16[128,2048]{1,0:T(8,128)(2,1)S(1)} %get-tuple-element.65.refs_4_), channel_id=1, source_target_pairs={{0,12},{1,13},{2,14},{3,15},{4,0},{5,1},{6,2},{7,3},{8,4},{9,5},{1... | collective-permute-start | bytes 1572872 | tf_op jit(solution)/shard_map/send_f0/ppermute | solution.py:343
  43.4 1.1 %collective-permute-start.7 = (bf16[128,2048]{1,0:T(8,128)(2,1)S(1)}, bf16[128,2048]{1,0:T(8,128)(2,1)S(1)}, u32[]{:S(2)}, u32[]{:S(2)}) collective-permute-start(bf16[128,2048]{1,0:T(8,128)(2,1)S(1)} %get-tuple-element.66.refs_2_), channel_id=1, source_target_pairs={{0,2},{1,3},{2,0},{3,1},{4,6},{5,7},{6,4},{7,5},{8,10},{9,11},{10,... | collective-permute-start | bytes 1572872 | tf_op jit(solution)/shard_map/send_yb0/ppermute | solution.py:343
  44.5 2.2 %copy-done = bf16[1024,2048]{1,0:T(8,128)(2,1)S(1)} copy-done((bf16[1024,2048]{1,0:T(8,128)(2,1)S(1)}, bf16[1024,2048]{1,0:T(8,128)(2,1)}, u32[]{:S(2)}) %copy-start) | copy-done | bytes 4194328
  46.7 5.1 %stage.8 = (f32[8,128]{1,0:T(8,128)S(1)}, f32[8,4,128,128]{3,2,1,0:T(8,128)S(1)}, f32[8,4,128,128]{3,2,1,0:T(8,128)S(1)}) custom-call(s32[8,16]{1,0:T(8,128)S(1)} %get-tuple-element.51.refs_0_, bf16[1024,2048]{1,0:T(8,128)(2,1)S(1)} %get-tuple-element.53.refs_1_, bf16[128,2048]{1,0:T(8,128)(2,1)S(1)} %get-tuple-element.54.refs_2_, ...), custom_call_target="tpu_custom_call" | custom-call | flops 1150000000 | bytes 1 | tf_op jit(solution)/shard_map/stage/pallas_call | solution.py:292
  51.8 1.1 %collective-permute-start.12 = (bf16[128,2048]{1,0:T(8,128)(2,1)S(1)}, bf16[128,2048]{1,0:T(8,128)(2,1)S(1)}, u32[]{:S(2)}, u32[]{:S(2)}) collective-permute-start(bf16[128,2048]{1,0:T(8,128)(2,1)S(1)} %collective-permute-done.8.refs_4_), channel_id=1, source_target_pairs={{0,4},{1,5},{2,6},{3,7},{4,8},{5,9},{6,10},{7,11},{8,12},{9,13},{1... | collective-permute-start | bytes 1572872 | tf_op jit(solution)/shard_map/send_f1/ppermute | solution.py:343
  53.4 5.2 %stage.9 = (f32[8,128]{1,0:T(8,128)S(1)}, f32[8,4,128,128]{3,2,1,0:T(8,128)S(1)}, f32[8,8,128,128]{3,2,1,0:T(8,128)S(1)}) custom-call(s32[8,16]{1,0:T(8,128)S(1)} %get-tuple-element.51.refs_0_, bf16[1024,2048]{1,0:T(8,128)(2,1)S(1)} %get-tuple-element.53.refs_1_, bf16[128,2048]{1,0:T(8,128)(2,1)S(1)} %get-tuple-element.66.refs_2_, ...), custom_call_target="tpu_custom_call" | custom-call | flops 1150000000 | bytes 1 | tf_op jit(solution)/shard_map/stage/pallas_call | solution.py:292
  58.6 3.4 %collective-permute-start.10 = (bf16[128,2048]{1,0:T(8,128)(2,1)S(1)}, bf16[128,2048]{1,0:T(8,128)(2,1)S(1)}, u32[]{:S(2)}, u32[]{:S(2)}) collective-permute-start(bf16[128,2048]{1,0:T(8,128)(2,1)S(1)} %get-tuple-element.71.refs_3_), channel_id=1, source_target_pairs={{0,12},{1,13},{2,14},{3,15},{4,0},{5,1},{6,2},{7,3},{8,4},{9,5},{1... | collective-permute-start | bytes 1572872 | tf_op jit(solution)/shard_map/send_a1/ppermute | solution.py:343
  62.0 1.1 %collective-permute-start.11 = (bf16[128,2048]{1,0:T(8,128)(2,1)S(1)}, bf16[128,2048]{1,0:T(8,128)(2,1)S(1)}, u32[]{:S(2)}, u32[]{:S(2)}) collective-permute-start(bf16[128,2048]{1,0:T(8,128)(2,1)S(1)} %collective-permute-done.6.refs_2_), channel_id=1, source_target_pairs={{0,2},{1,3},{2,0},{3,1},{4,6},{5,7},{6,4},{7,5},{8,10},{9,11},{10,... | collective-permute-start | bytes 1572872 | tf_op jit(solution)/shard_map/send_yf0/ppermute | solution.py:343
  63.2 3.0 %stage.10 = (f32[8,128]{1,0:T(8,128)S(1)}, f32[8,2,128,128]{3,2,1,0:T(8,128)S(1)}, f32[8,2,128,128]{3,2,1,0:T(8,128)S(1)}) custom-call(s32[8,16]{1,0:T(8,128)S(1)} %get-tuple-element.51.refs_0_, bf16[1024,2048]{1,0:T(8,128)(2,1)S(1)} %get-tuple-element.53.refs_1_, bf16[128,2048]{1,0:T(8,128)(2,1)S(1)} %collective-permute-done.6.refs_2_, ...), custom_call_target="tpu_custom_call" | custom-call | flops 1150000000 | bytes 1 | tf_op jit(solution)/shard_map/stage/pallas_call | solution.py:292
  66.2 2.4 %collective-permute-done.12.refs_2_ = bf16[128,2048]{1,0:T(8,128)(2,1)S(1)} collective-permute-done((bf16[128,2048]{1,0:T(8,128)(2,1)S(1)}, bf16[128,2048]{1,0:T(8,128)(2,1)S(1)}, u32[]{:S(2)}, u32[]{:S(2)}) %collective-permute-start.12) | collective-permute-done | bytes 524320 | tf_op jit(solution)/shard_map/send_f1/ppermute | solution.py:343
  69.4 3.0 %stage.11 = (f32[8,128]{1,0:T(8,128)S(1)}, f32[8,2,128,128]{3,2,1,0:T(8,128)S(1)}, f32[8,4,128,128]{3,2,1,0:T(8,128)S(1)}) custom-call(s32[8,16]{1,0:T(8,128)S(1)} %get-tuple-element.51.refs_0_, bf16[1024,2048]{1,0:T(8,128)(2,1)S(1)} %get-tuple-element.53.refs_1_, bf16[128,2048]{1,0:T(8,128)(2,1)S(1)} %collective-permute-done.12.refs_2_, ...), custom_call_target="tpu_custom_call" | custom-call | flops 1150000000 | bytes 1 | tf_op jit(solution)/shard_map/stage/pallas_call | solution.py:292
  72.5 1.8 %collective-permute-start.15 = (bf16[128,2048]{1,0:T(8,128)(2,1)S(1)}, bf16[128,2048]{1,0:T(8,128)(2,1)S(1)}, u32[]{:S(2)}, u32[]{:S(2)}) collective-permute-start(bf16[128,2048]{1,0:T(8,128)(2,1)S(1)} %get-tuple-element.78.refs_3_), channel_id=1, source_target_pairs={{0,12},{1,13},{2,14},{3,15},{4,0},{5,1},{6,2},{7,3},{8,4},{9,5},{1... | collective-permute-start | bytes 1572872 | tf_op jit(solution)/shard_map/send_xa1/ppermute | solution.py:343
  74.3 1.1 %collective-permute-start.16 = (bf16[128,2048]{1,0:T(8,128)(2,1)S(1)}, bf16[128,2048]{1,0:T(8,128)(2,1)S(1)}, u32[]{:S(2)}, u32[]{:S(2)}) collective-permute-start(bf16[128,2048]{1,0:T(8,128)(2,1)S(1)} %collective-permute-done.12.refs_2_), channel_id=1, source_target_pairs={{0,2},{1,3},{2,0},{3,1},{4,6},{5,7},{6,4},{7,5},{8,10},{9,11},{10,... | collective-permute-start | bytes 1572872 | tf_op jit(solution)/shard_map/send_yf1/ppermute | solution.py:343
  75.4 2.8 %collective-permute-done.10.refs_2_ = bf16[128,2048]{1,0:T(8,128)(2,1)S(1)} collective-permute-done((bf16[128,2048]{1,0:T(8,128)(2,1)S(1)}, bf16[128,2048]{1,0:T(8,128)(2,1)S(1)}, u32[]{:S(2)}, u32[]{:S(2)}) %collective-permute-start.10) | collective-permute-done | bytes 524320 | tf_op jit(solution)/shard_map/send_a1/ppermute | solution.py:343
  78.2 2.4 %collective-permute-done.11.refs_3_ = bf16[128,2048]{1,0:T(8,128)(2,1)S(1)} collective-permute-done((bf16[128,2048]{1,0:T(8,128)(2,1)S(1)}, bf16[128,2048]{1,0:T(8,128)(2,1)S(1)}, u32[]{:S(2)}, u32[]{:S(2)}) %collective-permute-start.11) | collective-permute-done | bytes 524320 | tf_op jit(solution)/shard_map/send_yf0/ppermute | solution.py:343
  80.6 3.0 %stage.12 = (f32[8,128]{1,0:T(8,128)S(1)}, f32[8,2,128,128]{3,2,1,0:T(8,128)S(1)}, f32[8,2,128,128]{3,2,1,0:T(8,128)S(1)}) custom-call(s32[8,16]{1,0:T(8,128)S(1)} %get-tuple-element.51.refs_0_, bf16[1024,2048]{1,0:T(8,128)(2,1)S(1)} %get-tuple-element.53.refs_1_, bf16[128,2048]{1,0:T(8,128)(2,1)S(1)} %collective-permute-done.10.refs_2_, ...), custom_call_target="tpu_custom_call" | custom-call | flops 1150000000 | bytes 1 | tf_op jit(solution)/shard_map/stage/pallas_call | solution.py:292
  83.7 2.8 %stage.13 = (f32[8,128]{1,0:T(8,128)S(1)}, f32[8,8,128,128]{3,2,1,0:T(8,128)}) custom-call(s32[8,16]{1,0:T(8,128)S(1)} %get-tuple-element.51.refs_0_, f32[8,4,128,128]{3,2,1,0:T(8,128)S(1)} %get-tuple-element.61.refs_1_, f32[8,8,128,128]{3,2,1,0:T(8,128)S(1)} %collective-permute-done.17.refs_2_.refs_4_, ...), custom_call_target="tpu_custom_call" | custom-call | flops 1150000000 | bytes 1 | tf_op jit(solution)/shard_map/stage/pallas_call | solution.py:292
  86.5 2.0 %collective-permute-done.15.refs_2_ = bf16[128,2048]{1,0:T(8,128)(2,1)S(1)} collective-permute-done((bf16[128,2048]{1,0:T(8,128)(2,1)S(1)}, bf16[128,2048]{1,0:T(8,128)(2,1)S(1)}, u32[]{:S(2)}, u32[]{:S(2)}) %collective-permute-start.15) | collective-permute-done | bytes 524320 | tf_op jit(solution)/shard_map/send_xa1/ppermute | solution.py:343
  88.5 1.3 %collective-permute-done.16.refs_3_ = bf16[128,2048]{1,0:T(8,128)(2,1)S(1)} collective-permute-done((bf16[128,2048]{1,0:T(8,128)(2,1)S(1)}, bf16[128,2048]{1,0:T(8,128)(2,1)S(1)}, u32[]{:S(2)}, u32[]{:S(2)}) %collective-permute-start.16) | collective-permute-done | bytes 524320 | tf_op jit(solution)/shard_map/send_yf1/ppermute | solution.py:343
  89.8 2.3 %stage.14 = (f32[8,128]{1,0:T(8,128)}, f32[8,2,128,128]{3,2,1,0:T(8,128)S(1)}) custom-call(s32[8,16]{1,0:T(8,128)S(1)} %get-tuple-element.51.refs_0_, bf16[1024,2048]{1,0:T(8,128)(2,1)S(1)} %get-tuple-element.53.refs_1_, bf16[128,2048]{1,0:T(8,128)(2,1)S(1)} %collective-permute-done.15.refs_2_, bf16[128,2048]{1,0:T(8,128)(2,1)S(1)} %collective-permute-done.16.refs_3_, ...), custom_call_target="tpu_custom_call" | custom-call | flops 13799999488 | bytes 1 | tf_op jit(solution)/shard_map/stage/pallas_call | solution.py:292
  92.1 3.7 %stage.15 = (f32[8,128]{1,0:T(8,128)}, f32[8,8,128,128]{3,2,1,0:T(8,128)}) custom-call(s32[8,16]{1,0:T(8,128)S(1)} %get-tuple-element.51.refs_0_, f32[8,4,128,128]{3,2,1,0:T(8,128)S(1)} %get-tuple-element.61.refs_1_, f32[8,2,128,128]{3,2,1,0:T(8,128)S(1)} %collective-permute-done.14.refs_2_, ...), custom_call_target="tpu_custom_call", output_to_operand_aliasing={{1}: (10, {})} | custom-call | flops 1150000000 | bytes 1 | tf_op jit(solution)/shard_map/stage/pallas_call | solution.py:292
  (34 shorter events, 7.5 us)
Async XLA Ops:
  1.3 2.1 %collective-permute-start = (bf16[128,2048]{1,0:T(8,128)(2,1)S(1)}, bf16[128,2048]{1,0:T(8,128)(2,1)S(1)}, u32[]{:S(2)}, u32[]{:S(2)}) collective-permute-start(bf16[128,2048]{1,0:T(8,128)(2,1)S(1)} %get-tuple-element.94), channel_id=1, source_target_pairs={{0,1},{1,0},{2,3},{3,2},{4,5},{5,4},{6,7},{7,6},{8,9},{9,8},{10,11... | collective-permute-start | bytes 1572872 | tf_op jit(solution)/shard_map/send_h1/ppermute | solution.py:343
  3.3 31.9 %collective-permute-start.1 = (bf16[1024,4096]{1,0:T(8,128)(2,1)}, bf16[1024,4096]{1,0:T(8,128)(2,1)}, u32[]{:S(2)}, u32[]{:S(2)}) collective-permute-start(bf16[1024,4096]{1,0:T(8,128)(2,1)} %train.1), channel_id=1, source_target_pairs={{0,1},{1,0},{2,3},{3,2},{4,5},{5,4},{6,7},{7,6},{8,9},{9,8},{10,11... | collective-permute-start | bytes 25165832 | tf_op jit(solution)/shard_map/send_train/ppermute | solution.py:343
  3.7 17.1 %collective-permute-start.2 = (bf16[128,2048]{1,0:T(8,128)(2,1)S(1)}, bf16[128,2048]{1,0:T(8,128)(2,1)S(1)}, u32[]{:S(2)}, u32[]{:S(2)}) collective-permute-start(bf16[128,2048]{1,0:T(8,128)(2,1)S(1)} %get-tuple-element.95.x0), channel_id=1, source_target_pairs={{0,12},{1,13},{2,14},{3,15},{4,0},{5,1},{6,2},{7,3},{8,4},{9,5},{1... | collective-permute-start | bytes 1572872 | tf_op jit(solution)/shard_map/send_a0/ppermute | solution.py:343
  8.5 14.8 %collective-permute-start.3 = (bf16[128,2048]{1,0:T(8,128)(2,1)S(1)}, bf16[128,2048]{1,0:T(8,128)(2,1)S(1)}, u32[]{:S(2)}, u32[]{:S(2)}) collective-permute-start(bf16[128,2048]{1,0:T(8,128)(2,1)S(1)} %get-tuple-element.95.x0), channel_id=1, source_target_pairs={{0,2},{1,3},{2,0},{3,1},{4,6},{5,7},{6,4},{7,5},{8,10},{9,11},{10,... | collective-permute-start | bytes 1572872 | tf_op jit(solution)/shard_map/send_y0/ppermute | solution.py:343
  10.0 22.9 %collective-permute-start.4 = (bf16[128,2048]{1,0:T(8,128)(2,1)S(1)}, bf16[128,2048]{1,0:T(8,128)(2,1)S(1)}, u32[]{:S(2)}, u32[]{:S(2)}) collective-permute-start(bf16[128,2048]{1,0:T(8,128)(2,1)S(1)} %get-tuple-element.95.x0), channel_id=1, source_target_pairs={{0,4},{1,5},{2,6},{3,7},{4,8},{5,9},{6,10},{7,11},{8,12},{9,13},{1... | collective-permute-start | bytes 1572872 | tf_op jit(solution)/shard_map/send_b0/ppermute | solution.py:343
  10.0 24.5 %collective-permute-start.5 = (bf16[128,2048]{1,0:T(8,128)(2,1)S(1)}, bf16[128,2048]{1,0:T(8,128)(2,1)S(1)}, u32[]{:S(2)}, u32[]{:S(2)}) collective-permute-start(bf16[128,2048]{1,0:T(8,128)(2,1)S(1)} %collective-permute-done.x1), channel_id=1, source_target_pairs={{0,2},{1,3},{2,0},{3,1},{4,6},{5,7},{6,4},{7,5},{8,10},{9,11},{10,... | collective-permute-start | bytes 1572872 | tf_op jit(solution)/shard_map/send_y1/ppermute | solution.py:343
  10.5 0.9 copy-start.1
  11.4 0.9 copy-start.2
  12.3 0.7 copy-start.3
  13.0 0.7 copy-start.4
  24.0 27.8 %collective-permute-start.8 = (bf16[128,2048]{1,0:T(8,128)(2,1)S(1)}, bf16[128,2048]{1,0:T(8,128)(2,1)S(1)}, u32[]{:S(2)}, u32[]{:S(2)}) collective-permute-start(bf16[128,2048]{1,0:T(8,128)(2,1)S(1)} %get-tuple-element.71.refs_3_), channel_id=1, source_target_pairs={{0,4},{1,5},{2,6},{3,7},{4,8},{5,9},{6,10},{7,11},{8,12},{9,13},{1... | collective-permute-start | bytes 1572872 | tf_op jit(solution)/shard_map/send_b1/ppermute | solution.py:343
  24.0 27.8 %collective-permute-start.9 = (bf16[128,2048]{1,0:T(8,128)(2,1)S(1)}, bf16[128,2048]{1,0:T(8,128)(2,1)S(1)}, u32[]{:S(2)}, u32[]{:S(2)}) collective-permute-start(bf16[128,2048]{1,0:T(8,128)(2,1)S(1)} %get-tuple-element.65.refs_4_), channel_id=1, source_target_pairs={{0,2},{1,3},{2,0},{3,1},{4,6},{5,7},{6,4},{7,5},{8,10},{9,11},{10,... | collective-permute-start | bytes 1572872 | tf_op jit(solution)/shard_map/send_ya0/ppermute | solution.py:343
  41.9 16.7 %collective-permute-start.6 = (bf16[128,2048]{1,0:T(8,128)(2,1)S(1)}, bf16[128,2048]{1,0:T(8,128)(2,1)S(1)}, u32[]{:S(2)}, u32[]{:S(2)}) collective-permute-start(bf16[128,2048]{1,0:T(8,128)(2,1)S(1)} %get-tuple-element.65.refs_4_), channel_id=1, source_target_pairs={{0,12},{1,13},{2,14},{3,15},{4,0},{5,1},{6,2},{7,3},{8,4},{9,5},{1... | collective-permute-start | bytes 1572872 | tf_op jit(solution)/shard_map/send_f0/ppermute | solution.py:343
  43.4 15.3 %collective-permute-start.7 = (bf16[128,2048]{1,0:T(8,128)(2,1)S(1)}, bf16[128,2048]{1,0:T(8,128)(2,1)S(1)}, u32[]{:S(2)}, u32[]{:S(2)}) collective-permute-start(bf16[128,2048]{1,0:T(8,128)(2,1)S(1)} %get-tuple-element.66.refs_2_), channel_id=1, source_target_pairs={{0,2},{1,3},{2,0},{3,1},{4,6},{5,7},{6,4},{7,5},{8,10},{9,11},{10,... | collective-permute-start | bytes 1572872 | tf_op jit(solution)/shard_map/send_yb0/ppermute | solution.py:343
  44.5 2.2 %copy-start = (bf16[1024,2048]{1,0:T(8,128)(2,1)S(1)}, bf16[1024,2048]{1,0:T(8,128)(2,1)}, u32[]{:S(2)}) copy-start(bf16[1024,2048]{1,0:T(8,128)(2,1)} %get-tuple-element.60.refs_6_.refs_4_) | copy-start | bytes 12582916
  51.8 16.8 %collective-permute-start.12 = (bf16[128,2048]{1,0:T(8,128)(2,1)S(1)}, bf16[128,2048]{1,0:T(8,128)(2,1)S(1)}, u32[]{:S(2)}, u32[]{:S(2)}) collective-permute-start(bf16[128,2048]{1,0:T(8,128)(2,1)S(1)} %collective-permute-done.8.refs_4_), channel_id=1, source_target_pairs={{0,4},{1,5},{2,6},{3,7},{4,8},{5,9},{6,10},{7,11},{8,12},{9,13},{1... | collective-permute-start | bytes 1572872 | tf_op jit(solution)/shard_map/send_f1/ppermute | solution.py:343
  52.9 16.5 %collective-permute-start.13 = (bf16[128,2048]{1,0:T(8,128)(2,1)S(1)}, bf16[128,2048]{1,0:T(8,128)(2,1)S(1)}, u32[]{:S(2)}, u32[]{:S(2)}) collective-permute-start(bf16[128,2048]{1,0:T(8,128)(2,1)S(1)} %collective-permute-done.8.refs_4_), channel_id=1, source_target_pairs={{0,2},{1,3},{2,0},{3,1},{4,6},{5,7},{6,4},{7,5},{8,10},{9,11},{10,... | collective-permute-start | bytes 1572872 | tf_op jit(solution)/shard_map/send_yb1/ppermute | solution.py:343
  58.6 19.6 %collective-permute-start.10 = (bf16[128,2048]{1,0:T(8,128)(2,1)S(1)}, bf16[128,2048]{1,0:T(8,128)(2,1)S(1)}, u32[]{:S(2)}, u32[]{:S(2)}) collective-permute-start(bf16[128,2048]{1,0:T(8,128)(2,1)S(1)} %get-tuple-element.71.refs_3_), channel_id=1, source_target_pairs={{0,12},{1,13},{2,14},{3,15},{4,0},{5,1},{6,2},{7,3},{8,4},{9,5},{1... | collective-permute-start | bytes 1572872 | tf_op jit(solution)/shard_map/send_a1/ppermute | solution.py:343
  62.0 18.6 %collective-permute-start.11 = (bf16[128,2048]{1,0:T(8,128)(2,1)S(1)}, bf16[128,2048]{1,0:T(8,128)(2,1)S(1)}, u32[]{:S(2)}, u32[]{:S(2)}) collective-permute-start(bf16[128,2048]{1,0:T(8,128)(2,1)S(1)} %collective-permute-done.6.refs_2_), channel_id=1, source_target_pairs={{0,2},{1,3},{2,0},{3,1},{4,6},{5,7},{6,4},{7,5},{8,10},{9,11},{10,... | collective-permute-start | bytes 1572872 | tf_op jit(solution)/shard_map/send_yf0/ppermute | solution.py:343
  63.2 20.5 %collective-permute-start.17 = (f32[8,8,128,128]{3,2,1,0:T(8,128)S(1)}, f32[8,8,128,128]{3,2,1,0:T(8,128)S(1)}, u32[]{:S(2)}, u32[]{:S(2)}) collective-permute-start(f32[8,8,128,128]{3,2,1,0:T(8,128)S(1)} %get-tuple-element.80), channel_id=1, source_target_pairs={{0,1},{1,0},{2,3},{3,2},{4,5},{5,4},{6,7},{7,6},{8,9},{9,8},{10,11... | collective-permute-start | bytes 12582920 | tf_op jit(solution)/shard_map/send_part4/ppermute | solution.py:343
  72.5 16.0 %collective-permute-start.15 = (bf16[128,2048]{1,0:T(8,128)(2,1)S(1)}, bf16[128,2048]{1,0:T(8,128)(2,1)S(1)}, u32[]{:S(2)}, u32[]{:S(2)}) collective-permute-start(bf16[128,2048]{1,0:T(8,128)(2,1)S(1)} %get-tuple-element.78.refs_3_), channel_id=1, source_target_pairs={{0,12},{1,13},{2,14},{3,15},{4,0},{5,1},{6,2},{7,3},{8,4},{9,5},{1... | collective-permute-start | bytes 1572872 | tf_op jit(solution)/shard_map/send_xa1/ppermute | solution.py:343
  74.3 15.5 %collective-permute-start.16 = (bf16[128,2048]{1,0:T(8,128)(2,1)S(1)}, bf16[128,2048]{1,0:T(8,128)(2,1)S(1)}, u32[]{:S(2)}, u32[]{:S(2)}) collective-permute-start(bf16[128,2048]{1,0:T(8,128)(2,1)S(1)} %collective-permute-done.12.refs_2_), channel_id=1, source_target_pairs={{0,2},{1,3},{2,0},{3,1},{4,6},{5,7},{6,4},{7,5},{8,10},{9,11},{10,... | collective-permute-start | bytes 1572872 | tf_op jit(solution)/shard_map/send_yf1/ppermute | solution.py:343
  78.2 5.4 %collective-permute-start.18 = (f32[8,4,128,128]{3,2,1,0:T(8,128)S(1)}, f32[8,4,128,128]{3,2,1,0:T(8,128)S(1)}, u32[]{:S(2)}, u32[]{:S(2)}) collective-permute-start(f32[8,4,128,128]{3,2,1,0:T(8,128)S(1)} %get-tuple-element.84), channel_id=1, source_target_pairs={{0,1},{1,0},{2,3},{3,2},{4,5},{5,4},{6,7},{7,6},{8,9},{9,8},{10,11... | collective-permute-start | bytes 6291464 | tf_op jit(solution)/shard_map/send_part6/ppermute | solution.py:343
  83.6 8.5 %collective-permute-start.14 = (f32[8,2,128,128]{3,2,1,0:T(8,128)S(1)}, f32[8,2,128,128]{3,2,1,0:T(8,128)S(1)}, u32[]{:S(2)}, u32[]{:S(2)}) collective-permute-start(f32[8,2,128,128]{3,2,1,0:T(8,128)S(1)} %get-tuple-element.77), channel_id=1, source_target_pairs={{0,1},{1,0},{2,3},{3,2},{4,5},{5,4},{6,7},{7,6},{8,9},{9,8},{10,11... | collective-permute-start | bytes 3145736 | tf_op jit(solution)/shard_map/send_part7/ppermute | solution.py:343
  88.5 3.6 %collective-permute-start.19 = (bf16[128,2048]{1,0:T(8,128)(2,1)S(1)}, bf16[128,2048]{1,0:T(8,128)(2,1)S(1)}, u32[]{:S(2)}, u32[]{:S(2)}) collective-permute-start(bf16[128,2048]{1,0:T(8,128)(2,1)S(1)} %collective-permute-done.15.refs_2_), channel_id=1, source_target_pairs={{0,1},{1,0},{2,3},{3,2},{4,5},{5,4},{6,7},{7,6},{8,9},{9,8},{10,11... | collective-permute-start | bytes 1572872 | tf_op jit(solution)/shard_map/send_cxa1/ppermute | solution.py:343
  89.8 2.3 %collective-permute-start.20 = (bf16[128,2048]{1,0:T(8,128)(2,1)S(1)}, bf16[128,2048]{1,0:T(8,128)(2,1)S(1)}, u32[]{:S(2)}, u32[]{:S(2)}) collective-permute-start(bf16[128,2048]{1,0:T(8,128)(2,1)S(1)} %collective-permute-done.16.refs_3_), channel_id=1, source_target_pairs={{0,1},{1,0},{2,3},{3,2},{4,5},{5,4},{6,7},{7,6},{8,9},{9,8},{10,11... | collective-permute-start | bytes 1572872 | tf_op jit(solution)/shard_map/send_cyf1/ppermute | solution.py:343

commit v5 on v4

--- a/solution.py
+++ b/solution.py
@@ -14,6 +14,7 @@
 HALVES_LIMIT = 44
 BF16 = jnp.bfloat16
 NT = (((1,), (1,)), ((), ()))
+BEHIND = pl.CostEstimate(flops=92 * 10**9, bytes_accessed=1, transcendentals=0)
 SMALL = pl.CostEstimate(flops=10**9, bytes_accessed=1, transcendentals=0)
 
 
@@ -136,7 +137,7 @@
             pltpu.VMEM((layers * PROJ, SLOT), F32),
         ],
         compiler_params=pltpu.CompilerParams(vmem_limit_bytes=16 << 20),
-        cost_estimate=SMALL,
+        cost_estimate=BEHIND,
         name="prepare",
     )(layer_slot, pair_query, a_rows, b_rows, x0, x1)
 

time: 96.2 us -> 94.4 us (0.981)
  waiting for transfers between devices: 28.6 us -> 27 us
    ppermute x21, waiting for transfers between devices: 28.6 us -> 27 us  [send(): return lax.ppermute(x, 'rows', perm)]
  transfers between devices with their start and end apart: 21 -> 21, of which waited for: 11 -> 10; matrix products, arithmetic and copies ran while one was open for 0% -> 0% of each run, Pallas kernels for 37% -> 38%
where the time goes in v5:
time: 94.4 us; the launch traced here: 94.1 us
  Pallas kernels  39.5 us (42%)
  waiting for transfers between devices  27 us (29%)
  starting transfers between devices  20.6 us (22%)
  local copies, waits for them, and re-layouts  5.34 us (6%)
  other arithmetic  1.27 us (1%)
    pallas_call x8, Pallas kernels, stage(): pl.pallas_call(body, out_shape=shapes, in_specs=specs, out_specs=out_spec...  28.2 us
    ppermute x21, waiting for transfers between devices, send(): return lax.ppermute(x, 'rows', perm)  27 us
    ppermute x21, starting transfers between devices, send(): return lax.ppermute(x, 'rows', perm)  20.6 us
    pallas_call x1, Pallas kernels, make_halves(): pl.pallas_call(halves_kernel, out_shape=[side] * 3 + [jax.ShapeDtypeStruc...  6.71 us
    unnamed x10, local copies, waits for them, and re-layouts  5.34 us
    pallas_call x1, Pallas kernels, prepare(): pl.pallas_call(functools.partial(prepare_kernel, layers), out_shape=[fact...  3.2 us
  transfers between devices with their start and end apart: 21, of which 10 were waited for; matrix products, arithmetic and copies ran while one was open for 0% of the time, Pallas kernels for 38%

profile of v5, /device:TPU:0, one launch (start us, length us, event | category | flops | bytes accessed | tf_op | source)
XLA Modules:
  0.0 94.1 jit_solution(1529548281744535471)
XLA Ops:
  0.0 1.3 %broadcast_select_fusion = (bf16[128,2048]{1,0:T(8,128)(2,1)S(1)}, bf16[128,2048]{1,0:T(8,128)(2,1)S(1)}) fusion(pred[]{:T(512)S(6)} %eq.6, bf16[128,4096]{1,0:T(8,128)(2,1)} %param.7), kind=kLoop, calls=%fused_computation | loop fusion | flops 524288 | bytes 2097153 | tf_op jit(solution)/shard_map/jit(_where)/select_n | solution.py:370
  1.8 4.7 %collective-permute-start.2 = (bf16[128,2048]{1,0:T(8,128)(2,1)S(1)}, bf16[128,2048]{1,0:T(8,128)(2,1)S(1)}, u32[]{:S(2)}, u32[]{:S(2)}) collective-permute-start(bf16[128,2048]{1,0:T(8,128)(2,1)S(1)} %get-tuple-element.95.x0), channel_id=1, source_target_pairs={{0,12},{1,13},{2,14},{3,15},{4,0},{5,1},{6,2},{7,3},{8,4},{9,5},{1... | collective-permute-start | bytes 1572872 | tf_op jit(solution)/shard_map/send_a0/ppermute | solution.py:344
  6.5 1.5 %collective-permute-start.3 = (bf16[128,2048]{1,0:T(8,128)(2,1)S(1)}, bf16[128,2048]{1,0:T(8,128)(2,1)S(1)}, u32[]{:S(2)}, u32[]{:S(2)}) collective-permute-start(bf16[128,2048]{1,0:T(8,128)(2,1)S(1)} %get-tuple-element.95.x0), channel_id=1, source_target_pairs={{0,2},{1,3},{2,0},{3,1},{4,6},{5,7},{6,4},{7,5},{8,10},{9,11},{10,... | collective-permute-start | bytes 1572872 | tf_op jit(solution)/shard_map/send_y0/ppermute | solution.py:344
  11.7 3.2 %prepare.1 = (bf16[8,256,256]{2,1,0:T(8,128)(2,1)S(1)}, bf16[8,256,256]{2,1,0:T(8,128)(2,1)S(1)}, bf16[128,2048]{1,0:T(8,128)(2,1)S(1)}, bf16[128,2048]{1,0:T(8,128)(2,1)S(1)}, s32[8,16]{1,0:T(8,128)S(1)}) custom-call(s32[16]{0:T(128)S(1)} %copy-done.4, s32[8,8]{1,0:T(8,128)S(1)} %copy-done.3, f32[256,16]{1,0:T(8,128)S(1)} %bitcast.2, ...), custom_call_target="tpu_custom_call" | custom-call | flops 92000002048 | bytes 1 | tf_op jit(solution)/shard_map/prepare/pallas_call | solution.py:130
  14.9 3.8 %collective-permute-done.2.x0 = bf16[128,2048]{1,0:T(8,128)(2,1)S(1)} collective-permute-done((bf16[128,2048]{1,0:T(8,128)(2,1)S(1)}, bf16[128,2048]{1,0:T(8,128)(2,1)S(1)}, u32[]{:S(2)}, u32[]{:S(2)}) %collective-permute-start.2) | collective-permute-done | bytes 524320 | tf_op jit(solution)/shard_map/send_a0/ppermute | solution.py:344
  18.7 2.5 %collective-permute-done.3.x1 = bf16[128,2048]{1,0:T(8,128)(2,1)S(1)} collective-permute-done((bf16[128,2048]{1,0:T(8,128)(2,1)S(1)}, bf16[128,2048]{1,0:T(8,128)(2,1)S(1)}, u32[]{:S(2)}, u32[]{:S(2)}) %collective-permute-start.3) | collective-permute-done | bytes 524320 | tf_op jit(solution)/shard_map/send_y0/ppermute | solution.py:344
  22.0 1.6 %collective-permute-start.9 = (bf16[128,2048]{1,0:T(8,128)(2,1)S(1)}, bf16[128,2048]{1,0:T(8,128)(2,1)S(1)}, u32[]{:S(2)}, u32[]{:S(2)}) collective-permute-start(bf16[128,2048]{1,0:T(8,128)(2,1)S(1)} %get-tuple-element.65.refs_4_), channel_id=1, source_target_pairs={{0,2},{1,3},{2,0},{3,1},{4,6},{5,7},{6,4},{7,5},{8,10},{9,11},{10,... | collective-permute-start | bytes 1572872 | tf_op jit(solution)/shard_map/send_ya0/ppermute | solution.py:344
  23.6 7.2 %collective-permute-done.4.x0 = bf16[128,2048]{1,0:T(8,128)(2,1)S(1)} collective-permute-done((bf16[128,2048]{1,0:T(8,128)(2,1)S(1)}, bf16[128,2048]{1,0:T(8,128)(2,1)S(1)}, u32[]{:S(2)}, u32[]{:S(2)}) %collective-permute-start.4) | collective-permute-done | bytes 524320 | tf_op jit(solution)/shard_map/send_b0/ppermute | solution.py:344
  30.8 1.6 %collective-permute-done.5.x1 = bf16[128,2048]{1,0:T(8,128)(2,1)S(1)} collective-permute-done((bf16[128,2048]{1,0:T(8,128)(2,1)S(1)}, bf16[128,2048]{1,0:T(8,128)(2,1)S(1)}, u32[]{:S(2)}, u32[]{:S(2)}) %collective-permute-start.5) | collective-permute-done | bytes 524320 | tf_op jit(solution)/shard_map/send_y1/ppermute | solution.py:344
  33.2 6.7 %halves.1 = (bf16[1024,2048]{1,0:T(8,128)(2,1)S(1)}, bf16[1024,2048]{1,0:T(8,128)(2,1)S(1)}, bf16[1024,2048]{1,0:T(8,128)(2,1)}, f32[8,128]{1,0:T(8,128)}) custom-call(bf16[1024,4096]{1,0:T(8,128)(2,1)} %train.1, bf16[1024,4096]{1,0:T(8,128)(2,1)} %collective-permute-done.1.twin_train), custom_call_target="tpu_custom_call" | custom-call | flops 1000000000 | bytes 1 | tf_op jit(solution)/shard_map/halves/pallas_call | solution.py:164
  39.9 1.5 %collective-permute-start.6 = (bf16[128,2048]{1,0:T(8,128)(2,1)S(1)}, bf16[128,2048]{1,0:T(8,128)(2,1)S(1)}, u32[]{:S(2)}, u32[]{:S(2)}) collective-permute-start(bf16[128,2048]{1,0:T(8,128)(2,1)S(1)} %get-tuple-element.65.refs_4_), channel_id=1, source_target_pairs={{0,12},{1,13},{2,14},{3,15},{4,0},{5,1},{6,2},{7,3},{8,4},{9,5},{1... | collective-permute-start | bytes 1572872 | tf_op jit(solution)/shard_map/send_f0/ppermute | solution.py:344
  41.4 1.0 %collective-permute-start.7 = (bf16[128,2048]{1,0:T(8,128)(2,1)S(1)}, bf16[128,2048]{1,0:T(8,128)(2,1)S(1)}, u32[]{:S(2)}, u32[]{:S(2)}) collective-permute-start(bf16[128,2048]{1,0:T(8,128)(2,1)S(1)} %get-tuple-element.66.refs_2_), channel_id=1, source_target_pairs={{0,2},{1,3},{2,0},{3,1},{4,6},{5,7},{6,4},{7,5},{8,10},{9,11},{10,... | collective-permute-start | bytes 1572872 | tf_op jit(solution)/shard_map/send_yb0/ppermute | solution.py:344
  42.5 2.2 %copy-done = bf16[1024,2048]{1,0:T(8,128)(2,1)S(1)} copy-done((bf16[1024,2048]{1,0:T(8,128)(2,1)S(1)}, bf16[1024,2048]{1,0:T(8,128)(2,1)}, u32[]{:S(2)}) %copy-start) | copy-done | bytes 4194328
  44.7 5.1 %stage.8 = (f32[8,128]{1,0:T(8,128)S(1)}, f32[8,4,128,128]{3,2,1,0:T(8,128)S(1)}, f32[8,4,128,128]{3,2,1,0:T(8,128)S(1)}) custom-call(s32[8,16]{1,0:T(8,128)S(1)} %get-tuple-element.51.refs_0_, bf16[1024,2048]{1,0:T(8,128)(2,1)S(1)} %get-tuple-element.53.refs_1_, bf16[128,2048]{1,0:T(8,128)(2,1)S(1)} %get-tuple-element.54.refs_2_, ...), custom_call_target="tpu_custom_call" | custom-call | flops 1150000000 | bytes 1 | tf_op jit(solution)/shard_map/stage/pallas_call | solution.py:293
  49.8 1.1 %collective-permute-start.12 = (bf16[128,2048]{1,0:T(8,128)(2,1)S(1)}, bf16[128,2048]{1,0:T(8,128)(2,1)S(1)}, u32[]{:S(2)}, u32[]{:S(2)}) collective-permute-start(bf16[128,2048]{1,0:T(8,128)(2,1)S(1)} %collective-permute-done.8.refs_4_), channel_id=1, source_target_pairs={{0,4},{1,5},{2,6},{3,7},{4,8},{5,9},{6,10},{7,11},{8,12},{9,13},{1... | collective-permute-start | bytes 1572872 | tf_op jit(solution)/shard_map/send_f1/ppermute | solution.py:344
  51.4 5.2 %stage.9 = (f32[8,128]{1,0:T(8,128)S(1)}, f32[8,4,128,128]{3,2,1,0:T(8,128)S(1)}, f32[8,8,128,128]{3,2,1,0:T(8,128)S(1)}) custom-call(s32[8,16]{1,0:T(8,128)S(1)} %get-tuple-element.51.refs_0_, bf16[1024,2048]{1,0:T(8,128)(2,1)S(1)} %get-tuple-element.53.refs_1_, bf16[128,2048]{1,0:T(8,128)(2,1)S(1)} %get-tuple-element.66.refs_2_, ...), custom_call_target="tpu_custom_call" | custom-call | flops 1150000000 | bytes 1 | tf_op jit(solution)/shard_map/stage/pallas_call | solution.py:293
  56.6 3.5 %collective-permute-start.10 = (bf16[128,2048]{1,0:T(8,128)(2,1)S(1)}, bf16[128,2048]{1,0:T(8,128)(2,1)S(1)}, u32[]{:S(2)}, u32[]{:S(2)}) collective-permute-start(bf16[128,2048]{1,0:T(8,128)(2,1)S(1)} %get-tuple-element.71.refs_3_), channel_id=1, source_target_pairs={{0,12},{1,13},{2,14},{3,15},{4,0},{5,1},{6,2},{7,3},{8,4},{9,5},{1... | collective-permute-start | bytes 1572872 | tf_op jit(solution)/shard_map/send_a1/ppermute | solution.py:344
  60.1 1.0 %collective-permute-start.11 = (bf16[128,2048]{1,0:T(8,128)(2,1)S(1)}, bf16[128,2048]{1,0:T(8,128)(2,1)S(1)}, u32[]{:S(2)}, u32[]{:S(2)}) collective-permute-start(bf16[128,2048]{1,0:T(8,128)(2,1)S(1)} %collective-permute-done.6.refs_2_), channel_id=1, source_target_pairs={{0,2},{1,3},{2,0},{3,1},{4,6},{5,7},{6,4},{7,5},{8,10},{9,11},{10,... | collective-permute-start | bytes 1572872 | tf_op jit(solution)/shard_map/send_yf0/ppermute | solution.py:344
  61.2 3.0 %stage.10 = (f32[8,128]{1,0:T(8,128)S(1)}, f32[8,2,128,128]{3,2,1,0:T(8,128)S(1)}, f32[8,2,128,128]{3,2,1,0:T(8,128)S(1)}) custom-call(s32[8,16]{1,0:T(8,128)S(1)} %get-tuple-element.51.refs_0_, bf16[1024,2048]{1,0:T(8,128)(2,1)S(1)} %get-tuple-element.53.refs_1_, bf16[128,2048]{1,0:T(8,128)(2,1)S(1)} %collective-permute-done.6.refs_2_, ...), custom_call_target="tpu_custom_call" | custom-call | flops 1150000000 | bytes 1 | tf_op jit(solution)/shard_map/stage/pallas_call | solution.py:293
  64.2 2.4 %collective-permute-done.12.refs_2_ = bf16[128,2048]{1,0:T(8,128)(2,1)S(1)} collective-permute-done((bf16[128,2048]{1,0:T(8,128)(2,1)S(1)}, bf16[128,2048]{1,0:T(8,128)(2,1)S(1)}, u32[]{:S(2)}, u32[]{:S(2)}) %collective-permute-start.12) | collective-permute-done | bytes 524320 | tf_op jit(solution)/shard_map/send_f1/ppermute | solution.py:344
  66.6 1.0 %collective-permute-done.13.refs_3_ = bf16[128,2048]{1,0:T(8,128)(2,1)S(1)} collective-permute-done((bf16[128,2048]{1,0:T(8,128)(2,1)S(1)}, bf16[128,2048]{1,0:T(8,128)(2,1)S(1)}, u32[]{:S(2)}, u32[]{:S(2)}) %collective-permute-start.13) | collective-permute-done | bytes 524320 | tf_op jit(solution)/shard_map/send_yb1/ppermute | solution.py:344
  67.5 3.0 %stage.11 = (f32[8,128]{1,0:T(8,128)S(1)}, f32[8,2,128,128]{3,2,1,0:T(8,128)S(1)}, f32[8,4,128,128]{3,2,1,0:T(8,128)S(1)}) custom-call(s32[8,16]{1,0:T(8,128)S(1)} %get-tuple-element.51.refs_0_, bf16[1024,2048]{1,0:T(8,128)(2,1)S(1)} %get-tuple-element.53.refs_1_, bf16[128,2048]{1,0:T(8,128)(2,1)S(1)} %collective-permute-done.12.refs_2_, ...), custom_call_target="tpu_custom_call" | custom-call | flops 1150000000 | bytes 1 | tf_op jit(solution)/shard_map/stage/pallas_call | solution.py:293
  70.5 1.8 %collective-permute-start.15 = (bf16[128,2048]{1,0:T(8,128)(2,1)S(1)}, bf16[128,2048]{1,0:T(8,128)(2,1)S(1)}, u32[]{:S(2)}, u32[]{:S(2)}) collective-permute-start(bf16[128,2048]{1,0:T(8,128)(2,1)S(1)} %get-tuple-element.78.refs_3_), channel_id=1, source_target_pairs={{0,12},{1,13},{2,14},{3,15},{4,0},{5,1},{6,2},{7,3},{8,4},{9,5},{1... | collective-permute-start | bytes 1572872 | tf_op jit(solution)/shard_map/send_xa1/ppermute | solution.py:344
  72.4 1.1 %collective-permute-start.16 = (bf16[128,2048]{1,0:T(8,128)(2,1)S(1)}, bf16[128,2048]{1,0:T(8,128)(2,1)S(1)}, u32[]{:S(2)}, u32[]{:S(2)}) collective-permute-start(bf16[128,2048]{1,0:T(8,128)(2,1)S(1)} %collective-permute-done.12.refs_2_), channel_id=1, source_target_pairs={{0,2},{1,3},{2,0},{3,1},{4,6},{5,7},{6,4},{7,5},{8,10},{9,11},{10,... | collective-permute-start | bytes 1572872 | tf_op jit(solution)/shard_map/send_yf1/ppermute | solution.py:344
  73.4 2.9 %collective-permute-done.10.refs_2_ = bf16[128,2048]{1,0:T(8,128)(2,1)S(1)} collective-permute-done((bf16[128,2048]{1,0:T(8,128)(2,1)S(1)}, bf16[128,2048]{1,0:T(8,128)(2,1)S(1)}, u32[]{:S(2)}, u32[]{:S(2)}) %collective-permute-start.10) | collective-permute-done | bytes 524320 | tf_op jit(solution)/shard_map/send_a1/ppermute | solution.py:344
  76.3 2.4 %collective-permute-done.11.refs_3_ = bf16[128,2048]{1,0:T(8,128)(2,1)S(1)} collective-permute-done((bf16[128,2048]{1,0:T(8,128)(2,1)S(1)}, bf16[128,2048]{1,0:T(8,128)(2,1)S(1)}, u32[]{:S(2)}, u32[]{:S(2)}) %collective-permute-start.11) | collective-permute-done | bytes 524320 | tf_op jit(solution)/shard_map/send_yf0/ppermute | solution.py:344
  78.7 3.0 %stage.12 = (f32[8,128]{1,0:T(8,128)S(1)}, f32[8,2,128,128]{3,2,1,0:T(8,128)S(1)}, f32[8,2,128,128]{3,2,1,0:T(8,128)S(1)}) custom-call(s32[8,16]{1,0:T(8,128)S(1)} %get-tuple-element.51.refs_0_, bf16[1024,2048]{1,0:T(8,128)(2,1)S(1)} %get-tuple-element.53.refs_1_, bf16[128,2048]{1,0:T(8,128)(2,1)S(1)} %collective-permute-done.10.refs_2_, ...), custom_call_target="tpu_custom_call" | custom-call | flops 1150000000 | bytes 1 | tf_op jit(solution)/shard_map/stage/pallas_call | solution.py:293
  81.8 2.9 %stage.13 = (f32[8,128]{1,0:T(8,128)S(1)}, f32[8,8,128,128]{3,2,1,0:T(8,128)}) custom-call(s32[8,16]{1,0:T(8,128)S(1)} %get-tuple-element.51.refs_0_, f32[8,4,128,128]{3,2,1,0:T(8,128)S(1)} %get-tuple-element.61.refs_1_, f32[8,8,128,128]{3,2,1,0:T(8,128)S(1)} %collective-permute-done.17.refs_2_.refs_4_, ...), custom_call_target="tpu_custom_call" | custom-call | flops 1150000000 | bytes 1 | tf_op jit(solution)/shard_map/stage/pallas_call | solution.py:293
  84.7 1.9 %collective-permute-done.15.refs_2_ = bf16[128,2048]{1,0:T(8,128)(2,1)S(1)} collective-permute-done((bf16[128,2048]{1,0:T(8,128)(2,1)S(1)}, bf16[128,2048]{1,0:T(8,128)(2,1)S(1)}, u32[]{:S(2)}, u32[]{:S(2)}) %collective-permute-start.15) | collective-permute-done | bytes 524320 | tf_op jit(solution)/shard_map/send_xa1/ppermute | solution.py:344
  86.6 1.3 %collective-permute-done.16.refs_3_ = bf16[128,2048]{1,0:T(8,128)(2,1)S(1)} collective-permute-done((bf16[128,2048]{1,0:T(8,128)(2,1)S(1)}, bf16[128,2048]{1,0:T(8,128)(2,1)S(1)}, u32[]{:S(2)}, u32[]{:S(2)}) %collective-permute-start.16) | collective-permute-done | bytes 524320 | tf_op jit(solution)/shard_map/send_yf1/ppermute | solution.py:344
  87.9 2.3 %stage.14 = (f32[8,128]{1,0:T(8,128)}, f32[8,2,128,128]{3,2,1,0:T(8,128)S(1)}) custom-call(s32[8,16]{1,0:T(8,128)S(1)} %get-tuple-element.51.refs_0_, bf16[1024,2048]{1,0:T(8,128)(2,1)S(1)} %get-tuple-element.53.refs_1_, bf16[128,2048]{1,0:T(8,128)(2,1)S(1)} %collective-permute-done.15.refs_2_, bf16[128,2048]{1,0:T(8,128)(2,1)S(1)} %collective-permute-done.16.refs_3_, ...), custom_call_target="tpu_custom_call" | custom-call | flops 13799999488 | bytes 1 | tf_op jit(solution)/shard_map/stage/pallas_call | solution.py:293
  90.2 3.7 %stage.15 = (f32[8,128]{1,0:T(8,128)}, f32[8,8,128,128]{3,2,1,0:T(8,128)}) custom-call(s32[8,16]{1,0:T(8,128)S(1)} %get-tuple-element.51.refs_0_, f32[8,4,128,128]{3,2,1,0:T(8,128)S(1)} %get-tuple-element.61.refs_1_, f32[8,2,128,128]{3,2,1,0:T(8,128)S(1)} %collective-permute-done.14.refs_2_, ...), custom_call_target="tpu_custom_call", output_to_operand_aliasing={{1}: (10, {})} | custom-call | flops 1150000000 | bytes 1 | tf_op jit(solution)/shard_map/stage/pallas_call | solution.py:293
  (34 shorter events, 6.3 us)
Async XLA Ops:
  1.3 6.7 %collective-permute-start = (bf16[128,2048]{1,0:T(8,128)(2,1)S(1)}, bf16[128,2048]{1,0:T(8,128)(2,1)S(1)}, u32[]{:S(2)}, u32[]{:S(2)}) collective-permute-start(bf16[128,2048]{1,0:T(8,128)(2,1)S(1)} %get-tuple-element.94), channel_id=1, source_target_pairs={{0,1},{1,0},{2,3},{3,2},{4,5},{5,4},{6,7},{7,6},{8,9},{9,8},{10,11... | collective-permute-start | bytes 1572872 | tf_op jit(solution)/shard_map/send_h1/ppermute | solution.py:344
  1.8 16.9 %collective-permute-start.2 = (bf16[128,2048]{1,0:T(8,128)(2,1)S(1)}, bf16[128,2048]{1,0:T(8,128)(2,1)S(1)}, u32[]{:S(2)}, u32[]{:S(2)}) collective-permute-start(bf16[128,2048]{1,0:T(8,128)(2,1)S(1)} %get-tuple-element.95.x0), channel_id=1, source_target_pairs={{0,12},{1,13},{2,14},{3,15},{4,0},{5,1},{6,2},{7,3},{8,4},{9,5},{1... | collective-permute-start | bytes 1572872 | tf_op jit(solution)/shard_map/send_a0/ppermute | solution.py:344
  6.5 14.8 %collective-permute-start.3 = (bf16[128,2048]{1,0:T(8,128)(2,1)S(1)}, bf16[128,2048]{1,0:T(8,128)(2,1)S(1)}, u32[]{:S(2)}, u32[]{:S(2)}) collective-permute-start(bf16[128,2048]{1,0:T(8,128)(2,1)S(1)} %get-tuple-element.95.x0), channel_id=1, source_target_pairs={{0,2},{1,3},{2,0},{3,1},{4,6},{5,7},{6,4},{7,5},{8,10},{9,11},{10,... | collective-permute-start | bytes 1572872 | tf_op jit(solution)/shard_map/send_y0/ppermute | solution.py:344
  8.0 22.9 %collective-permute-start.4 = (bf16[128,2048]{1,0:T(8,128)(2,1)S(1)}, bf16[128,2048]{1,0:T(8,128)(2,1)S(1)}, u32[]{:S(2)}, u32[]{:S(2)}) collective-permute-start(bf16[128,2048]{1,0:T(8,128)(2,1)S(1)} %get-tuple-element.95.x0), channel_id=1, source_target_pairs={{0,4},{1,5},{2,6},{3,7},{4,8},{5,9},{6,10},{7,11},{8,12},{9,13},{1... | collective-permute-start | bytes 1572872 | tf_op jit(solution)/shard_map/send_b0/ppermute | solution.py:344
  8.0 25.2 %collective-permute-start.1 = (bf16[1024,4096]{1,0:T(8,128)(2,1)}, bf16[1024,4096]{1,0:T(8,128)(2,1)}, u32[]{:S(2)}, u32[]{:S(2)}) collective-permute-start(bf16[1024,4096]{1,0:T(8,128)(2,1)} %train.1), channel_id=1, source_target_pairs={{0,1},{1,0},{2,3},{3,2},{4,5},{5,4},{6,7},{7,6},{8,9},{9,8},{10,11... | collective-permute-start | bytes 25165832 | tf_op jit(solution)/shard_map/send_train/ppermute | solution.py:344
  8.0 24.5 %collective-permute-start.5 = (bf16[128,2048]{1,0:T(8,128)(2,1)S(1)}, bf16[128,2048]{1,0:T(8,128)(2,1)S(1)}, u32[]{:S(2)}, u32[]{:S(2)}) collective-permute-start(bf16[128,2048]{1,0:T(8,128)(2,1)S(1)} %collective-permute-done.x1), channel_id=1, source_target_pairs={{0,2},{1,3},{2,0},{3,1},{4,6},{5,7},{6,4},{7,5},{8,10},{9,11},{10,... | collective-permute-start | bytes 1572872 | tf_op jit(solution)/shard_map/send_y1/ppermute | solution.py:344
  8.6 0.9 copy-start.1
  9.5 0.9 copy-start.2
  10.4 0.7 copy-start.3
  11.1 0.7 copy-start.4
  21.9 27.9 %collective-permute-start.8 = (bf16[128,2048]{1,0:T(8,128)(2,1)S(1)}, bf16[128,2048]{1,0:T(8,128)(2,1)S(1)}, u32[]{:S(2)}, u32[]{:S(2)}) collective-permute-start(bf16[128,2048]{1,0:T(8,128)(2,1)S(1)} %get-tuple-element.71.refs_3_), channel_id=1, source_target_pairs={{0,4},{1,5},{2,6},{3,7},{4,8},{5,9},{6,10},{7,11},{8,12},{9,13},{1... | collective-permute-start | bytes 1572872 | tf_op jit(solution)/shard_map/send_b1/ppermute | solution.py:344
  22.0 27.8 %collective-permute-start.9 = (bf16[128,2048]{1,0:T(8,128)(2,1)S(1)}, bf16[128,2048]{1,0:T(8,128)(2,1)S(1)}, u32[]{:S(2)}, u32[]{:S(2)}) collective-permute-start(bf16[128,2048]{1,0:T(8,128)(2,1)S(1)} %get-tuple-element.65.refs_4_), channel_id=1, source_target_pairs={{0,2},{1,3},{2,0},{3,1},{4,6},{5,7},{6,4},{7,5},{8,10},{9,11},{10,... | collective-permute-start | bytes 1572872 | tf_op jit(solution)/shard_map/send_ya0/ppermute | solution.py:344
  39.9 16.7 %collective-permute-start.6 = (bf16[128,2048]{1,0:T(8,128)(2,1)S(1)}, bf16[128,2048]{1,0:T(8,128)(2,1)S(1)}, u32[]{:S(2)}, u32[]{:S(2)}) collective-permute-start(bf16[128,2048]{1,0:T(8,128)(2,1)S(1)} %get-tuple-element.65.refs_4_), channel_id=1, source_target_pairs={{0,12},{1,13},{2,14},{3,15},{4,0},{5,1},{6,2},{7,3},{8,4},{9,5},{1... | collective-permute-start | bytes 1572872 | tf_op jit(solution)/shard_map/send_f0/ppermute | solution.py:344
  41.4 15.2 %collective-permute-start.7 = (bf16[128,2048]{1,0:T(8,128)(2,1)S(1)}, bf16[128,2048]{1,0:T(8,128)(2,1)S(1)}, u32[]{:S(2)}, u32[]{:S(2)}) collective-permute-start(bf16[128,2048]{1,0:T(8,128)(2,1)S(1)} %get-tuple-element.66.refs_2_), channel_id=1, source_target_pairs={{0,2},{1,3},{2,0},{3,1},{4,6},{5,7},{6,4},{7,5},{8,10},{9,11},{10,... | collective-permute-start | bytes 1572872 | tf_op jit(solution)/shard_map/send_yb0/ppermute | solution.py:344
  42.5 2.2 %copy-start = (bf16[1024,2048]{1,0:T(8,128)(2,1)S(1)}, bf16[1024,2048]{1,0:T(8,128)(2,1)}, u32[]{:S(2)}) copy-start(bf16[1024,2048]{1,0:T(8,128)(2,1)} %get-tuple-element.60.refs_6_.refs_4_) | copy-start | bytes 12582916
  49.8 16.8 %collective-permute-start.12 = (bf16[128,2048]{1,0:T(8,128)(2,1)S(1)}, bf16[128,2048]{1,0:T(8,128)(2,1)S(1)}, u32[]{:S(2)}, u32[]{:S(2)}) collective-permute-start(bf16[128,2048]{1,0:T(8,128)(2,1)S(1)} %collective-permute-done.8.refs_4_), channel_id=1, source_target_pairs={{0,4},{1,5},{2,6},{3,7},{4,8},{5,9},{6,10},{7,11},{8,12},{9,13},{1... | collective-permute-start | bytes 1572872 | tf_op jit(solution)/shard_map/send_f1/ppermute | solution.py:344
  50.9 16.6 %collective-permute-start.13 = (bf16[128,2048]{1,0:T(8,128)(2,1)S(1)}, bf16[128,2048]{1,0:T(8,128)(2,1)S(1)}, u32[]{:S(2)}, u32[]{:S(2)}) collective-permute-start(bf16[128,2048]{1,0:T(8,128)(2,1)S(1)} %collective-permute-done.8.refs_4_), channel_id=1, source_target_pairs={{0,2},{1,3},{2,0},{3,1},{4,6},{5,7},{6,4},{7,5},{8,10},{9,11},{10,... | collective-permute-start | bytes 1572872 | tf_op jit(solution)/shard_map/send_yb1/ppermute | solution.py:344
  56.6 19.7 %collective-permute-start.10 = (bf16[128,2048]{1,0:T(8,128)(2,1)S(1)}, bf16[128,2048]{1,0:T(8,128)(2,1)S(1)}, u32[]{:S(2)}, u32[]{:S(2)}) collective-permute-start(bf16[128,2048]{1,0:T(8,128)(2,1)S(1)} %get-tuple-element.71.refs_3_), channel_id=1, source_target_pairs={{0,12},{1,13},{2,14},{3,15},{4,0},{5,1},{6,2},{7,3},{8,4},{9,5},{1... | collective-permute-start | bytes 1572872 | tf_op jit(solution)/shard_map/send_a1/ppermute | solution.py:344
  60.1 18.6 %collective-permute-start.11 = (bf16[128,2048]{1,0:T(8,128)(2,1)S(1)}, bf16[128,2048]{1,0:T(8,128)(2,1)S(1)}, u32[]{:S(2)}, u32[]{:S(2)}) collective-permute-start(bf16[128,2048]{1,0:T(8,128)(2,1)S(1)} %collective-permute-done.6.refs_2_), channel_id=1, source_target_pairs={{0,2},{1,3},{2,0},{3,1},{4,6},{5,7},{6,4},{7,5},{8,10},{9,11},{10,... | collective-permute-start | bytes 1572872 | tf_op jit(solution)/shard_map/send_yf0/ppermute | solution.py:344
  61.2 20.6 %collective-permute-start.17 = (f32[8,8,128,128]{3,2,1,0:T(8,128)S(1)}, f32[8,8,128,128]{3,2,1,0:T(8,128)S(1)}, u32[]{:S(2)}, u32[]{:S(2)}) collective-permute-start(f32[8,8,128,128]{3,2,1,0:T(8,128)S(1)} %get-tuple-element.80), channel_id=1, source_target_pairs={{0,1},{1,0},{2,3},{3,2},{4,5},{5,4},{6,7},{7,6},{8,9},{9,8},{10,11... | collective-permute-start | bytes 12582920 | tf_op jit(solution)/shard_map/send_part4/ppermute | solution.py:344
  70.5 16.0 %collective-permute-start.15 = (bf16[128,2048]{1,0:T(8,128)(2,1)S(1)}, bf16[128,2048]{1,0:T(8,128)(2,1)S(1)}, u32[]{:S(2)}, u32[]{:S(2)}) collective-permute-start(bf16[128,2048]{1,0:T(8,128)(2,1)S(1)} %get-tuple-element.78.refs_3_), channel_id=1, source_target_pairs={{0,12},{1,13},{2,14},{3,15},{4,0},{5,1},{6,2},{7,3},{8,4},{9,5},{1... | collective-permute-start | bytes 1572872 | tf_op jit(solution)/shard_map/send_xa1/ppermute | solution.py:344
  72.4 15.5 %collective-permute-start.16 = (bf16[128,2048]{1,0:T(8,128)(2,1)S(1)}, bf16[128,2048]{1,0:T(8,128)(2,1)S(1)}, u32[]{:S(2)}, u32[]{:S(2)}) collective-permute-start(bf16[128,2048]{1,0:T(8,128)(2,1)S(1)} %collective-permute-done.12.refs_2_), channel_id=1, source_target_pairs={{0,2},{1,3},{2,0},{3,1},{4,6},{5,7},{6,4},{7,5},{8,10},{9,11},{10,... | collective-permute-start | bytes 1572872 | tf_op jit(solution)/shard_map/send_yf1/ppermute | solution.py:344
  76.3 5.4 %collective-permute-start.18 = (f32[8,4,128,128]{3,2,1,0:T(8,128)S(1)}, f32[8,4,128,128]{3,2,1,0:T(8,128)S(1)}, u32[]{:S(2)}, u32[]{:S(2)}) collective-permute-start(f32[8,4,128,128]{3,2,1,0:T(8,128)S(1)} %get-tuple-element.84), channel_id=1, source_target_pairs={{0,1},{1,0},{2,3},{3,2},{4,5},{5,4},{6,7},{7,6},{8,9},{9,8},{10,11... | collective-permute-start | bytes 6291464 | tf_op jit(solution)/shard_map/send_part6/ppermute | solution.py:344
  81.7 8.5 %collective-permute-start.14 = (f32[8,2,128,128]{3,2,1,0:T(8,128)S(1)}, f32[8,2,128,128]{3,2,1,0:T(8,128)S(1)}, u32[]{:S(2)}, u32[]{:S(2)}) collective-permute-start(f32[8,2,128,128]{3,2,1,0:T(8,128)S(1)} %get-tuple-element.77), channel_id=1, source_target_pairs={{0,1},{1,0},{2,3},{3,2},{4,5},{5,4},{6,7},{7,6},{8,9},{9,8},{10,11... | collective-permute-start | bytes 3145736 | tf_op jit(solution)/shard_map/send_part7/ppermute | solution.py:344
  86.6 3.6 %collective-permute-start.19 = (bf16[128,2048]{1,0:T(8,128)(2,1)S(1)}, bf16[128,2048]{1,0:T(8,128)(2,1)S(1)}, u32[]{:S(2)}, u32[]{:S(2)}) collective-permute-start(bf16[128,2048]{1,0:T(8,128)(2,1)S(1)} %collective-permute-done.15.refs_2_), channel_id=1, source_target_pairs={{0,1},{1,0},{2,3},{3,2},{4,5},{5,4},{6,7},{7,6},{8,9},{9,8},{10,11... | collective-permute-start | bytes 1572872 | tf_op jit(solution)/shard_map/send_cxa1/ppermute | solution.py:344
  87.9 2.3 %collective-permute-start.20 = (bf16[128,2048]{1,0:T(8,128)(2,1)S(1)}, bf16[128,2048]{1,0:T(8,128)(2,1)S(1)}, u32[]{:S(2)}, u32[]{:S(2)}) collective-permute-start(bf16[128,2048]{1,0:T(8,128)(2,1)S(1)} %collective-permute-done.16.refs_3_), channel_id=1, source_target_pairs={{0,1},{1,0},{2,3},{3,2},{4,5},{5,4},{6,7},{7,6},{8,9},{9,8},{10,11... | collective-permute-start | bytes 1572872 | tf_op jit(solution)/shard_map/send_cyf1/ppermute | solution.py:344

commit v6 on v5

--- a/solution.py
+++ b/solution.py
@@ -23,57 +23,7 @@
     rest = x - one.astype(F32)
     two = rest.astype(BF16)
     three = (rest - two.astype(F32)).astype(BF16)
-    return jnp.concatenate([one, two, three], axis=1)
-
-
-def split3(x):
-    one = x.astype(BF16)
-    rest = x - one.astype(F32)
-    two = rest.astype(BF16)
-    three = (rest - two.astype(F32)).astype(BF16)
     return one, two, three
-
-
-def halves_kernel(train, twin_train, keep, rest, theirs, token, sems):
-    token[...] = jnp.zeros_like(token)
-    half = keep.shape[1]
-    core = lax.axis_index("rows") & 1
-    mine = pl.ds(pl.multiple_of(core * half, half), half)
-    other = pl.ds(pl.multiple_of((1 - core) * half, half), half)
-    copies = [
-        pltpu.make_async_copy(train.at[:, mine], keep, sems.at[0]),
-        pltpu.make_async_copy(twin_train.at[:, mine], theirs, sems.at[1]),
-        pltpu.make_async_copy(train.at[:, other], rest, sems.at[2]),
-    ]
-    for copy in copies:
-        copy.start()
-    for copy in copies:
-        copy.wait()
-
-
-def make_halves(train, twin_train):
-    side = jax.ShapeDtypeStruct((train.shape[0], train.shape[1] // 2), BF16)
-    return pl.pallas_call(
-        halves_kernel,
-        out_shape=[side] * 3 + [jax.ShapeDtypeStruct((8, 128), F32)],
-        in_specs=[pl.BlockSpec(memory_space=pl.ANY)] * 2,
-        out_specs=[pl.BlockSpec(memory_space=pltpu.VMEM)] * 4,
-        scratch_shapes=[pltpu.SemaphoreType.DMA((3,))],
-        compiler_params=pltpu.CompilerParams(vmem_limit_bytes=HALVES_LIMIT << 20),
-        cost_estimate=SMALL,
-        name="halves",
-    )(train, twin_train)
-
-
-def precondition(x_refs, y_refs, high, low, skip):
-    rows = x_refs[0].shape[0]
-    for s in range(x_refs[0].shape[1] // SLOT):
-        cols = slice(s * SLOT, (s + 1) * SLOT)
-        x = jnp.concatenate([ref[:, cols] for ref in x_refs], axis=0)
-        y = jnp.dot(x, high[skip + s], preferred_element_type=F32)
-        y += jnp.dot(x, low[skip + s], preferred_element_type=F32)
-        for i, ref in enumerate(y_refs):
-            ref[:, cols] = y[i * rows : (i + 1) * rows].astype(BF16)
 
 
 def prepare_kernel(layers, slot_ref, pair_ref, a_ref, b_ref, x0, x1, high_ref, low_ref, y0, y1, table, xa, xb):

time: 94.4 us -> 94.3 us (level)
  no operation moved by 1% of the time
where the time goes in v6:
time: 94.3 us; the launch traced here: 94 us
  Pallas kernels  39.6 us (42%)
  waiting for transfers between devices  26.8 us (28%)
  starting transfers between devices  20.6 us (22%)
  local copies, waits for them, and re-layouts  5.34 us (6%)
  other arithmetic  1.27 us (1%)
    pallas_call x8, Pallas kernels, stage(): pl.pallas_call(body, out_shape=shapes, in_specs=specs, out_specs=out_spec...  28.3 us
    ppermute x21, waiting for transfers between devices, send(): return lax.ppermute(x, 'rows', perm)  26.8 us
    ppermute x21, starting transfers between devices, send(): return lax.ppermute(x, 'rows', perm)  20.6 us
    pallas_call x1, Pallas kernels, make_halves(): pl.pallas_call(halves_kernel, out_shape=[side] * 3 + [jax.ShapeDtypeStruc...  6.71 us
    unnamed x10, local copies, waits for them, and re-layouts  5.34 us
    pallas_call x1, Pallas kernels, prepare(): pl.pallas_call(functools.partial(prepare_kernel, layers), out_shape=[fact...  3.23 us
  transfers between devices with their start and end apart: 21, of which 10 were waited for; matrix products, arithmetic and copies ran while one was open for 0% of the time, Pallas kernels for 38%

profile of v6, /device:TPU:0, one launch (start us, length us, event | category | flops | bytes accessed | tf_op | source)
XLA Modules:
  0.0 94.0 jit_solution(1529548281744535471)
XLA Ops:
  0.0 1.3 %broadcast_select_fusion = (bf16[128,2048]{1,0:T(8,128)(2,1)S(1)}, bf16[128,2048]{1,0:T(8,128)(2,1)S(1)}) fusion(pred[]{:T(512)S(6)} %eq.6, bf16[128,4096]{1,0:T(8,128)(2,1)} %param.7), kind=kLoop, calls=%fused_computation | loop fusion | flops 524288 | bytes 2097153 | tf_op jit(solution)/shard_map/jit(_where)/select_n | solution.py:320
  1.8 4.7 %collective-permute-start.2 = (bf16[128,2048]{1,0:T(8,128)(2,1)S(1)}, bf16[128,2048]{1,0:T(8,128)(2,1)S(1)}, u32[]{:S(2)}, u32[]{:S(2)}) collective-permute-start(bf16[128,2048]{1,0:T(8,128)(2,1)S(1)} %get-tuple-element.95.x0), channel_id=1, source_target_pairs={{0,12},{1,13},{2,14},{3,15},{4,0},{5,1},{6,2},{7,3},{8,4},{9,5},{1... | collective-permute-start | bytes 1572872 | tf_op jit(solution)/shard_map/send_a0/ppermute | solution.py:294
  6.5 1.5 %collective-permute-start.3 = (bf16[128,2048]{1,0:T(8,128)(2,1)S(1)}, bf16[128,2048]{1,0:T(8,128)(2,1)S(1)}, u32[]{:S(2)}, u32[]{:S(2)}) collective-permute-start(bf16[128,2048]{1,0:T(8,128)(2,1)S(1)} %get-tuple-element.95.x0), channel_id=1, source_target_pairs={{0,2},{1,3},{2,0},{3,1},{4,6},{5,7},{6,4},{7,5},{8,10},{9,11},{10,... | collective-permute-start | bytes 1572872 | tf_op jit(solution)/shard_map/send_y0/ppermute | solution.py:294
  11.7 3.2 %prepare.1 = (bf16[8,256,256]{2,1,0:T(8,128)(2,1)S(1)}, bf16[8,256,256]{2,1,0:T(8,128)(2,1)S(1)}, bf16[128,2048]{1,0:T(8,128)(2,1)S(1)}, bf16[128,2048]{1,0:T(8,128)(2,1)S(1)}, s32[8,16]{1,0:T(8,128)S(1)}) custom-call(s32[16]{0:T(128)S(1)} %copy-done.4, s32[8,8]{1,0:T(8,128)S(1)} %copy-done.3, f32[256,16]{1,0:T(8,128)S(1)} %bitcast.2, ...), custom_call_target="tpu_custom_call" | custom-call | flops 92000002048 | bytes 1 | tf_op jit(solution)/shard_map/prepare/pallas_call | solution.py:80
  15.0 3.8 %collective-permute-done.2.x0 = bf16[128,2048]{1,0:T(8,128)(2,1)S(1)} collective-permute-done((bf16[128,2048]{1,0:T(8,128)(2,1)S(1)}, bf16[128,2048]{1,0:T(8,128)(2,1)S(1)}, u32[]{:S(2)}, u32[]{:S(2)}) %collective-permute-start.2) | collective-permute-done | bytes 524320 | tf_op jit(solution)/shard_map/send_a0/ppermute | solution.py:294
  18.7 2.5 %collective-permute-done.3.x1 = bf16[128,2048]{1,0:T(8,128)(2,1)S(1)} collective-permute-done((bf16[128,2048]{1,0:T(8,128)(2,1)S(1)}, bf16[128,2048]{1,0:T(8,128)(2,1)S(1)}, u32[]{:S(2)}, u32[]{:S(2)}) %collective-permute-start.3) | collective-permute-done | bytes 524320 | tf_op jit(solution)/shard_map/send_y0/ppermute | solution.py:294
  22.0 1.6 %collective-permute-start.9 = (bf16[128,2048]{1,0:T(8,128)(2,1)S(1)}, bf16[128,2048]{1,0:T(8,128)(2,1)S(1)}, u32[]{:S(2)}, u32[]{:S(2)}) collective-permute-start(bf16[128,2048]{1,0:T(8,128)(2,1)S(1)} %get-tuple-element.65.refs_4_), channel_id=1, source_target_pairs={{0,2},{1,3},{2,0},{3,1},{4,6},{5,7},{6,4},{7,5},{8,10},{9,11},{10,... | collective-permute-start | bytes 1572872 | tf_op jit(solution)/shard_map/send_ya0/ppermute | solution.py:294
  23.6 7.2 %collective-permute-done.4.x0 = bf16[128,2048]{1,0:T(8,128)(2,1)S(1)} collective-permute-done((bf16[128,2048]{1,0:T(8,128)(2,1)S(1)}, bf16[128,2048]{1,0:T(8,128)(2,1)S(1)}, u32[]{:S(2)}, u32[]{:S(2)}) %collective-permute-start.4) | collective-permute-done | bytes 524320 | tf_op jit(solution)/shard_map/send_b0/ppermute | solution.py:294
  30.8 1.6 %collective-permute-done.5.x1 = bf16[128,2048]{1,0:T(8,128)(2,1)S(1)} collective-permute-done((bf16[128,2048]{1,0:T(8,128)(2,1)S(1)}, bf16[128,2048]{1,0:T(8,128)(2,1)S(1)}, u32[]{:S(2)}, u32[]{:S(2)}) %collective-permute-start.5) | collective-permute-done | bytes 524320 | tf_op jit(solution)/shard_map/send_y1/ppermute | solution.py:294
  33.2 6.7 %halves.1 = (bf16[1024,2048]{1,0:T(8,128)(2,1)S(1)}, bf16[1024,2048]{1,0:T(8,128)(2,1)S(1)}, bf16[1024,2048]{1,0:T(8,128)(2,1)}, f32[8,128]{1,0:T(8,128)}) custom-call(bf16[1024,4096]{1,0:T(8,128)(2,1)} %train.1, bf16[1024,4096]{1,0:T(8,128)(2,1)} %collective-permute-done.1.twin_train), custom_call_target="tpu_custom_call" | custom-call | flops 1000000000 | bytes 1 | tf_op jit(solution)/shard_map/halves/pallas_call | solution.py:114
  39.9 1.5 %collective-permute-start.6 = (bf16[128,2048]{1,0:T(8,128)(2,1)S(1)}, bf16[128,2048]{1,0:T(8,128)(2,1)S(1)}, u32[]{:S(2)}, u32[]{:S(2)}) collective-permute-start(bf16[128,2048]{1,0:T(8,128)(2,1)S(1)} %get-tuple-element.65.refs_4_), channel_id=1, source_target_pairs={{0,12},{1,13},{2,14},{3,15},{4,0},{5,1},{6,2},{7,3},{8,4},{9,5},{1... | collective-permute-start | bytes 1572872 | tf_op jit(solution)/shard_map/send_f0/ppermute | solution.py:294
  41.4 1.0 %collective-permute-start.7 = (bf16[128,2048]{1,0:T(8,128)(2,1)S(1)}, bf16[128,2048]{1,0:T(8,128)(2,1)S(1)}, u32[]{:S(2)}, u32[]{:S(2)}) collective-permute-start(bf16[128,2048]{1,0:T(8,128)(2,1)S(1)} %get-tuple-element.66.refs_2_), channel_id=1, source_target_pairs={{0,2},{1,3},{2,0},{3,1},{4,6},{5,7},{6,4},{7,5},{8,10},{9,11},{10,... | collective-permute-start | bytes 1572872 | tf_op jit(solution)/shard_map/send_yb0/ppermute | solution.py:294
  42.5 2.2 %copy-done = bf16[1024,2048]{1,0:T(8,128)(2,1)S(1)} copy-done((bf16[1024,2048]{1,0:T(8,128)(2,1)S(1)}, bf16[1024,2048]{1,0:T(8,128)(2,1)}, u32[]{:S(2)}) %copy-start) | copy-done | bytes 4194328
  44.7 5.1 %stage.8 = (f32[8,128]{1,0:T(8,128)S(1)}, f32[8,4,128,128]{3,2,1,0:T(8,128)S(1)}, f32[8,4,128,128]{3,2,1,0:T(8,128)S(1)}) custom-call(s32[8,16]{1,0:T(8,128)S(1)} %get-tuple-element.51.refs_0_, bf16[1024,2048]{1,0:T(8,128)(2,1)S(1)} %get-tuple-element.53.refs_1_, bf16[128,2048]{1,0:T(8,128)(2,1)S(1)} %get-tuple-element.54.refs_2_, ...), custom_call_target="tpu_custom_call" | custom-call | flops 1150000000 | bytes 1 | tf_op jit(solution)/shard_map/stage/pallas_call | solution.py:243
  49.8 1.1 %collective-permute-start.12 = (bf16[128,2048]{1,0:T(8,128)(2,1)S(1)}, bf16[128,2048]{1,0:T(8,128)(2,1)S(1)}, u32[]{:S(2)}, u32[]{:S(2)}) collective-permute-start(bf16[128,2048]{1,0:T(8,128)(2,1)S(1)} %collective-permute-done.8.refs_4_), channel_id=1, source_target_pairs={{0,4},{1,5},{2,6},{3,7},{4,8},{5,9},{6,10},{7,11},{8,12},{9,13},{1... | collective-permute-start | bytes 1572872 | tf_op jit(solution)/shard_map/send_f1/ppermute | solution.py:294
  51.4 5.2 %stage.9 = (f32[8,128]{1,0:T(8,128)S(1)}, f32[8,4,128,128]{3,2,1,0:T(8,128)S(1)}, f32[8,8,128,128]{3,2,1,0:T(8,128)S(1)}) custom-call(s32[8,16]{1,0:T(8,128)S(1)} %get-tuple-element.51.refs_0_, bf16[1024,2048]{1,0:T(8,128)(2,1)S(1)} %get-tuple-element.53.refs_1_, bf16[128,2048]{1,0:T(8,128)(2,1)S(1)} %get-tuple-element.66.refs_2_, ...), custom_call_target="tpu_custom_call" | custom-call | flops 1150000000 | bytes 1 | tf_op jit(solution)/shard_map/stage/pallas_call | solution.py:243
  56.6 3.5 %collective-permute-start.10 = (bf16[128,2048]{1,0:T(8,128)(2,1)S(1)}, bf16[128,2048]{1,0:T(8,128)(2,1)S(1)}, u32[]{:S(2)}, u32[]{:S(2)}) collective-permute-start(bf16[128,2048]{1,0:T(8,128)(2,1)S(1)} %get-tuple-element.71.refs_3_), channel_id=1, source_target_pairs={{0,12},{1,13},{2,14},{3,15},{4,0},{5,1},{6,2},{7,3},{8,4},{9,5},{1... | collective-permute-start | bytes 1572872 | tf_op jit(solution)/shard_map/send_a1/ppermute | solution.py:294
  60.1 1.0 %collective-permute-start.11 = (bf16[128,2048]{1,0:T(8,128)(2,1)S(1)}, bf16[128,2048]{1,0:T(8,128)(2,1)S(1)}, u32[]{:S(2)}, u32[]{:S(2)}) collective-permute-start(bf16[128,2048]{1,0:T(8,128)(2,1)S(1)} %collective-permute-done.6.refs_2_), channel_id=1, source_target_pairs={{0,2},{1,3},{2,0},{3,1},{4,6},{5,7},{6,4},{7,5},{8,10},{9,11},{10,... | collective-permute-start | bytes 1572872 | tf_op jit(solution)/shard_map/send_yf0/ppermute | solution.py:294
  61.2 3.0 %stage.10 = (f32[8,128]{1,0:T(8,128)S(1)}, f32[8,2,128,128]{3,2,1,0:T(8,128)S(1)}, f32[8,2,128,128]{3,2,1,0:T(8,128)S(1)}) custom-call(s32[8,16]{1,0:T(8,128)S(1)} %get-tuple-element.51.refs_0_, bf16[1024,2048]{1,0:T(8,128)(2,1)S(1)} %get-tuple-element.53.refs_1_, bf16[128,2048]{1,0:T(8,128)(2,1)S(1)} %collective-permute-done.6.refs_2_, ...), custom_call_target="tpu_custom_call" | custom-call | flops 1150000000 | bytes 1 | tf_op jit(solution)/shard_map/stage/pallas_call | solution.py:243
  64.2 2.4 %collective-permute-done.12.refs_2_ = bf16[128,2048]{1,0:T(8,128)(2,1)S(1)} collective-permute-done((bf16[128,2048]{1,0:T(8,128)(2,1)S(1)}, bf16[128,2048]{1,0:T(8,128)(2,1)S(1)}, u32[]{:S(2)}, u32[]{:S(2)}) %collective-permute-start.12) | collective-permute-done | bytes 524320 | tf_op jit(solution)/shard_map/send_f1/ppermute | solution.py:294
  66.6 1.0 %collective-permute-done.13.refs_3_ = bf16[128,2048]{1,0:T(8,128)(2,1)S(1)} collective-permute-done((bf16[128,2048]{1,0:T(8,128)(2,1)S(1)}, bf16[128,2048]{1,0:T(8,128)(2,1)S(1)}, u32[]{:S(2)}, u32[]{:S(2)}) %collective-permute-start.13) | collective-permute-done | bytes 524320 | tf_op jit(solution)/shard_map/send_yb1/ppermute | solution.py:294
  67.5 3.0 %stage.11 = (f32[8,128]{1,0:T(8,128)S(1)}, f32[8,2,128,128]{3,2,1,0:T(8,128)S(1)}, f32[8,4,128,128]{3,2,1,0:T(8,128)S(1)}) custom-call(s32[8,16]{1,0:T(8,128)S(1)} %get-tuple-element.51.refs_0_, bf16[1024,2048]{1,0:T(8,128)(2,1)S(1)} %get-tuple-element.53.refs_1_, bf16[128,2048]{1,0:T(8,128)(2,1)S(1)} %collective-permute-done.12.refs_2_, ...), custom_call_target="tpu_custom_call" | custom-call | flops 1150000000 | bytes 1 | tf_op jit(solution)/shard_map/stage/pallas_call | solution.py:243
  70.5 1.8 %collective-permute-start.15 = (bf16[128,2048]{1,0:T(8,128)(2,1)S(1)}, bf16[128,2048]{1,0:T(8,128)(2,1)S(1)}, u32[]{:S(2)}, u32[]{:S(2)}) collective-permute-start(bf16[128,2048]{1,0:T(8,128)(2,1)S(1)} %get-tuple-element.78.refs_3_), channel_id=1, source_target_pairs={{0,12},{1,13},{2,14},{3,15},{4,0},{5,1},{6,2},{7,3},{8,4},{9,5},{1... | collective-permute-start | bytes 1572872 | tf_op jit(solution)/shard_map/send_xa1/ppermute | solution.py:294
  72.4 1.1 %collective-permute-start.16 = (bf16[128,2048]{1,0:T(8,128)(2,1)S(1)}, bf16[128,2048]{1,0:T(8,128)(2,1)S(1)}, u32[]{:S(2)}, u32[]{:S(2)}) collective-permute-start(bf16[128,2048]{1,0:T(8,128)(2,1)S(1)} %collective-permute-done.12.refs_2_), channel_id=1, source_target_pairs={{0,2},{1,3},{2,0},{3,1},{4,6},{5,7},{6,4},{7,5},{8,10},{9,11},{10,... | collective-permute-start | bytes 1572872 | tf_op jit(solution)/shard_map/send_yf1/ppermute | solution.py:294
  73.4 2.9 %collective-permute-done.10.refs_2_ = bf16[128,2048]{1,0:T(8,128)(2,1)S(1)} collective-permute-done((bf16[128,2048]{1,0:T(8,128)(2,1)S(1)}, bf16[128,2048]{1,0:T(8,128)(2,1)S(1)}, u32[]{:S(2)}, u32[]{:S(2)}) %collective-permute-start.10) | collective-permute-done | bytes 524320 | tf_op jit(solution)/shard_map/send_a1/ppermute | solution.py:294
  76.3 2.4 %collective-permute-done.11.refs_3_ = bf16[128,2048]{1,0:T(8,128)(2,1)S(1)} collective-permute-done((bf16[128,2048]{1,0:T(8,128)(2,1)S(1)}, bf16[128,2048]{1,0:T(8,128)(2,1)S(1)}, u32[]{:S(2)}, u32[]{:S(2)}) %collective-permute-start.11) | collective-permute-done | bytes 524320 | tf_op jit(solution)/shard_map/send_yf0/ppermute | solution.py:294
  78.7 3.0 %stage.12 = (f32[8,128]{1,0:T(8,128)S(1)}, f32[8,2,128,128]{3,2,1,0:T(8,128)S(1)}, f32[8,2,128,128]{3,2,1,0:T(8,128)S(1)}) custom-call(s32[8,16]{1,0:T(8,128)S(1)} %get-tuple-element.51.refs_0_, bf16[1024,2048]{1,0:T(8,128)(2,1)S(1)} %get-tuple-element.53.refs_1_, bf16[128,2048]{1,0:T(8,128)(2,1)S(1)} %collective-permute-done.10.refs_2_, ...), custom_call_target="tpu_custom_call" | custom-call | flops 1150000000 | bytes 1 | tf_op jit(solution)/shard_map/stage/pallas_call | solution.py:243
  81.8 3.1 %stage.13 = (f32[8,128]{1,0:T(8,128)S(1)}, f32[8,8,128,128]{3,2,1,0:T(8,128)}) custom-call(s32[8,16]{1,0:T(8,128)S(1)} %get-tuple-element.51.refs_0_, f32[8,4,128,128]{3,2,1,0:T(8,128)S(1)} %get-tuple-element.61.refs_1_, f32[8,8,128,128]{3,2,1,0:T(8,128)S(1)} %collective-permute-done.17.refs_2_.refs_4_, ...), custom_call_target="tpu_custom_call" | custom-call | flops 1150000000 | bytes 1 | tf_op jit(solution)/shard_map/stage/pallas_call | solution.py:243
  84.9 1.7 %collective-permute-done.15.refs_2_ = bf16[128,2048]{1,0:T(8,128)(2,1)S(1)} collective-permute-done((bf16[128,2048]{1,0:T(8,128)(2,1)S(1)}, bf16[128,2048]{1,0:T(8,128)(2,1)S(1)}, u32[]{:S(2)}, u32[]{:S(2)}) %collective-permute-start.15) | collective-permute-done | bytes 524320 | tf_op jit(solution)/shard_map/send_xa1/ppermute | solution.py:294
  86.6 1.3 %collective-permute-done.16.refs_3_ = bf16[128,2048]{1,0:T(8,128)(2,1)S(1)} collective-permute-done((bf16[128,2048]{1,0:T(8,128)(2,1)S(1)}, bf16[128,2048]{1,0:T(8,128)(2,1)S(1)}, u32[]{:S(2)}, u32[]{:S(2)}) %collective-permute-start.16) | collective-permute-done | bytes 524320 | tf_op jit(solution)/shard_map/send_yf1/ppermute | solution.py:294
  87.9 2.3 %stage.14 = (f32[8,128]{1,0:T(8,128)}, f32[8,2,128,128]{3,2,1,0:T(8,128)S(1)}) custom-call(s32[8,16]{1,0:T(8,128)S(1)} %get-tuple-element.51.refs_0_, bf16[1024,2048]{1,0:T(8,128)(2,1)S(1)} %get-tuple-element.53.refs_1_, bf16[128,2048]{1,0:T(8,128)(2,1)S(1)} %collective-permute-done.15.refs_2_, bf16[128,2048]{1,0:T(8,128)(2,1)S(1)} %collective-permute-done.16.refs_3_, ...), custom_call_target="tpu_custom_call" | custom-call | flops 13799999488 | bytes 1 | tf_op jit(solution)/shard_map/stage/pallas_call | solution.py:243
  90.2 3.6 %stage.15 = (f32[8,128]{1,0:T(8,128)}, f32[8,8,128,128]{3,2,1,0:T(8,128)}) custom-call(s32[8,16]{1,0:T(8,128)S(1)} %get-tuple-element.51.refs_0_, f32[8,4,128,128]{3,2,1,0:T(8,128)S(1)} %get-tuple-element.61.refs_1_, f32[8,2,128,128]{3,2,1,0:T(8,128)S(1)} %collective-permute-done.14.refs_2_, ...), custom_call_target="tpu_custom_call", output_to_operand_aliasing={{1}: (10, {})} | custom-call | flops 1150000000 | bytes 1 | tf_op jit(solution)/shard_map/stage/pallas_call | solution.py:243
  (34 shorter events, 6.3 us)
Async XLA Ops:
  1.3 6.7 %collective-permute-start = (bf16[128,2048]{1,0:T(8,128)(2,1)S(1)}, bf16[128,2048]{1,0:T(8,128)(2,1)S(1)}, u32[]{:S(2)}, u32[]{:S(2)}) collective-permute-start(bf16[128,2048]{1,0:T(8,128)(2,1)S(1)} %get-tuple-element.94), channel_id=1, source_target_pairs={{0,1},{1,0},{2,3},{3,2},{4,5},{5,4},{6,7},{7,6},{8,9},{9,8},{10,11... | collective-permute-start | bytes 1572872 | tf_op jit(solution)/shard_map/send_h1/ppermute | solution.py:294
  1.8 16.9 %collective-permute-start.2 = (bf16[128,2048]{1,0:T(8,128)(2,1)S(1)}, bf16[128,2048]{1,0:T(8,128)(2,1)S(1)}, u32[]{:S(2)}, u32[]{:S(2)}) collective-permute-start(bf16[128,2048]{1,0:T(8,128)(2,1)S(1)} %get-tuple-element.95.x0), channel_id=1, source_target_pairs={{0,12},{1,13},{2,14},{3,15},{4,0},{5,1},{6,2},{7,3},{8,4},{9,5},{1... | collective-permute-start | bytes 1572872 | tf_op jit(solution)/shard_map/send_a0/ppermute | solution.py:294
  6.5 14.8 %collective-permute-start.3 = (bf16[128,2048]{1,0:T(8,128)(2,1)S(1)}, bf16[128,2048]{1,0:T(8,128)(2,1)S(1)}, u32[]{:S(2)}, u32[]{:S(2)}) collective-permute-start(bf16[128,2048]{1,0:T(8,128)(2,1)S(1)} %get-tuple-element.95.x0), channel_id=1, source_target_pairs={{0,2},{1,3},{2,0},{3,1},{4,6},{5,7},{6,4},{7,5},{8,10},{9,11},{10,... | collective-permute-start | bytes 1572872 | tf_op jit(solution)/shard_map/send_y0/ppermute | solution.py:294
  8.0 22.9 %collective-permute-start.4 = (bf16[128,2048]{1,0:T(8,128)(2,1)S(1)}, bf16[128,2048]{1,0:T(8,128)(2,1)S(1)}, u32[]{:S(2)}, u32[]{:S(2)}) collective-permute-start(bf16[128,2048]{1,0:T(8,128)(2,1)S(1)} %get-tuple-element.95.x0), channel_id=1, source_target_pairs={{0,4},{1,5},{2,6},{3,7},{4,8},{5,9},{6,10},{7,11},{8,12},{9,13},{1... | collective-permute-start | bytes 1572872 | tf_op jit(solution)/shard_map/send_b0/ppermute | solution.py:294
  8.0 25.2 %collective-permute-start.1 = (bf16[1024,4096]{1,0:T(8,128)(2,1)}, bf16[1024,4096]{1,0:T(8,128)(2,1)}, u32[]{:S(2)}, u32[]{:S(2)}) collective-permute-start(bf16[1024,4096]{1,0:T(8,128)(2,1)} %train.1), channel_id=1, source_target_pairs={{0,1},{1,0},{2,3},{3,2},{4,5},{5,4},{6,7},{7,6},{8,9},{9,8},{10,11... | collective-permute-start | bytes 25165832 | tf_op jit(solution)/shard_map/send_train/ppermute | solution.py:294
  8.0 24.5 %collective-permute-start.5 = (bf16[128,2048]{1,0:T(8,128)(2,1)S(1)}, bf16[128,2048]{1,0:T(8,128)(2,1)S(1)}, u32[]{:S(2)}, u32[]{:S(2)}) collective-permute-start(bf16[128,2048]{1,0:T(8,128)(2,1)S(1)} %collective-permute-done.x1), channel_id=1, source_target_pairs={{0,2},{1,3},{2,0},{3,1},{4,6},{5,7},{6,4},{7,5},{8,10},{9,11},{10,... | collective-permute-start | bytes 1572872 | tf_op jit(solution)/shard_map/send_y1/ppermute | solution.py:294
  8.6 0.9 copy-start.1
  9.5 0.9 copy-start.2
  10.4 0.7 copy-start.3
  11.1 0.7 copy-start.4
  21.9 27.9 %collective-permute-start.8 = (bf16[128,2048]{1,0:T(8,128)(2,1)S(1)}, bf16[128,2048]{1,0:T(8,128)(2,1)S(1)}, u32[]{:S(2)}, u32[]{:S(2)}) collective-permute-start(bf16[128,2048]{1,0:T(8,128)(2,1)S(1)} %get-tuple-element.71.refs_3_), channel_id=1, source_target_pairs={{0,4},{1,5},{2,6},{3,7},{4,8},{5,9},{6,10},{7,11},{8,12},{9,13},{1... | collective-permute-start | bytes 1572872 | tf_op jit(solution)/shard_map/send_b1/ppermute | solution.py:294
  22.0 27.8 %collective-permute-start.9 = (bf16[128,2048]{1,0:T(8,128)(2,1)S(1)}, bf16[128,2048]{1,0:T(8,128)(2,1)S(1)}, u32[]{:S(2)}, u32[]{:S(2)}) collective-permute-start(bf16[128,2048]{1,0:T(8,128)(2,1)S(1)} %get-tuple-element.65.refs_4_), channel_id=1, source_target_pairs={{0,2},{1,3},{2,0},{3,1},{4,6},{5,7},{6,4},{7,5},{8,10},{9,11},{10,... | collective-permute-start | bytes 1572872 | tf_op jit(solution)/shard_map/send_ya0/ppermute | solution.py:294
  39.9 16.7 %collective-permute-start.6 = (bf16[128,2048]{1,0:T(8,128)(2,1)S(1)}, bf16[128,2048]{1,0:T(8,128)(2,1)S(1)}, u32[]{:S(2)}, u32[]{:S(2)}) collective-permute-start(bf16[128,2048]{1,0:T(8,128)(2,1)S(1)} %get-tuple-element.65.refs_4_), channel_id=1, source_target_pairs={{0,12},{1,13},{2,14},{3,15},{4,0},{5,1},{6,2},{7,3},{8,4},{9,5},{1... | collective-permute-start | bytes 1572872 | tf_op jit(solution)/shard_map/send_f0/ppermute | solution.py:294
  41.4 15.2 %collective-permute-start.7 = (bf16[128,2048]{1,0:T(8,128)(2,1)S(1)}, bf16[128,2048]{1,0:T(8,128)(2,1)S(1)}, u32[]{:S(2)}, u32[]{:S(2)}) collective-permute-start(bf16[128,2048]{1,0:T(8,128)(2,1)S(1)} %get-tuple-element.66.refs_2_), channel_id=1, source_target_pairs={{0,2},{1,3},{2,0},{3,1},{4,6},{5,7},{6,4},{7,5},{8,10},{9,11},{10,... | collective-permute-start | bytes 1572872 | tf_op jit(solution)/shard_map/send_yb0/ppermute | solution.py:294
  42.5 2.2 %copy-start = (bf16[1024,2048]{1,0:T(8,128)(2,1)S(1)}, bf16[1024,2048]{1,0:T(8,128)(2,1)}, u32[]{:S(2)}) copy-start(bf16[1024,2048]{1,0:T(8,128)(2,1)} %get-tuple-element.60.refs_6_.refs_4_) | copy-start | bytes 12582916
  49.8 16.8 %collective-permute-start.12 = (bf16[128,2048]{1,0:T(8,128)(2,1)S(1)}, bf16[128,2048]{1,0:T(8,128)(2,1)S(1)}, u32[]{:S(2)}, u32[]{:S(2)}) collective-permute-start(bf16[128,2048]{1,0:T(8,128)(2,1)S(1)} %collective-permute-done.8.refs_4_), channel_id=1, source_target_pairs={{0,4},{1,5},{2,6},{3,7},{4,8},{5,9},{6,10},{7,11},{8,12},{9,13},{1... | collective-permute-start | bytes 1572872 | tf_op jit(solution)/shard_map/send_f1/ppermute | solution.py:294
  50.9 16.6 %collective-permute-start.13 = (bf16[128,2048]{1,0:T(8,128)(2,1)S(1)}, bf16[128,2048]{1,0:T(8,128)(2,1)S(1)}, u32[]{:S(2)}, u32[]{:S(2)}) collective-permute-start(bf16[128,2048]{1,0:T(8,128)(2,1)S(1)} %collective-permute-done.8.refs_4_), channel_id=1, source_target_pairs={{0,2},{1,3},{2,0},{3,1},{4,6},{5,7},{6,4},{7,5},{8,10},{9,11},{10,... | collective-permute-start | bytes 1572872 | tf_op jit(solution)/shard_map/send_yb1/ppermute | solution.py:294
  56.6 19.7 %collective-permute-start.10 = (bf16[128,2048]{1,0:T(8,128)(2,1)S(1)}, bf16[128,2048]{1,0:T(8,128)(2,1)S(1)}, u32[]{:S(2)}, u32[]{:S(2)}) collective-permute-start(bf16[128,2048]{1,0:T(8,128)(2,1)S(1)} %get-tuple-element.71.refs_3_), channel_id=1, source_target_pairs={{0,12},{1,13},{2,14},{3,15},{4,0},{5,1},{6,2},{7,3},{8,4},{9,5},{1... | collective-permute-start | bytes 1572872 | tf_op jit(solution)/shard_map/send_a1/ppermute | solution.py:294
  60.1 18.6 %collective-permute-start.11 = (bf16[128,2048]{1,0:T(8,128)(2,1)S(1)}, bf16[128,2048]{1,0:T(8,128)(2,1)S(1)}, u32[]{:S(2)}, u32[]{:S(2)}) collective-permute-start(bf16[128,2048]{1,0:T(8,128)(2,1)S(1)} %collective-permute-done.6.refs_2_), channel_id=1, source_target_pairs={{0,2},{1,3},{2,0},{3,1},{4,6},{5,7},{6,4},{7,5},{8,10},{9,11},{10,... | collective-permute-start | bytes 1572872 | tf_op jit(solution)/shard_map/send_yf0/ppermute | solution.py:294
  61.2 20.6 %collective-permute-start.17 = (f32[8,8,128,128]{3,2,1,0:T(8,128)S(1)}, f32[8,8,128,128]{3,2,1,0:T(8,128)S(1)}, u32[]{:S(2)}, u32[]{:S(2)}) collective-permute-start(f32[8,8,128,128]{3,2,1,0:T(8,128)S(1)} %get-tuple-element.80), channel_id=1, source_target_pairs={{0,1},{1,0},{2,3},{3,2},{4,5},{5,4},{6,7},{7,6},{8,9},{9,8},{10,11... | collective-permute-start | bytes 12582920 | tf_op jit(solution)/shard_map/send_part4/ppermute | solution.py:294
  70.5 16.0 %collective-permute-start.15 = (bf16[128,2048]{1,0:T(8,128)(2,1)S(1)}, bf16[128,2048]{1,0:T(8,128)(2,1)S(1)}, u32[]{:S(2)}, u32[]{:S(2)}) collective-permute-start(bf16[128,2048]{1,0:T(8,128)(2,1)S(1)} %get-tuple-element.78.refs_3_), channel_id=1, source_target_pairs={{0,12},{1,13},{2,14},{3,15},{4,0},{5,1},{6,2},{7,3},{8,4},{9,5},{1... | collective-permute-start | bytes 1572872 | tf_op jit(solution)/shard_map/send_xa1/ppermute | solution.py:294
  72.4 15.5 %collective-permute-start.16 = (bf16[128,2048]{1,0:T(8,128)(2,1)S(1)}, bf16[128,2048]{1,0:T(8,128)(2,1)S(1)}, u32[]{:S(2)}, u32[]{:S(2)}) collective-permute-start(bf16[128,2048]{1,0:T(8,128)(2,1)S(1)} %collective-permute-done.12.refs_2_), channel_id=1, source_target_pairs={{0,2},{1,3},{2,0},{3,1},{4,6},{5,7},{6,4},{7,5},{8,10},{9,11},{10,... | collective-permute-start | bytes 1572872 | tf_op jit(solution)/shard_map/send_yf1/ppermute | solution.py:294
  76.3 5.4 %collective-permute-start.18 = (f32[8,4,128,128]{3,2,1,0:T(8,128)S(1)}, f32[8,4,128,128]{3,2,1,0:T(8,128)S(1)}, u32[]{:S(2)}, u32[]{:S(2)}) collective-permute-start(f32[8,4,128,128]{3,2,1,0:T(8,128)S(1)} %get-tuple-element.84), channel_id=1, source_target_pairs={{0,1},{1,0},{2,3},{3,2},{4,5},{5,4},{6,7},{7,6},{8,9},{9,8},{10,11... | collective-permute-start | bytes 6291464 | tf_op jit(solution)/shard_map/send_part6/ppermute | solution.py:294
  81.7 8.5 %collective-permute-start.14 = (f32[8,2,128,128]{3,2,1,0:T(8,128)S(1)}, f32[8,2,128,128]{3,2,1,0:T(8,128)S(1)}, u32[]{:S(2)}, u32[]{:S(2)}) collective-permute-start(f32[8,2,128,128]{3,2,1,0:T(8,128)S(1)} %get-tuple-element.77), channel_id=1, source_target_pairs={{0,1},{1,0},{2,3},{3,2},{4,5},{5,4},{6,7},{7,6},{8,9},{9,8},{10,11... | collective-permute-start | bytes 3145736 | tf_op jit(solution)/shard_map/send_part7/ppermute | solution.py:294
  86.6 3.6 %collective-permute-start.19 = (bf16[128,2048]{1,0:T(8,128)(2,1)S(1)}, bf16[128,2048]{1,0:T(8,128)(2,1)S(1)}, u32[]{:S(2)}, u32[]{:S(2)}) collective-permute-start(bf16[128,2048]{1,0:T(8,128)(2,1)S(1)} %collective-permute-done.15.refs_2_), channel_id=1, source_target_pairs={{0,1},{1,0},{2,3},{3,2},{4,5},{5,4},{6,7},{7,6},{8,9},{9,8},{10,11... | collective-permute-start | bytes 1572872 | tf_op jit(solution)/shard_map/send_cxa1/ppermute | solution.py:294
  87.9 2.3 %collective-permute-start.20 = (bf16[128,2048]{1,0:T(8,128)(2,1)S(1)}, bf16[128,2048]{1,0:T(8,128)(2,1)S(1)}, u32[]{:S(2)}, u32[]{:S(2)}) collective-permute-start(bf16[128,2048]{1,0:T(8,128)(2,1)S(1)} %collective-permute-done.16.refs_3_), channel_id=1, source_target_pairs={{0,1},{1,0},{2,3},{3,2},{4,5},{5,4},{6,7},{7,6},{8,9},{9,8},{10,11... | collective-permute-start | bytes 1572872 | tf_op jit(solution)/shard_map/send_cyf1/ppermute | solution.py:294

commit v7 on v6

--- a/solution.py
+++ b/solution.py
@@ -174,9 +174,9 @@
         for t in range(table.shape[0]):
             put(t, job, arrays[ours][t, j] + arrays[theirs][t, k])
 
-    step = 2 * BLK
     for (train, pieces, sums, before), part in zip(products, parts):
         skip = 0
+        step = 8 * BLK if sums else 2 * BLK
         if before is not None:
             skip = arrays[before].shape[1]
             part[:, :skip] = arrays[before][...]
@@ -310,7 +310,7 @@
     ]
     work = {3: ["h0", "h1", "a0", "y0"], 4: ["b0", "y1", "b1", "ya0"], 5: ["f0", "yb0"], 6: ["f1", "yb1"], 7: ["a1", "yf0"]}
     exchange = (4, 6, 7)
-    cost = {3: 1, 4: 1, 5: 1, 6: 1, 7: 1, 8: 12, 9: 1}
+    cost = {3: 2, 4: 2, 5: 2, 6: 2, 7: 2, 8: 12, 9: 1}
     stand_cost = 60
     slots = pair_query.shape[1]
     half = query_grads.shape[1] // 2

time: 94.3 us -> 94.3 us (level)
  no operation moved by 1% of the time
where the time goes in v7:
time: 94.3 us; the launch traced here: 94 us
  Pallas kernels  39.4 us (42%)
  waiting for transfers between devices  27 us (29%)
  starting transfers between devices  20.6 us (22%)
  local copies, waits for them, and re-layouts  5.34 us (6%)
  other arithmetic  1.27 us (1%)
    pallas_call x8, Pallas kernels, stage(): pl.pallas_call(body, out_shape=shapes, in_specs=specs, out_specs=out_spec...  28.1 us
    ppermute x21, waiting for transfers between devices, send(): return lax.ppermute(x, 'rows', perm)  27 us
    ppermute x21, starting transfers between devices, send(): return lax.ppermute(x, 'rows', perm)  20.6 us
    pallas_call x1, Pallas kernels, make_halves(): pl.pallas_call(halves_kernel, out_shape=[side] * 3 + [jax.ShapeDtypeStruc...  6.71 us
    unnamed x10, local copies, waits for them, and re-layouts  5.34 us
    pallas_call x1, Pallas kernels, prepare(): pl.pallas_call(functools.partial(prepare_kernel, layers), out_shape=[fact...  3.23 us
  transfers between devices with their start and end apart: 21, of which 10 were waited for; matrix products, arithmetic and copies ran while one was open for 0% of the time, Pallas kernels for 38%

profile of v7, /device:TPU:0, one launch (start us, length us, event | category | flops | bytes accessed | tf_op | source)
XLA Modules:
  0.0 94.0 jit_solution(5028204641251321546)
XLA Ops:
  0.0 1.3 %broadcast_select_fusion = (bf16[128,2048]{1,0:T(8,128)(2,1)S(1)}, bf16[128,2048]{1,0:T(8,128)(2,1)S(1)}) fusion(pred[]{:T(512)S(6)} %eq.6, bf16[128,4096]{1,0:T(8,128)(2,1)} %param.7), kind=kLoop, calls=%fused_computation | loop fusion | flops 524288 | bytes 2097153 | tf_op jit(solution)/shard_map/jit(_where)/select_n | solution.py:320
  1.8 4.7 %collective-permute-start.2 = (bf16[128,2048]{1,0:T(8,128)(2,1)S(1)}, bf16[128,2048]{1,0:T(8,128)(2,1)S(1)}, u32[]{:S(2)}, u32[]{:S(2)}) collective-permute-start(bf16[128,2048]{1,0:T(8,128)(2,1)S(1)} %get-tuple-element.95.x0), channel_id=1, source_target_pairs={{0,12},{1,13},{2,14},{3,15},{4,0},{5,1},{6,2},{7,3},{8,4},{9,5},{1... | collective-permute-start | bytes 1572872 | tf_op jit(solution)/shard_map/send_a0/ppermute | solution.py:294
  6.5 1.5 %collective-permute-start.3 = (bf16[128,2048]{1,0:T(8,128)(2,1)S(1)}, bf16[128,2048]{1,0:T(8,128)(2,1)S(1)}, u32[]{:S(2)}, u32[]{:S(2)}) collective-permute-start(bf16[128,2048]{1,0:T(8,128)(2,1)S(1)} %get-tuple-element.95.x0), channel_id=1, source_target_pairs={{0,2},{1,3},{2,0},{3,1},{4,6},{5,7},{6,4},{7,5},{8,10},{9,11},{10,... | collective-permute-start | bytes 1572872 | tf_op jit(solution)/shard_map/send_y0/ppermute | solution.py:294
  11.7 3.2 %prepare.1 = (bf16[8,256,256]{2,1,0:T(8,128)(2,1)S(1)}, bf16[8,256,256]{2,1,0:T(8,128)(2,1)S(1)}, bf16[128,2048]{1,0:T(8,128)(2,1)S(1)}, bf16[128,2048]{1,0:T(8,128)(2,1)S(1)}, s32[8,16]{1,0:T(8,128)S(1)}) custom-call(s32[16]{0:T(128)S(1)} %copy-done.4, s32[8,8]{1,0:T(8,128)S(1)} %copy-done.3, f32[256,16]{1,0:T(8,128)S(1)} %bitcast.2, ...), custom_call_target="tpu_custom_call" | custom-call | flops 92000002048 | bytes 1 | tf_op jit(solution)/shard_map/prepare/pallas_call | solution.py:80
  15.0 3.8 %collective-permute-done.2.x0 = bf16[128,2048]{1,0:T(8,128)(2,1)S(1)} collective-permute-done((bf16[128,2048]{1,0:T(8,128)(2,1)S(1)}, bf16[128,2048]{1,0:T(8,128)(2,1)S(1)}, u32[]{:S(2)}, u32[]{:S(2)}) %collective-permute-start.2) | collective-permute-done | bytes 524320 | tf_op jit(solution)/shard_map/send_a0/ppermute | solution.py:294
  18.7 2.5 %collective-permute-done.3.x1 = bf16[128,2048]{1,0:T(8,128)(2,1)S(1)} collective-permute-done((bf16[128,2048]{1,0:T(8,128)(2,1)S(1)}, bf16[128,2048]{1,0:T(8,128)(2,1)S(1)}, u32[]{:S(2)}, u32[]{:S(2)}) %collective-permute-start.3) | collective-permute-done | bytes 524320 | tf_op jit(solution)/shard_map/send_y0/ppermute | solution.py:294
  22.0 1.6 %collective-permute-start.9 = (bf16[128,2048]{1,0:T(8,128)(2,1)S(1)}, bf16[128,2048]{1,0:T(8,128)(2,1)S(1)}, u32[]{:S(2)}, u32[]{:S(2)}) collective-permute-start(bf16[128,2048]{1,0:T(8,128)(2,1)S(1)} %get-tuple-element.65.refs_4_), channel_id=1, source_target_pairs={{0,2},{1,3},{2,0},{3,1},{4,6},{5,7},{6,4},{7,5},{8,10},{9,11},{10,... | collective-permute-start | bytes 1572872 | tf_op jit(solution)/shard_map/send_ya0/ppermute | solution.py:294
  23.6 7.2 %collective-permute-done.4.x0 = bf16[128,2048]{1,0:T(8,128)(2,1)S(1)} collective-permute-done((bf16[128,2048]{1,0:T(8,128)(2,1)S(1)}, bf16[128,2048]{1,0:T(8,128)(2,1)S(1)}, u32[]{:S(2)}, u32[]{:S(2)}) %collective-permute-start.4) | collective-permute-done | bytes 524320 | tf_op jit(solution)/shard_map/send_b0/ppermute | solution.py:294
  30.8 1.6 %collective-permute-done.5.x1 = bf16[128,2048]{1,0:T(8,128)(2,1)S(1)} collective-permute-done((bf16[128,2048]{1,0:T(8,128)(2,1)S(1)}, bf16[128,2048]{1,0:T(8,128)(2,1)S(1)}, u32[]{:S(2)}, u32[]{:S(2)}) %collective-permute-start.5) | collective-permute-done | bytes 524320 | tf_op jit(solution)/shard_map/send_y1/ppermute | solution.py:294
  33.2 6.7 %halves.1 = (bf16[1024,2048]{1,0:T(8,128)(2,1)S(1)}, bf16[1024,2048]{1,0:T(8,128)(2,1)S(1)}, bf16[1024,2048]{1,0:T(8,128)(2,1)}, f32[8,128]{1,0:T(8,128)}) custom-call(bf16[1024,4096]{1,0:T(8,128)(2,1)} %train.1, bf16[1024,4096]{1,0:T(8,128)(2,1)} %collective-permute-done.1.twin_train), custom_call_target="tpu_custom_call" | custom-call | flops 1000000000 | bytes 1 | tf_op jit(solution)/shard_map/halves/pallas_call | solution.py:114
  39.9 1.5 %collective-permute-start.6 = (bf16[128,2048]{1,0:T(8,128)(2,1)S(1)}, bf16[128,2048]{1,0:T(8,128)(2,1)S(1)}, u32[]{:S(2)}, u32[]{:S(2)}) collective-permute-start(bf16[128,2048]{1,0:T(8,128)(2,1)S(1)} %get-tuple-element.65.refs_4_), channel_id=1, source_target_pairs={{0,12},{1,13},{2,14},{3,15},{4,0},{5,1},{6,2},{7,3},{8,4},{9,5},{1... | collective-permute-start | bytes 1572872 | tf_op jit(solution)/shard_map/send_f0/ppermute | solution.py:294
  41.4 1.0 %collective-permute-start.7 = (bf16[128,2048]{1,0:T(8,128)(2,1)S(1)}, bf16[128,2048]{1,0:T(8,128)(2,1)S(1)}, u32[]{:S(2)}, u32[]{:S(2)}) collective-permute-start(bf16[128,2048]{1,0:T(8,128)(2,1)S(1)} %get-tuple-element.66.refs_2_), channel_id=1, source_target_pairs={{0,2},{1,3},{2,0},{3,1},{4,6},{5,7},{6,4},{7,5},{8,10},{9,11},{10,... | collective-permute-start | bytes 1572872 | tf_op jit(solution)/shard_map/send_yb0/ppermute | solution.py:294
  42.5 2.2 %copy-done = bf16[1024,2048]{1,0:T(8,128)(2,1)S(1)} copy-done((bf16[1024,2048]{1,0:T(8,128)(2,1)S(1)}, bf16[1024,2048]{1,0:T(8,128)(2,1)}, u32[]{:S(2)}) %copy-start) | copy-done | bytes 4194328
  44.7 5.1 %stage.8 = (f32[8,128]{1,0:T(8,128)S(1)}, f32[8,4,128,128]{3,2,1,0:T(8,128)S(1)}, f32[8,4,128,128]{3,2,1,0:T(8,128)S(1)}) custom-call(s32[8,16]{1,0:T(8,128)S(1)} %get-tuple-element.51.refs_0_, bf16[1024,2048]{1,0:T(8,128)(2,1)S(1)} %get-tuple-element.53.refs_1_, bf16[128,2048]{1,0:T(8,128)(2,1)S(1)} %get-tuple-element.54.refs_2_, ...), custom_call_target="tpu_custom_call" | custom-call | flops 2300000000 | bytes 1 | tf_op jit(solution)/shard_map/stage/pallas_call | solution.py:243
  49.8 1.1 %collective-permute-start.12 = (bf16[128,2048]{1,0:T(8,128)(2,1)S(1)}, bf16[128,2048]{1,0:T(8,128)(2,1)S(1)}, u32[]{:S(2)}, u32[]{:S(2)}) collective-permute-start(bf16[128,2048]{1,0:T(8,128)(2,1)S(1)} %collective-permute-done.8.refs_4_), channel_id=1, source_target_pairs={{0,4},{1,5},{2,6},{3,7},{4,8},{5,9},{6,10},{7,11},{8,12},{9,13},{1... | collective-permute-start | bytes 1572872 | tf_op jit(solution)/shard_map/send_f1/ppermute | solution.py:294
  51.4 5.2 %stage.9 = (f32[8,128]{1,0:T(8,128)S(1)}, f32[8,4,128,128]{3,2,1,0:T(8,128)S(1)}, f32[8,8,128,128]{3,2,1,0:T(8,128)S(1)}) custom-call(s32[8,16]{1,0:T(8,128)S(1)} %get-tuple-element.51.refs_0_, bf16[1024,2048]{1,0:T(8,128)(2,1)S(1)} %get-tuple-element.53.refs_1_, bf16[128,2048]{1,0:T(8,128)(2,1)S(1)} %get-tuple-element.66.refs_2_, ...), custom_call_target="tpu_custom_call" | custom-call | flops 2300000000 | bytes 1 | tf_op jit(solution)/shard_map/stage/pallas_call | solution.py:243
  56.6 3.5 %collective-permute-start.10 = (bf16[128,2048]{1,0:T(8,128)(2,1)S(1)}, bf16[128,2048]{1,0:T(8,128)(2,1)S(1)}, u32[]{:S(2)}, u32[]{:S(2)}) collective-permute-start(bf16[128,2048]{1,0:T(8,128)(2,1)S(1)} %get-tuple-element.71.refs_3_), channel_id=1, source_target_pairs={{0,12},{1,13},{2,14},{3,15},{4,0},{5,1},{6,2},{7,3},{8,4},{9,5},{1... | collective-permute-start | bytes 1572872 | tf_op jit(solution)/shard_map/send_a1/ppermute | solution.py:294
  60.1 1.0 %collective-permute-start.11 = (bf16[128,2048]{1,0:T(8,128)(2,1)S(1)}, bf16[128,2048]{1,0:T(8,128)(2,1)S(1)}, u32[]{:S(2)}, u32[]{:S(2)}) collective-permute-start(bf16[128,2048]{1,0:T(8,128)(2,1)S(1)} %collective-permute-done.6.refs_2_), channel_id=1, source_target_pairs={{0,2},{1,3},{2,0},{3,1},{4,6},{5,7},{6,4},{7,5},{8,10},{9,11},{10,... | collective-permute-start | bytes 1572872 | tf_op jit(solution)/shard_map/send_yf0/ppermute | solution.py:294
  61.2 3.0 %stage.10 = (f32[8,128]{1,0:T(8,128)S(1)}, f32[8,2,128,128]{3,2,1,0:T(8,128)S(1)}, f32[8,2,128,128]{3,2,1,0:T(8,128)S(1)}) custom-call(s32[8,16]{1,0:T(8,128)S(1)} %get-tuple-element.51.refs_0_, bf16[1024,2048]{1,0:T(8,128)(2,1)S(1)} %get-tuple-element.53.refs_1_, bf16[128,2048]{1,0:T(8,128)(2,1)S(1)} %collective-permute-done.6.refs_2_, ...), custom_call_target="tpu_custom_call" | custom-call | flops 2300000000 | bytes 1 | tf_op jit(solution)/shard_map/stage/pallas_call | solution.py:243
  64.2 2.4 %collective-permute-done.12.refs_2_ = bf16[128,2048]{1,0:T(8,128)(2,1)S(1)} collective-permute-done((bf16[128,2048]{1,0:T(8,128)(2,1)S(1)}, bf16[128,2048]{1,0:T(8,128)(2,1)S(1)}, u32[]{:S(2)}, u32[]{:S(2)}) %collective-permute-start.12) | collective-permute-done | bytes 524320 | tf_op jit(solution)/shard_map/send_f1/ppermute | solution.py:294
  66.6 1.0 %collective-permute-done.13.refs_3_ = bf16[128,2048]{1,0:T(8,128)(2,1)S(1)} collective-permute-done((bf16[128,2048]{1,0:T(8,128)(2,1)S(1)}, bf16[128,2048]{1,0:T(8,128)(2,1)S(1)}, u32[]{:S(2)}, u32[]{:S(2)}) %collective-permute-start.13) | collective-permute-done | bytes 524320 | tf_op jit(solution)/shard_map/send_yb1/ppermute | solution.py:294
  67.5 3.0 %stage.11 = (f32[8,128]{1,0:T(8,128)S(1)}, f32[8,2,128,128]{3,2,1,0:T(8,128)S(1)}, f32[8,4,128,128]{3,2,1,0:T(8,128)S(1)}) custom-call(s32[8,16]{1,0:T(8,128)S(1)} %get-tuple-element.51.refs_0_, bf16[1024,2048]{1,0:T(8,128)(2,1)S(1)} %get-tuple-element.53.refs_1_, bf16[128,2048]{1,0:T(8,128)(2,1)S(1)} %collective-permute-done.12.refs_2_, ...), custom_call_target="tpu_custom_call" | custom-call | flops 2300000000 | bytes 1 | tf_op jit(solution)/shard_map/stage/pallas_call | solution.py:243
  70.5 1.8 %collective-permute-start.15 = (bf16[128,2048]{1,0:T(8,128)(2,1)S(1)}, bf16[128,2048]{1,0:T(8,128)(2,1)S(1)}, u32[]{:S(2)}, u32[]{:S(2)}) collective-permute-start(bf16[128,2048]{1,0:T(8,128)(2,1)S(1)} %get-tuple-element.78.refs_3_), channel_id=1, source_target_pairs={{0,12},{1,13},{2,14},{3,15},{4,0},{5,1},{6,2},{7,3},{8,4},{9,5},{1... | collective-permute-start | bytes 1572872 | tf_op jit(solution)/shard_map/send_xa1/ppermute | solution.py:294
  72.4 1.1 %collective-permute-start.16 = (bf16[128,2048]{1,0:T(8,128)(2,1)S(1)}, bf16[128,2048]{1,0:T(8,128)(2,1)S(1)}, u32[]{:S(2)}, u32[]{:S(2)}) collective-permute-start(bf16[128,2048]{1,0:T(8,128)(2,1)S(1)} %collective-permute-done.12.refs_2_), channel_id=1, source_target_pairs={{0,2},{1,3},{2,0},{3,1},{4,6},{5,7},{6,4},{7,5},{8,10},{9,11},{10,... | collective-permute-start | bytes 1572872 | tf_op jit(solution)/shard_map/send_yf1/ppermute | solution.py:294
  73.4 2.9 %collective-permute-done.10.refs_2_ = bf16[128,2048]{1,0:T(8,128)(2,1)S(1)} collective-permute-done((bf16[128,2048]{1,0:T(8,128)(2,1)S(1)}, bf16[128,2048]{1,0:T(8,128)(2,1)S(1)}, u32[]{:S(2)}, u32[]{:S(2)}) %collective-permute-start.10) | collective-permute-done | bytes 524320 | tf_op jit(solution)/shard_map/send_a1/ppermute | solution.py:294
  76.3 2.4 %collective-permute-done.11.refs_3_ = bf16[128,2048]{1,0:T(8,128)(2,1)S(1)} collective-permute-done((bf16[128,2048]{1,0:T(8,128)(2,1)S(1)}, bf16[128,2048]{1,0:T(8,128)(2,1)S(1)}, u32[]{:S(2)}, u32[]{:S(2)}) %collective-permute-start.11) | collective-permute-done | bytes 524320 | tf_op jit(solution)/shard_map/send_yf0/ppermute | solution.py:294
  78.7 3.0 %stage.12 = (f32[8,128]{1,0:T(8,128)S(1)}, f32[8,2,128,128]{3,2,1,0:T(8,128)S(1)}, f32[8,2,128,128]{3,2,1,0:T(8,128)S(1)}) custom-call(s32[8,16]{1,0:T(8,128)S(1)} %get-tuple-element.51.refs_0_, bf16[1024,2048]{1,0:T(8,128)(2,1)S(1)} %get-tuple-element.53.refs_1_, bf16[128,2048]{1,0:T(8,128)(2,1)S(1)} %collective-permute-done.10.refs_2_, ...), custom_call_target="tpu_custom_call" | custom-call | flops 2300000000 | bytes 1 | tf_op jit(solution)/shard_map/stage/pallas_call | solution.py:243
  81.8 2.9 %stage.13 = (f32[8,128]{1,0:T(8,128)S(1)}, f32[8,8,128,128]{3,2,1,0:T(8,128)}) custom-call(s32[8,16]{1,0:T(8,128)S(1)} %get-tuple-element.51.refs_0_, f32[8,4,128,128]{3,2,1,0:T(8,128)S(1)} %get-tuple-element.61.refs_1_, f32[8,8,128,128]{3,2,1,0:T(8,128)S(1)} %collective-permute-done.17.refs_2_.refs_4_, ...), custom_call_target="tpu_custom_call" | custom-call | flops 1150000000 | bytes 1 | tf_op jit(solution)/shard_map/stage/pallas_call | solution.py:243
  84.6 1.9 %collective-permute-done.15.refs_2_ = bf16[128,2048]{1,0:T(8,128)(2,1)S(1)} collective-permute-done((bf16[128,2048]{1,0:T(8,128)(2,1)S(1)}, bf16[128,2048]{1,0:T(8,128)(2,1)S(1)}, u32[]{:S(2)}, u32[]{:S(2)}) %collective-permute-start.15) | collective-permute-done | bytes 524320 | tf_op jit(solution)/shard_map/send_xa1/ppermute | solution.py:294
  86.6 1.3 %collective-permute-done.16.refs_3_ = bf16[128,2048]{1,0:T(8,128)(2,1)S(1)} collective-permute-done((bf16[128,2048]{1,0:T(8,128)(2,1)S(1)}, bf16[128,2048]{1,0:T(8,128)(2,1)S(1)}, u32[]{:S(2)}, u32[]{:S(2)}) %collective-permute-start.16) | collective-permute-done | bytes 524320 | tf_op jit(solution)/shard_map/send_yf1/ppermute | solution.py:294
  87.9 2.3 %stage.14 = (f32[8,128]{1,0:T(8,128)}, f32[8,2,128,128]{3,2,1,0:T(8,128)S(1)}) custom-call(s32[8,16]{1,0:T(8,128)S(1)} %get-tuple-element.51.refs_0_, bf16[1024,2048]{1,0:T(8,128)(2,1)S(1)} %get-tuple-element.53.refs_1_, bf16[128,2048]{1,0:T(8,128)(2,1)S(1)} %collective-permute-done.15.refs_2_, bf16[128,2048]{1,0:T(8,128)(2,1)S(1)} %collective-permute-done.16.refs_3_, ...), custom_call_target="tpu_custom_call" | custom-call | flops 13799999488 | bytes 1 | tf_op jit(solution)/shard_map/stage/pallas_call | solution.py:243
  90.2 3.6 %stage.15 = (f32[8,128]{1,0:T(8,128)}, f32[8,8,128,128]{3,2,1,0:T(8,128)}) custom-call(s32[8,16]{1,0:T(8,128)S(1)} %get-tuple-element.51.refs_0_, f32[8,4,128,128]{3,2,1,0:T(8,128)S(1)} %get-tuple-element.61.refs_1_, f32[8,2,128,128]{3,2,1,0:T(8,128)S(1)} %collective-permute-done.14.refs_2_, ...), custom_call_target="tpu_custom_call", output_to_operand_aliasing={{1}: (10, {})} | custom-call | flops 1150000000 | bytes 1 | tf_op jit(solution)/shard_map/stage/pallas_call | solution.py:243
  (34 shorter events, 6.3 us)
Async XLA Ops:
  1.3 6.7 %collective-permute-start = (bf16[128,2048]{1,0:T(8,128)(2,1)S(1)}, bf16[128,2048]{1,0:T(8,128)(2,1)S(1)}, u32[]{:S(2)}, u32[]{:S(2)}) collective-permute-start(bf16[128,2048]{1,0:T(8,128)(2,1)S(1)} %get-tuple-element.94), channel_id=1, source_target_pairs={{0,1},{1,0},{2,3},{3,2},{4,5},{5,4},{6,7},{7,6},{8,9},{9,8},{10,11... | collective-permute-start | bytes 1572872 | tf_op jit(solution)/shard_map/send_h1/ppermute | solution.py:294
  1.8 16.9 %collective-permute-start.2 = (bf16[128,2048]{1,0:T(8,128)(2,1)S(1)}, bf16[128,2048]{1,0:T(8,128)(2,1)S(1)}, u32[]{:S(2)}, u32[]{:S(2)}) collective-permute-start(bf16[128,2048]{1,0:T(8,128)(2,1)S(1)} %get-tuple-element.95.x0), channel_id=1, source_target_pairs={{0,12},{1,13},{2,14},{3,15},{4,0},{5,1},{6,2},{7,3},{8,4},{9,5},{1... | collective-permute-start | bytes 1572872 | tf_op jit(solution)/shard_map/send_a0/ppermute | solution.py:294
  6.5 14.8 %collective-permute-start.3 = (bf16[128,2048]{1,0:T(8,128)(2,1)S(1)}, bf16[128,2048]{1,0:T(8,128)(2,1)S(1)}, u32[]{:S(2)}, u32[]{:S(2)}) collective-permute-start(bf16[128,2048]{1,0:T(8,128)(2,1)S(1)} %get-tuple-element.95.x0), channel_id=1, source_target_pairs={{0,2},{1,3},{2,0},{3,1},{4,6},{5,7},{6,4},{7,5},{8,10},{9,11},{10,... | collective-permute-start | bytes 1572872 | tf_op jit(solution)/shard_map/send_y0/ppermute | solution.py:294
  8.0 22.9 %collective-permute-start.4 = (bf16[128,2048]{1,0:T(8,128)(2,1)S(1)}, bf16[128,2048]{1,0:T(8,128)(2,1)S(1)}, u32[]{:S(2)}, u32[]{:S(2)}) collective-permute-start(bf16[128,2048]{1,0:T(8,128)(2,1)S(1)} %get-tuple-element.95.x0), channel_id=1, source_target_pairs={{0,4},{1,5},{2,6},{3,7},{4,8},{5,9},{6,10},{7,11},{8,12},{9,13},{1... | collective-permute-start | bytes 1572872 | tf_op jit(solution)/shard_map/send_b0/ppermute | solution.py:294
  8.0 25.2 %collective-permute-start.1 = (bf16[1024,4096]{1,0:T(8,128)(2,1)}, bf16[1024,4096]{1,0:T(8,128)(2,1)}, u32[]{:S(2)}, u32[]{:S(2)}) collective-permute-start(bf16[1024,4096]{1,0:T(8,128)(2,1)} %train.1), channel_id=1, source_target_pairs={{0,1},{1,0},{2,3},{3,2},{4,5},{5,4},{6,7},{7,6},{8,9},{9,8},{10,11... | collective-permute-start | bytes 25165832 | tf_op jit(solution)/shard_map/send_train/ppermute | solution.py:294
  8.0 24.5 %collective-permute-start.5 = (bf16[128,2048]{1,0:T(8,128)(2,1)S(1)}, bf16[128,2048]{1,0:T(8,128)(2,1)S(1)}, u32[]{:S(2)}, u32[]{:S(2)}) collective-permute-start(bf16[128,2048]{1,0:T(8,128)(2,1)S(1)} %collective-permute-done.x1), channel_id=1, source_target_pairs={{0,2},{1,3},{2,0},{3,1},{4,6},{5,7},{6,4},{7,5},{8,10},{9,11},{10,... | collective-permute-start | bytes 1572872 | tf_op jit(solution)/shard_map/send_y1/ppermute | solution.py:294
  8.6 0.9 copy-start.1
  9.5 0.9 copy-start.2
  10.4 0.7 copy-start.3
  11.1 0.7 copy-start.4
  21.9 27.9 %collective-permute-start.8 = (bf16[128,2048]{1,0:T(8,128)(2,1)S(1)}, bf16[128,2048]{1,0:T(8,128)(2,1)S(1)}, u32[]{:S(2)}, u32[]{:S(2)}) collective-permute-start(bf16[128,2048]{1,0:T(8,128)(2,1)S(1)} %get-tuple-element.71.refs_3_), channel_id=1, source_target_pairs={{0,4},{1,5},{2,6},{3,7},{4,8},{5,9},{6,10},{7,11},{8,12},{9,13},{1... | collective-permute-start | bytes 1572872 | tf_op jit(solution)/shard_map/send_b1/ppermute | solution.py:294
  22.0 27.8 %collective-permute-start.9 = (bf16[128,2048]{1,0:T(8,128)(2,1)S(1)}, bf16[128,2048]{1,0:T(8,128)(2,1)S(1)}, u32[]{:S(2)}, u32[]{:S(2)}) collective-permute-start(bf16[128,2048]{1,0:T(8,128)(2,1)S(1)} %get-tuple-element.65.refs_4_), channel_id=1, source_target_pairs={{0,2},{1,3},{2,0},{3,1},{4,6},{5,7},{6,4},{7,5},{8,10},{9,11},{10,... | collective-permute-start | bytes 1572872 | tf_op jit(solution)/shard_map/send_ya0/ppermute | solution.py:294
  39.9 16.7 %collective-permute-start.6 = (bf16[128,2048]{1,0:T(8,128)(2,1)S(1)}, bf16[128,2048]{1,0:T(8,128)(2,1)S(1)}, u32[]{:S(2)}, u32[]{:S(2)}) collective-permute-start(bf16[128,2048]{1,0:T(8,128)(2,1)S(1)} %get-tuple-element.65.refs_4_), channel_id=1, source_target_pairs={{0,12},{1,13},{2,14},{3,15},{4,0},{5,1},{6,2},{7,3},{8,4},{9,5},{1... | collective-permute-start | bytes 1572872 | tf_op jit(solution)/shard_map/send_f0/ppermute | solution.py:294
  41.4 15.2 %collective-permute-start.7 = (bf16[128,2048]{1,0:T(8,128)(2,1)S(1)}, bf16[128,2048]{1,0:T(8,128)(2,1)S(1)}, u32[]{:S(2)}, u32[]{:S(2)}) collective-permute-start(bf16[128,2048]{1,0:T(8,128)(2,1)S(1)} %get-tuple-element.66.refs_2_), channel_id=1, source_target_pairs={{0,2},{1,3},{2,0},{3,1},{4,6},{5,7},{6,4},{7,5},{8,10},{9,11},{10,... | collective-permute-start | bytes 1572872 | tf_op jit(solution)/shard_map/send_yb0/ppermute | solution.py:294
  42.5 2.2 %copy-start = (bf16[1024,2048]{1,0:T(8,128)(2,1)S(1)}, bf16[1024,2048]{1,0:T(8,128)(2,1)}, u32[]{:S(2)}) copy-start(bf16[1024,2048]{1,0:T(8,128)(2,1)} %get-tuple-element.60.refs_6_.refs_4_) | copy-start | bytes 12582916
  49.8 16.8 %collective-permute-start.12 = (bf16[128,2048]{1,0:T(8,128)(2,1)S(1)}, bf16[128,2048]{1,0:T(8,128)(2,1)S(1)}, u32[]{:S(2)}, u32[]{:S(2)}) collective-permute-start(bf16[128,2048]{1,0:T(8,128)(2,1)S(1)} %collective-permute-done.8.refs_4_), channel_id=1, source_target_pairs={{0,4},{1,5},{2,6},{3,7},{4,8},{5,9},{6,10},{7,11},{8,12},{9,13},{1... | collective-permute-start | bytes 1572872 | tf_op jit(solution)/shard_map/send_f1/ppermute | solution.py:294
  50.9 16.6 %collective-permute-start.13 = (bf16[128,2048]{1,0:T(8,128)(2,1)S(1)}, bf16[128,2048]{1,0:T(8,128)(2,1)S(1)}, u32[]{:S(2)}, u32[]{:S(2)}) collective-permute-start(bf16[128,2048]{1,0:T(8,128)(2,1)S(1)} %collective-permute-done.8.refs_4_), channel_id=1, source_target_pairs={{0,2},{1,3},{2,0},{3,1},{4,6},{5,7},{6,4},{7,5},{8,10},{9,11},{10,... | collective-permute-start | bytes 1572872 | tf_op jit(solution)/shard_map/send_yb1/ppermute | solution.py:294
  56.6 19.7 %collective-permute-start.10 = (bf16[128,2048]{1,0:T(8,128)(2,1)S(1)}, bf16[128,2048]{1,0:T(8,128)(2,1)S(1)}, u32[]{:S(2)}, u32[]{:S(2)}) collective-permute-start(bf16[128,2048]{1,0:T(8,128)(2,1)S(1)} %get-tuple-element.71.refs_3_), channel_id=1, source_target_pairs={{0,12},{1,13},{2,14},{3,15},{4,0},{5,1},{6,2},{7,3},{8,4},{9,5},{1... | collective-permute-start | bytes 1572872 | tf_op jit(solution)/shard_map/send_a1/ppermute | solution.py:294
  60.1 18.6 %collective-permute-start.11 = (bf16[128,2048]{1,0:T(8,128)(2,1)S(1)}, bf16[128,2048]{1,0:T(8,128)(2,1)S(1)}, u32[]{:S(2)}, u32[]{:S(2)}) collective-permute-start(bf16[128,2048]{1,0:T(8,128)(2,1)S(1)} %collective-permute-done.6.refs_2_), channel_id=1, source_target_pairs={{0,2},{1,3},{2,0},{3,1},{4,6},{5,7},{6,4},{7,5},{8,10},{9,11},{10,... | collective-permute-start | bytes 1572872 | tf_op jit(solution)/shard_map/send_yf0/ppermute | solution.py:294
  61.2 20.6 %collective-permute-start.17 = (f32[8,8,128,128]{3,2,1,0:T(8,128)S(1)}, f32[8,8,128,128]{3,2,1,0:T(8,128)S(1)}, u32[]{:S(2)}, u32[]{:S(2)}) collective-permute-start(f32[8,8,128,128]{3,2,1,0:T(8,128)S(1)} %get-tuple-element.80), channel_id=1, source_target_pairs={{0,1},{1,0},{2,3},{3,2},{4,5},{5,4},{6,7},{7,6},{8,9},{9,8},{10,11... | collective-permute-start | bytes 12582920 | tf_op jit(solution)/shard_map/send_part4/ppermute | solution.py:294
  70.5 16.0 %collective-permute-start.15 = (bf16[128,2048]{1,0:T(8,128)(2,1)S(1)}, bf16[128,2048]{1,0:T(8,128)(2,1)S(1)}, u32[]{:S(2)}, u32[]{:S(2)}) collective-permute-start(bf16[128,2048]{1,0:T(8,128)(2,1)S(1)} %get-tuple-element.78.refs_3_), channel_id=1, source_target_pairs={{0,12},{1,13},{2,14},{3,15},{4,0},{5,1},{6,2},{7,3},{8,4},{9,5},{1... | collective-permute-start | bytes 1572872 | tf_op jit(solution)/shard_map/send_xa1/ppermute | solution.py:294
  72.4 15.5 %collective-permute-start.16 = (bf16[128,2048]{1,0:T(8,128)(2,1)S(1)}, bf16[128,2048]{1,0:T(8,128)(2,1)S(1)}, u32[]{:S(2)}, u32[]{:S(2)}) collective-permute-start(bf16[128,2048]{1,0:T(8,128)(2,1)S(1)} %collective-permute-done.12.refs_2_), channel_id=1, source_target_pairs={{0,2},{1,3},{2,0},{3,1},{4,6},{5,7},{6,4},{7,5},{8,10},{9,11},{10,... | collective-permute-start | bytes 1572872 | tf_op jit(solution)/shard_map/send_yf1/ppermute | solution.py:294
  76.3 5.4 %collective-permute-start.18 = (f32[8,4,128,128]{3,2,1,0:T(8,128)S(1)}, f32[8,4,128,128]{3,2,1,0:T(8,128)S(1)}, u32[]{:S(2)}, u32[]{:S(2)}) collective-permute-start(f32[8,4,128,128]{3,2,1,0:T(8,128)S(1)} %get-tuple-element.84), channel_id=1, source_target_pairs={{0,1},{1,0},{2,3},{3,2},{4,5},{5,4},{6,7},{7,6},{8,9},{9,8},{10,11... | collective-permute-start | bytes 6291464 | tf_op jit(solution)/shard_map/send_part6/ppermute | solution.py:294
  81.7 8.5 %collective-permute-start.14 = (f32[8,2,128,128]{3,2,1,0:T(8,128)S(1)}, f32[8,2,128,128]{3,2,1,0:T(8,128)S(1)}, u32[]{:S(2)}, u32[]{:S(2)}) collective-permute-start(f32[8,2,128,128]{3,2,1,0:T(8,128)S(1)} %get-tuple-element.77), channel_id=1, source_target_pairs={{0,1},{1,0},{2,3},{3,2},{4,5},{5,4},{6,7},{7,6},{8,9},{9,8},{10,11... | collective-permute-start | bytes 3145736 | tf_op jit(solution)/shard_map/send_part7/ppermute | solution.py:294
  86.6 3.6 %collective-permute-start.19 = (bf16[128,2048]{1,0:T(8,128)(2,1)S(1)}, bf16[128,2048]{1,0:T(8,128)(2,1)S(1)}, u32[]{:S(2)}, u32[]{:S(2)}) collective-permute-start(bf16[128,2048]{1,0:T(8,128)(2,1)S(1)} %collective-permute-done.15.refs_2_), channel_id=1, source_target_pairs={{0,1},{1,0},{2,3},{3,2},{4,5},{5,4},{6,7},{7,6},{8,9},{9,8},{10,11... | collective-permute-start | bytes 1572872 | tf_op jit(solution)/shard_map/send_cxa1/ppermute | solution.py:294
  87.9 2.3 %collective-permute-start.20 = (bf16[128,2048]{1,0:T(8,128)(2,1)S(1)}, bf16[128,2048]{1,0:T(8,128)(2,1)S(1)}, u32[]{:S(2)}, u32[]{:S(2)}) collective-permute-start(bf16[128,2048]{1,0:T(8,128)(2,1)S(1)} %collective-permute-done.16.refs_3_), channel_id=1, source_target_pairs={{0,1},{1,0},{2,3},{3,2},{4,5},{5,4},{6,7},{7,6},{8,9},{9,8},{10,11... | collective-permute-start | bytes 1572872 | tf_op jit(solution)/shard_map/send_cyf1/ppermute | solution.py:294
